TPU v7x, 256 devices: a whole 4x4x8 slice. The times are simulated.
256 devices in a mesh: lat: 8 (over x, core), lon: 32 (over z, y).
Axes of the slice: x: 4, y: 4, z: 8, core: 2. Of those that a mesh axis runs over, the one named last changes fastest.
Arguments:
- heat_anomaly: float32 [62, 128, 4096], P(None, 'lat', 'lon'), may hold values from -6 to 6
- saltiness_anomaly: float32 [62, 128, 4096], P(None, 'lat', 'lon'), may hold values from -6 to 6
- zonal_current_array: float32 [62, 128, 4096], P(None, 'lat', 'lon'), may hold values from -6 to 6
- meridional_current_array: float32 [62, 128, 4096], P(None, 'lat', 'lon'), may hold values from -6 to 6
- sea_height_prior: float32 [128, 4096], P('lat', 'lon'), may hold values from -4 to 4
- ocean_layer_number: int32 [128, 4096], P('lat', 'lon'), may hold values from 0 to 62, as said below
Outputs:
- heat_anomaly_next: float32 [62, 128, 4096], P(None, 'lat', 'lon')
- saltiness_next: float32 [62, 128, 4096], P(None, 'lat', 'lon')
- zonal_current_next: float32 [62, 128, 4096], P(None, 'lat', 'lon')
- meridional_current_next: float32 [62, 128, 4096], P(None, 'lat', 'lon')
- sea_height_result: float32 [128, 4096], P('lat', 'lon')
Inputs may be any that keep to these rules, and one draw needn't show every extreme that they name: `ocean_layer_number`: 0 marks land; elsewhere the number of wet levels counted from the top.
All inputs are finite; a program needn't handle non-finite values.
Results may differ from a plain program's by a relative error of at most 0.0003.
Values sent between devices are 32-bit elements; how exact they have to be, the bound alone decides.
No kernel may reach another device: no remote copies, remote signals or barrier semaphores. Data moves between devices by JAX's collectives and lax.ppermute only.
A program may use at most 128 MiB of HBM per device.

v0:
```python
import jax
import jax.numpy as jnp
from jax import lax
from jax.sharding import PartitionSpec as P

ITERATIONS = 32


TIME_STEP = 0.1
MIX_TRACER = 0.05
MIX_MOMENTUM = 0.05
HEAT_INDEX = 0.2
SALT_INDEX = 0.2
CORIOLIS = 2.0
SURFACE_TERM = 0.0005
TRANSPORT_SCALE = 0.05


def with_halo(cells, sides, width):
    for axis, dim in sides:
        count = lax.axis_size(axis)
        head = lax.slice_in_dim(cells, 0, width, axis=dim)
        tail = lax.slice_in_dim(cells, cells.shape[dim] - width, cells.shape[dim], axis=dim)
        cells = jnp.concatenate(
            [
                lax.ppermute(tail, axis, [(i, (i + 1) % count) for i in range(count)]),
                cells,
                lax.ppermute(head, axis, [((i + 1) % count, i) for i in range(count)]),
            ],
            axis=dim,
        )
    return cells


def shifted(value, axis, by):
    size = lax.axis_size(axis)
    return lax.ppermute(value, axis, [(i, (i + by) % size) for i in range(size)])


def shifted_2(value, axis, steps):
    count = lax.axis_size(axis)
    first, last = (max(0, -steps), min(count, count - steps))
    return lax.ppermute(value, axis, [(source, source + steps) for source in range(first, last)])


def chebyshev_weights(total_steps):
    low_bound = SURFACE_TERM / (SURFACE_TERM + 4.0)
    high_bound = 2.0 - low_bound
    spread_ratio = (high_bound - low_bound) / (high_bound + low_bound)
    middle = 0.5 * (high_bound + low_bound)
    weights = [1.0]
    for number in range(1, total_steps):
        if number == 1:
            weights.append(2.0 / (2.0 - spread_ratio * spread_ratio))
        else:
            weights.append(1.0 / (1.0 - spread_ratio * spread_ratio * weights[-1] / 4.0))
    scales = jnp.asarray([weight_value / middle for weight_value in weights], jnp.float32)
    carries = jnp.asarray([weight_value - 1.0 for weight_value in weights], jnp.float32)
    return (scales, carries)


def crop(source, margin):
    if margin == 0:
        return source
    return source[..., margin:-margin, margin:-margin]


def global_rows(parallel_sum_value, margin):
    return (
        lax.axis_index("lat") * parallel_sum_value
        + jnp.arange(parallel_sum_value + 2 * margin, dtype=jnp.int32)
        - margin
    )


def valid_rows(parallel_sum_value, margin):
    position = global_rows(parallel_sum_value, margin)
    inside = (position >= 0) & (position < parallel_sum_value * lax.axis_size("lat"))
    return inside.astype(jnp.float32)[:, None]


def laplacian(source, mask_field):
    centre = source[..., 1:-1, 1:-1]
    return mask_field[..., 1:-1, 1:-1] * (
        mask_field[..., 1:-1, 2:] * (source[..., 1:-1, 2:] - centre)
        + mask_field[..., 1:-1, :-2] * (source[..., 1:-1, :-2] - centre)
        + mask_field[..., 2:, 1:-1] * (source[..., 2:, 1:-1] - centre)
        + mask_field[..., :-2, 1:-1] * (source[..., :-2, 1:-1] - centre)
    )


def advection(tracer, eastward, northward, water_indicator):
    east_flux = (
        0.25
        * (eastward[..., :, :-1] + eastward[..., :, 1:])
        * (tracer[..., :, :-1] + tracer[..., :, 1:])
        * (water_indicator[..., :, :-1] * water_indicator[..., :, 1:])
    )
    north_flux = (
        0.25
        * (northward[..., :-1, :] + northward[..., 1:, :])
        * (tracer[..., :-1, :] + tracer[..., 1:, :])
        * (water_indicator[..., :-1, :] * water_indicator[..., 1:, :])
    )
    return (
        east_flux[..., 1:-1, 1:]
        - east_flux[..., 1:-1, :-1]
        + (north_flux[..., 1:, 1:-1] - north_flux[..., :-1, 1:-1])
    )


def face_set(depth_plane, layer_pile):
    east_all = jnp.minimum(depth_plane[:, :-1], depth_plane[:, 1:]) / layer_pile
    north_all = jnp.minimum(depth_plane[:-1, :], depth_plane[1:, :]) / layer_pile
    east_face = east_all[1:-1, 1:]
    west_face = east_all[1:-1, :-1]
    north_face = north_all[1:, 1:-1]
    south_face = north_all[:-1, 1:-1]
    diagonal_term = SURFACE_TERM + (east_face + west_face + north_face) + south_face
    return (east_face, west_face, north_face, south_face, diagonal_term)


def apply_operator(height, face_terms):
    east_face, west_face, north_face, south_face, diagonal_term = face_terms
    centre = height[1:-1, 1:-1]
    return diagonal_term * centre - (
        east_face * height[1:-1, 2:]
        + west_face * height[1:-1, :-2]
        + north_face * height[2:, 1:-1]
        + south_face * height[:-2, 1:-1]
    )


def per_device(
    heat_anomaly,
    saltiness_anomaly,
    zonal_current_array,
    meridional_current_array,
    sea_height_prior,
    ocean_layer_number,
):
    layer_pile, parallel_sum_value, vertical_integral = heat_anomaly.shape
    lat_total = parallel_sum_value * lax.axis_size("lat")
    depth_plane = ocean_layer_number.astype(jnp.float32)[None]
    margin = 2
    heat_haloed, haline_haloed, lateral_flow_haloed, meridional_flow_haloed, bathymetry_haloed = (
        with_halo(heat_anomaly, (("lat", 1), ("lon", 2)), 2),
        with_halo(saltiness_anomaly, (("lat", 1), ("lon", 2)), 2),
        with_halo(zonal_current_array, (("lat", 1), ("lon", 2)), 2),
        with_halo(meridional_current_array, (("lat", 1), ("lon", 2)), 2),
        with_halo(depth_plane, (("lat", 1), ("lon", 2)), 2),
    )
    parallel_validity = valid_rows(parallel_sum_value, margin)
    heat_haloed = heat_haloed * parallel_validity
    haline_haloed = haline_haloed * parallel_validity
    lateral_flow_haloed = lateral_flow_haloed * parallel_validity
    meridional_flow_haloed = meridional_flow_haloed * parallel_validity
    bathymetry_haloed = bathymetry_haloed * parallel_validity
    level_float = jnp.arange(layer_pile, dtype=jnp.float32)[:, None, None]
    water_indicator = (level_float < bathymetry_haloed).astype(jnp.float32)
    inner_wet = crop(water_indicator, 1)

    def scalar_stepper(tracer):
        mixing = laplacian(laplacian(tracer, water_indicator), inner_wet)
        advected = advection(tracer, lateral_flow_haloed, meridional_flow_haloed, water_indicator)
        return crop(water_indicator, margin) * (
            crop(tracer, margin)
            - TIME_STEP * (crop(advected, margin - 1) + MIX_TRACER * crop(mixing, margin - 2))
        )

    heat_anomaly_next = scalar_stepper(heat_haloed)
    saltiness_next = scalar_stepper(haline_haloed)
    hydrostatic_load = jnp.cumsum(
        (SALT_INDEX * haline_haloed - HEAT_INDEX * heat_haloed) * water_indicator, axis=0
    )
    zonal_grad = 0.5 * (hydrostatic_load[:, 1:-1, 2:] - hydrostatic_load[:, 1:-1, :-2])
    north_grad = 0.5 * (hydrostatic_load[:, 2:, 1:-1] - hydrostatic_load[:, :-2, 1:-1])
    row_position = global_rows(parallel_sum_value, margin).astype(jnp.float32)[:, None]
    coriolis = CORIOLIS * (2.0 * (row_position + 0.5) / lat_total - 1.0)
    coriolis = coriolis[2 : parallel_sum_value + 2 * margin - 2]
    zonal_mix = laplacian(laplacian(lateral_flow_haloed, water_indicator), inner_wet)
    north_mix = laplacian(laplacian(meridional_flow_haloed, water_indicator), inner_wet)
    velocity_wet = crop(water_indicator, 2)
    eastward_following = velocity_wet * (
        crop(lateral_flow_haloed, 2)
        + TIME_STEP
        * (
            coriolis * crop(meridional_flow_haloed, 2)
            - crop(zonal_grad, 1)
            - MIX_MOMENTUM * zonal_mix
        )
    )
    northward_following = velocity_wet * (
        crop(meridional_flow_haloed, 2)
        - TIME_STEP
        * (coriolis * crop(lateral_flow_haloed, 2) + crop(north_grad, 1) + MIX_MOMENTUM * north_mix)
    )
    zonal_sum = jnp.sum(eastward_following, axis=0)
    north_sum = jnp.sum(northward_following, axis=0)
    west_column = shifted(zonal_sum[:, -1:], "lon", 1)
    south_row = shifted_2(north_sum[-1:, :], "lat", 1)
    zonal_faces = jnp.concatenate([west_column, zonal_sum], axis=1)
    north_faces = jnp.concatenate([south_row, north_sum], axis=0)
    depth_near = crop(bathymetry_haloed[0], margin - 1)
    ocean_near = (depth_near > 0).astype(jnp.float32)
    zonal_flow = zonal_faces * (ocean_near[1:-1, :-1] * ocean_near[1:-1, 1:])
    north_flow = north_faces * (ocean_near[:-1, 1:-1] * ocean_near[1:, 1:-1])
    divergence = zonal_flow[:, 1:] - zonal_flow[:, :-1] + (north_flow[1:, :] - north_flow[:-1, :])
    right_side = SURFACE_TERM * sea_height_prior - TRANSPORT_SCALE * divergence
    ocean = crop(ocean_near, 1)
    scales, carries = chebyshev_weights(ITERATIONS)
    face_terms = face_set(depth_near, layer_pile)
    diagonal_term = face_terms[4]

    def single_iteration(number, solver_state):
        height, change = solver_state
        height_ext = with_halo(height, (("lat", 0), ("lon", 1)), 1) * valid_rows(
            parallel_sum_value, 1
        )
        residual = right_side - apply_operator(height_ext, face_terms)
        change = scales[number] * residual / diagonal_term + carries[number] * change
        return (height + change, change)

    height, change = lax.fori_loop(
        0, ITERATIONS, single_iteration, (sea_height_prior, jnp.zeros_like(sea_height_prior))
    )
    sea_height_result = ocean * height
    return (
        heat_anomaly_next,
        saltiness_next,
        eastward_following,
        northward_following,
        sea_height_result,
    )


def solution(mesh):
    in_specs = (
        P(None, "lat", "lon"),
        P(None, "lat", "lon"),
        P(None, "lat", "lon"),
        P(None, "lat", "lon"),
        P("lat", "lon"),
        P("lat", "lon"),
    )
    out_specs = (
        P(None, "lat", "lon"),
        P(None, "lat", "lon"),
        P(None, "lat", "lon"),
        P(None, "lat", "lon"),
        P("lat", "lon"),
    )
    return jax.shard_map(
        per_device, mesh=mesh, in_specs=in_specs, out_specs=out_specs, check_vma=False
    )
```

profile of v0, /device:TPU:1, one launch (start us, length us, event | category | flops | bytes accessed | tf_op | source)
XLA Modules:
  0.0 564.3 jit_solution(11637378003133587645)
XLA Ops:
  16.1 6.8 %collective-permute-start.7 = (f32[1,20,2]{2,1,0:T(8,128)S(1)}, f32[1,20,2]{2,1,0:T(8,128)S(1)}, u32[]{:S(2)}, u32[]{:S(2)}) collective-permute-start(f32[1,20,2]{2,1,0:T(8,128)S(1)} %get-tuple-element.398), channel_id=1, source_target_pairs={{1,0},{2,1},{3,2},{4,3},{5,4},{6,5},{7,6},{8,7},{9,8},{10,9},{11,1... | collective-permute-start | bytes 488 | tf_op jit(solution)/shard_map/ppermute | solution.py:28
  37.1 4.8 collective-permute-start.15
  47.1 4.8 collective-permute-start.19
  60.3 4.8 collective-permute-start.23
  65.1 4.9 collective-permute-start.11
  86.8 4.5 maximum_multiply_fusion.4
  91.8 4.3 fusion.18
  101.9 4.6 fusion.26
  106.5 4.4 fusion.38
  114.8 6.9 %fusion.130 = (f32[16,128]{1,0:T(8,128)S(1)}, f32[62,16,128]{2,1,0:T(8,128)}) fusion(f32[62,18,130]{2,1,0:T(8,128)} %fusion.18, f32[62,20,132]{2,1,0:T(8,128)S(1)} %fusion.55, f32[62,18,130]{2,1,0:T(8,128)} %get-tuple-element.366, f32[62,18,130]{2,1,0:T(8,128)} %get-tuple-element.367, f32[62,20,132]{2,1,0:T(8,128)S(1)} %get-tuple-element.405, ...), kind=kLoop, calls=%fused_computation.208 | loop fusion | flops 2791424 | bytes 7626816 | tf_op jit(solution)/shard_map/reduce_sum | solution.py:198
  121.8 4.4 fusion.132
  136.0 5.6 fusion.96
  141.5 4.1 fusion.110
  145.9 417.3 %while.19 = (s32[]{:T(128)}, f32[16,128]{1,0:T(8,128)S(1)}, f32[16,128]{1,0:T(8,128)S(1)}, f32[16,128]{1,0:T(8,128)S(1)}, f32[16,128]{1,0:T(8,128)S(1)}, /*index...) while((s32[]{:T(128)}, f32[16,128]{1,0:T(8,128)S(1)}, ...), condition=%wide.region_4.5_spmd.clone.clone, body=%wide.region_3.4_spmd.sunk.clone.clone.sunk | while | flops 49191 | bytes 167583 | solution.py:224
  150.8 5.1 collective-permute-start.2
  156.7 5.0 collective-permute-done.3
  163.2 4.4 collective-permute-start
  189.3 4.1 collective-permute-start
  202.2 4.1 collective-permute-start
  215.1 4.1 collective-permute-start
  240.9 4.1 collective-permute-start
  253.8 4.1 collective-permute-start
  266.6 4.1 collective-permute-start
  305.3 4.1 collective-permute-start
  318.2 4.1 collective-permute-start
  331.1 4.1 collective-permute-start
  369.8 4.1 collective-permute-start
  382.7 4.1 collective-permute-start
  395.6 4.1 collective-permute-start
  434.3 4.1 collective-permute-start
  447.2 4.1 collective-permute-start
  460.1 4.1 collective-permute-start
  (616 shorter events, 420.8 us)
Async XLA Ops:
  2.5 24.1 %collective-permute-start.12 = (f32[62,2,128]{2,1,0:T(2,128)S(1)}, f32[62,2,128]{2,1,0:T(2,128)S(1)}, u32[]{:S(2)}, u32[]{:S(2)}) collective-permute-start(f32[62,2,128]{2,1,0:T(2,128)S(1)} %get-tuple-element.386), channel_id=1, source_target_pairs={{0,32},{32,64},{64,96},{96,128},{128,160},{160,192},{192,224},{224... | collective-permute-start | bytes 190472 | tf_op jit(solution)/shard_map/ppermute | solution.py:26
  5.1 23.6 %collective-permute-start.13 = (f32[62,2,128]{2,1,0:T(2,128)S(1)}, f32[62,2,128]{2,1,0:T(2,128)S(1)}, u32[]{:S(2)}, u32[]{:S(2)}) collective-permute-start(f32[62,2,128]{2,1,0:T(2,128)S(1)} %get-tuple-element.387), channel_id=1, source_target_pairs={{32,0},{64,32},{96,64},{128,96},{160,128},{192,160},{224,192},{0,2... | collective-permute-start | bytes 190472 | tf_op jit(solution)/shard_map/ppermute | solution.py:28
  6.5 8.3 %collective-permute-start.4 = (f32[1,2,128]{2,1,0:T(2,128)S(1)}, f32[1,2,128]{2,1,0:T(2,128)S(1)}, u32[]{:S(2)}, u32[]{:S(2)}) collective-permute-start(f32[1,2,128]{2,1,0:T(2,128)S(1)} %get-tuple-element.401), channel_id=1, source_target_pairs={{0,32},{32,64},{64,96},{96,128},{128,160},{160,192},{192,224},{224... | collective-permute-start | bytes 3080 | tf_op jit(solution)/shard_map/ppermute | solution.py:26
  7.6 7.3 %collective-permute-start.5 = (f32[1,2,128]{2,1,0:T(2,128)S(1)}, f32[1,2,128]{2,1,0:T(2,128)S(1)}, u32[]{:S(2)}, u32[]{:S(2)}) collective-permute-start(f32[1,2,128]{2,1,0:T(2,128)S(1)} %get-tuple-element.402), channel_id=1, source_target_pairs={{32,0},{64,32},{96,64},{128,96},{160,128},{192,160},{224,192},{0,2... | collective-permute-start | bytes 3080 | tf_op jit(solution)/shard_map/ppermute | solution.py:28
  14.8 15.2 %collective-permute-start.16 = (f32[62,2,128]{2,1,0:T(2,128)}, f32[62,2,128]{2,1,0:T(2,128)S(1)}, u32[]{:S(2)}, u32[]{:S(2)}) collective-permute-start(f32[62,2,128]{2,1,0:T(2,128)} %get-tuple-element.388), channel_id=1, source_target_pairs={{0,32},{32,64},{64,96},{96,128},{128,160},{160,192},{192,224},{224... | collective-permute-start | bytes 190472 | tf_op jit(solution)/shard_map/ppermute | solution.py:26
  14.9 9.0 %collective-permute-start.6 = (f32[1,20,2]{2,1,0:T(8,128)S(1)}, f32[1,20,2]{2,1,0:T(8,128)S(1)}, u32[]{:S(2)}, u32[]{:S(2)}) collective-permute-start(f32[1,20,2]{2,1,0:T(8,128)S(1)} %get-tuple-element.397), channel_id=1, source_target_pairs={{0,1},{1,2},{2,3},{3,4},{4,5},{5,6},{6,7},{7,8},{8,9},{9,10},{10,1... | collective-permute-start | bytes 488 | tf_op jit(solution)/shard_map/ppermute | solution.py:26
  16.1 10.0 %collective-permute-start.7 = (f32[1,20,2]{2,1,0:T(8,128)S(1)}, f32[1,20,2]{2,1,0:T(8,128)S(1)}, u32[]{:S(2)}, u32[]{:S(2)}) collective-permute-start(f32[1,20,2]{2,1,0:T(8,128)S(1)} %get-tuple-element.398), channel_id=1, source_target_pairs={{1,0},{2,1},{3,2},{4,3},{5,4},{6,5},{7,6},{8,7},{9,8},{10,9},{11,1... | collective-permute-start | bytes 488 | tf_op jit(solution)/shard_map/ppermute | solution.py:28
  23.9 9.0 %collective-permute-start.17 = (f32[62,2,128]{2,1,0:T(2,128)}, f32[62,2,128]{2,1,0:T(2,128)S(1)}, u32[]{:S(2)}, u32[]{:S(2)}) collective-permute-start(f32[62,2,128]{2,1,0:T(2,128)} %get-tuple-element.389), channel_id=1, source_target_pairs={{32,0},{64,32},{96,64},{128,96},{160,128},{192,160},{224,192},{0,2... | collective-permute-start | bytes 190472 | tf_op jit(solution)/shard_map/ppermute | solution.py:28
  26.6 10.5 %collective-permute-start.20 = (f32[62,2,128]{2,1,0:T(2,128)}, f32[62,2,128]{2,1,0:T(2,128)S(1)}, u32[]{:S(2)}, u32[]{:S(2)}) collective-permute-start(f32[62,2,128]{2,1,0:T(2,128)} %get-tuple-element.384), channel_id=1, source_target_pairs={{0,32},{32,64},{64,96},{96,128},{128,160},{160,192},{192,224},{224... | collective-permute-start | bytes 190472 | tf_op jit(solution)/shard_map/ppermute | solution.py:26
  26.6 15.3 %collective-permute-start.21 = (f32[62,2,128]{2,1,0:T(2,128)}, f32[62,2,128]{2,1,0:T(2,128)S(1)}, u32[]{:S(2)}, u32[]{:S(2)}) collective-permute-start(f32[62,2,128]{2,1,0:T(2,128)} %get-tuple-element.385), channel_id=1, source_target_pairs={{32,0},{64,32},{96,64},{128,96},{160,128},{192,160},{224,192},{0,2... | collective-permute-start | bytes 190472 | tf_op jit(solution)/shard_map/ppermute | solution.py:28
  30.0 17.1 %collective-permute-start.8 = (f32[62,2,128]{2,1,0:T(2,128)}, f32[62,2,128]{2,1,0:T(2,128)}, u32[]{:S(2)}, u32[]{:S(2)}) collective-permute-start(f32[62,2,128]{2,1,0:T(2,128)} %get-tuple-element.390), channel_id=1, source_target_pairs={{0,32},{32,64},{64,96},{96,128},{128,160},{160,192},{192,224},{224... | collective-permute-start | bytes 190472 | tf_op jit(solution)/shard_map/ppermute | solution.py:26
  30.0 21.9 %collective-permute-start.9 = (f32[62,2,128]{2,1,0:T(2,128)}, f32[62,2,128]{2,1,0:T(2,128)}, u32[]{:S(2)}, u32[]{:S(2)}) collective-permute-start(f32[62,2,128]{2,1,0:T(2,128)} %get-tuple-element.391), channel_id=1, source_target_pairs={{32,0},{64,32},{96,64},{128,96},{160,128},{192,160},{224,192},{0,2... | collective-permute-start | bytes 190472 | tf_op jit(solution)/shard_map/ppermute | solution.py:28
  37.1 23.2 %collective-permute-start.14 = (f32[62,20,2]{0,2,1:T(2,128)}, f32[62,20,2]{0,2,1:T(2,128)S(1)}, u32[]{:S(2)}, u32[]{:S(2)}) collective-permute-start(f32[62,20,2]{0,2,1:T(2,128)} %copy.25), channel_id=1, source_target_pairs={{0,1},{1,2},{2,3},{3,4},{4,5},{5,6},{6,7},{7,8},{8,9},{9,10},{10,1... | collective-permute-start | bytes 29768 | tf_op jit(solution)/shard_map/ppermute | solution.py:26
  37.1 28.0 %collective-permute-start.15 = (f32[62,20,2]{0,2,1:T(2,128)}, f32[62,20,2]{0,2,1:T(2,128)}, u32[]{:S(2)}, u32[]{:S(2)}) collective-permute-start(f32[62,20,2]{0,2,1:T(2,128)} %copy.26), channel_id=1, source_target_pairs={{1,0},{2,1},{3,2},{4,3},{5,4},{6,5},{7,6},{8,7},{9,8},{10,9},{11,1... | collective-permute-start | bytes 29768 | tf_op jit(solution)/shard_map/ppermute | solution.py:28
  47.1 18.0 %collective-permute-start.18 = (f32[62,20,2]{0,2,1:T(2,128)}, f32[62,20,2]{0,2,1:T(2,128)}, u32[]{:S(2)}, u32[]{:S(2)}) collective-permute-start(f32[62,20,2]{0,2,1:T(2,128)} %copy.29), channel_id=1, source_target_pairs={{0,1},{1,2},{2,3},{3,4},{4,5},{5,6},{6,7},{7,8},{8,9},{9,10},{10,1... | collective-permute-start | bytes 29768 | tf_op jit(solution)/shard_map/ppermute | solution.py:26
  47.1 27.2 %collective-permute-start.19 = (f32[62,20,2]{0,2,1:T(2,128)}, f32[62,20,2]{0,2,1:T(2,128)}, u32[]{:S(2)}, u32[]{:S(2)}) collective-permute-start(f32[62,20,2]{0,2,1:T(2,128)} %copy.30), channel_id=1, source_target_pairs={{1,0},{2,1},{3,2},{4,3},{5,4},{6,5},{7,6},{8,7},{9,8},{10,9},{11,1... | collective-permute-start | bytes 29768 | tf_op jit(solution)/shard_map/ppermute | solution.py:28
  60.3 16.0 %collective-permute-start.22 = (f32[62,20,2]{0,2,1:T(2,128)}, f32[62,20,2]{0,2,1:T(2,128)}, u32[]{:S(2)}, u32[]{:S(2)}) collective-permute-start(f32[62,20,2]{0,2,1:T(2,128)} %copy.33), channel_id=1, source_target_pairs={{0,1},{1,2},{2,3},{3,4},{4,5},{5,6},{6,7},{7,8},{8,9},{9,10},{10,1... | collective-permute-start | bytes 29768 | tf_op jit(solution)/shard_map/ppermute | solution.py:26
  60.3 17.9 %collective-permute-start.23 = (f32[62,20,2]{0,2,1:T(2,128)}, f32[62,20,2]{0,2,1:T(2,128)}, u32[]{:S(2)}, u32[]{:S(2)}) collective-permute-start(f32[62,20,2]{0,2,1:T(2,128)} %copy.34), channel_id=1, source_target_pairs={{1,0},{2,1},{3,2},{4,3},{5,4},{6,5},{7,6},{8,7},{9,8},{10,9},{11,1... | collective-permute-start | bytes 29768 | tf_op jit(solution)/shard_map/ppermute | solution.py:28
  65.1 15.1 %collective-permute-start.10 = (f32[62,20,2]{0,2,1:T(2,128)}, f32[62,20,2]{0,2,1:T(2,128)}, u32[]{:S(2)}, u32[]{:S(2)}) collective-permute-start(f32[62,20,2]{0,2,1:T(2,128)} %copy.21), channel_id=1, source_target_pairs={{0,1},{1,2},{2,3},{3,4},{4,5},{5,6},{6,7},{7,8},{8,9},{9,10},{10,1... | collective-permute-start | bytes 29768 | tf_op jit(solution)/shard_map/ppermute | solution.py:26
  65.1 17.0 %collective-permute-start.11 = (f32[62,20,2]{0,2,1:T(2,128)}, f32[62,20,2]{0,2,1:T(2,128)}, u32[]{:S(2)}, u32[]{:S(2)}) collective-permute-start(f32[62,20,2]{0,2,1:T(2,128)} %copy.22), channel_id=1, source_target_pairs={{1,0},{2,1},{3,2},{4,3},{5,4},{6,5},{7,6},{8,7},{9,8},{10,9},{11,1... | collective-permute-start | bytes 29768 | tf_op jit(solution)/shard_map/ppermute | solution.py:28
  121.8 23.8 %collective-permute-start.24 = (f32[16,1]{1,0:T(8,128)S(1)}, f32[16,1]{1,0:T(8,128)S(1)}, u32[]{:S(2)}, u32[]{:S(2)}) collective-permute-start(f32[16,1]{1,0:T(8,128)S(1)} %slice.801), channel_id=1, source_target_pairs={{0,1},{1,2},{2,3},{3,4},{4,5},{5,6},{6,7},{7,8},{8,9},{9,10},{10,1... | collective-permute-start | bytes 200 | tf_op jit(solution)/shard_map/ppermute | solution.py:37
  126.2 19.5 %collective-permute-start.25 = (f32[1,128]{1,0:T(1,128)S(1)}, f32[1,128]{1,0:T(1,128)S(1)}, u32[]{:S(2)}, u32[]{:S(2)}) collective-permute-start(f32[1,128]{1,0:T(1,128)S(1)} %slice.806), channel_id=1, source_target_pairs={{0,32},{32,64},{64,96},{96,128},{128,160},{160,192},{192,224},{1,3... | collective-permute-start | bytes 1544 | tf_op jit(solution)/shard_map/ppermute | solution.py:43
  169.0 5.9 %collective-permute-start.3 = (f32[18,1]{1,0:T(8,128)S(1)}, f32[18,1]{1,0:T(8,128)S(1)}, u32[]{:S(2)}, u32[]{:S(2)}) collective-permute-start(f32[18,1]{1,0:T(8,128)S(1)} %get-tuple-element.474), channel_id=1, source_target_pairs={{0,1},{1,2},{2,3},{3,4},{4,5},{5,6},{6,7},{7,8},{8,9},{9,10},{10,1... | collective-permute-start | bytes 224 | tf_op jit(solution)/shard_map/while/body/eval_jaxpr/ppermute | solution.py:26
  181.9 5.9 %collective-permute-start.3 = (f32[18,1]{1,0:T(8,128)S(1)}, f32[18,1]{1,0:T(8,128)S(1)}, u32[]{:S(2)}, u32[]{:S(2)}) collective-permute-start(f32[18,1]{1,0:T(8,128)S(1)} %get-tuple-element.474), channel_id=1, source_target_pairs={{0,1},{1,2},{2,3},{3,4},{4,5},{5,6},{6,7},{7,8},{8,9},{9,10},{10,1... | collective-permute-start | bytes 224 | tf_op jit(solution)/shard_map/while/body/eval_jaxpr/ppermute | solution.py:26
  194.8 5.9 %collective-permute-start.3 = (f32[18,1]{1,0:T(8,128)S(1)}, f32[18,1]{1,0:T(8,128)S(1)}, u32[]{:S(2)}, u32[]{:S(2)}) collective-permute-start(f32[18,1]{1,0:T(8,128)S(1)} %get-tuple-element.474), channel_id=1, source_target_pairs={{0,1},{1,2},{2,3},{3,4},{4,5},{5,6},{6,7},{7,8},{8,9},{9,10},{10,1... | collective-permute-start | bytes 224 | tf_op jit(solution)/shard_map/while/body/eval_jaxpr/ppermute | solution.py:26
  207.6 5.9 %collective-permute-start.3 = (f32[18,1]{1,0:T(8,128)S(1)}, f32[18,1]{1,0:T(8,128)S(1)}, u32[]{:S(2)}, u32[]{:S(2)}) collective-permute-start(f32[18,1]{1,0:T(8,128)S(1)} %get-tuple-element.474), channel_id=1, source_target_pairs={{0,1},{1,2},{2,3},{3,4},{4,5},{5,6},{6,7},{7,8},{8,9},{9,10},{10,1... | collective-permute-start | bytes 224 | tf_op jit(solution)/shard_map/while/body/eval_jaxpr/ppermute | solution.py:26
  220.5 5.9 %collective-permute-start.3 = (f32[18,1]{1,0:T(8,128)S(1)}, f32[18,1]{1,0:T(8,128)S(1)}, u32[]{:S(2)}, u32[]{:S(2)}) collective-permute-start(f32[18,1]{1,0:T(8,128)S(1)} %get-tuple-element.474), channel_id=1, source_target_pairs={{0,1},{1,2},{2,3},{3,4},{4,5},{5,6},{6,7},{7,8},{8,9},{9,10},{10,1... | collective-permute-start | bytes 224 | tf_op jit(solution)/shard_map/while/body/eval_jaxpr/ppermute | solution.py:26
  233.4 5.9 %collective-permute-start.3 = (f32[18,1]{1,0:T(8,128)S(1)}, f32[18,1]{1,0:T(8,128)S(1)}, u32[]{:S(2)}, u32[]{:S(2)}) collective-permute-start(f32[18,1]{1,0:T(8,128)S(1)} %get-tuple-element.474), channel_id=1, source_target_pairs={{0,1},{1,2},{2,3},{3,4},{4,5},{5,6},{6,7},{7,8},{8,9},{9,10},{10,1... | collective-permute-start | bytes 224 | tf_op jit(solution)/shard_map/while/body/eval_jaxpr/ppermute | solution.py:26
  259.2 5.9 %collective-permute-start.3 = (f32[18,1]{1,0:T(8,128)S(1)}, f32[18,1]{1,0:T(8,128)S(1)}, u32[]{:S(2)}, u32[]{:S(2)}) collective-permute-start(f32[18,1]{1,0:T(8,128)S(1)} %get-tuple-element.474), channel_id=1, source_target_pairs={{0,1},{1,2},{2,3},{3,4},{4,5},{5,6},{6,7},{7,8},{8,9},{9,10},{10,1... | collective-permute-start | bytes 224 | tf_op jit(solution)/shard_map/while/body/eval_jaxpr/ppermute | solution.py:26
  272.1 5.9 %collective-permute-start.3 = (f32[18,1]{1,0:T(8,128)S(1)}, f32[18,1]{1,0:T(8,128)S(1)}, u32[]{:S(2)}, u32[]{:S(2)}) collective-permute-start(f32[18,1]{1,0:T(8,128)S(1)} %get-tuple-element.474), channel_id=1, source_target_pairs={{0,1},{1,2},{2,3},{3,4},{4,5},{5,6},{6,7},{7,8},{8,9},{9,10},{10,1... | collective-permute-start | bytes 224 | tf_op jit(solution)/shard_map/while/body/eval_jaxpr/ppermute | solution.py:26
  285.0 5.9 %collective-permute-start.3 = (f32[18,1]{1,0:T(8,128)S(1)}, f32[18,1]{1,0:T(8,128)S(1)}, u32[]{:S(2)}, u32[]{:S(2)}) collective-permute-start(f32[18,1]{1,0:T(8,128)S(1)} %get-tuple-element.474), channel_id=1, source_target_pairs={{0,1},{1,2},{2,3},{3,4},{4,5},{5,6},{6,7},{7,8},{8,9},{9,10},{10,1... | collective-permute-start | bytes 224 | tf_op jit(solution)/shard_map/while/body/eval_jaxpr/ppermute | solution.py:26
  297.9 5.9 %collective-permute-start.3 = (f32[18,1]{1,0:T(8,128)S(1)}, f32[18,1]{1,0:T(8,128)S(1)}, u32[]{:S(2)}, u32[]{:S(2)}) collective-permute-start(f32[18,1]{1,0:T(8,128)S(1)} %get-tuple-element.474), channel_id=1, source_target_pairs={{0,1},{1,2},{2,3},{3,4},{4,5},{5,6},{6,7},{7,8},{8,9},{9,10},{10,1... | collective-permute-start | bytes 224 | tf_op jit(solution)/shard_map/while/body/eval_jaxpr/ppermute | solution.py:26
  (131 other events, 501.3 us)
where the time goes:
time: 575 us; the launch traced here: 564 us
  starting transfers between devices  225 us (39%)
  waiting for transfers between devices  146 us (25%)
  other arithmetic  98.8 us (17%)
  local copies, waits for them, and re-layouts  91.3 us (16%)
    ppermute x74, starting transfers between devices, with_halo(): lax.ppermute(head, axis, [((i + 1) % count, i) for i in range(count)])  172 us
    ppermute x74, waiting for transfers between devices, with_halo(): lax.ppermute(tail, axis, [(i, (i + 1) % count) for i in range(count)])  112 us
    ppermute x74, starting transfers between devices, with_halo(): lax.ppermute(tail, axis, [(i, (i + 1) % count) for i in range(count)])  50 us
    add x32, other arithmetic, single_iteration(): return (height + change, change)  43.5 us
    ppermute x74, waiting for transfers between devices, with_halo(): lax.ppermute(head, axis, [((i + 1) % count, i) for i in range(count)])  34.4 us
    slice x78, local copies, waits for them, and re-layouts, with_halo(): lax.slice_in_dim(cells, cells.shape[dim] - width, cells.shape[dim], axis=...  21.9 us
    dynamic_slice x32, local copies, waits for them, and re-layouts, single_iteration(): carries[number] * change  20.9 us
    dynamic_slice x32, local copies, waits for them, and re-layouts, single_iteration(): scales[number] * residual / diagonal_term + carries[number] * change  19.5 us
  transfers between devices with their start and end apart: 150, of which 65 were waited for; matrix products, arithmetic and copies ran while one was open for 18% of the time, Pallas kernels for 0%

commit v1 on v0

v1 whole, which is shorter than its diff:
```python
import functools

import jax
import jax.numpy as jnp
from jax import lax
from jax.experimental import pallas as pl
from jax.experimental.pallas import tpu as pltpu
from jax.sharding import PartitionSpec as P

ITERATIONS = 32

TIME_STEP = 0.1
MIX_TRACER = 0.05
MIX_MOMENTUM = 0.05
HEAT_INDEX = 0.2
SALT_INDEX = 0.2
CORIOLIS = 2.0
SURFACE_TERM = 0.0005
TRANSPORT_SCALE = 0.05

ROWS = 16
COLS = 128
GROUP = 8
TILE = (GROUP, COLS)


def chebyshev_weights(total_steps):
    low_bound = SURFACE_TERM / (SURFACE_TERM + 4.0)
    high_bound = 2.0 - low_bound
    spread_ratio = (high_bound - low_bound) / (high_bound + low_bound)
    middle = 0.5 * (high_bound + low_bound)
    weights = [1.0]
    for number in range(1, total_steps):
        if number == 1:
            weights.append(2.0 / (2.0 - spread_ratio * spread_ratio))
        else:
            weights.append(1.0 / (1.0 - spread_ratio * spread_ratio * weights[-1] / 4.0))
    return [weight / middle for weight in weights], [weight - 1.0 for weight in weights]


def lanes():
    return lax.broadcasted_iota(jnp.int32, TILE, 1)


def sublanes():
    return lax.broadcasted_iota(jnp.int32, TILE, 0)


def turn(value, by, axis=1):
    size = value.shape[axis]
    by = by % size
    return value if by == 0 else pltpu.roll(value, by, axis)


def row_of(ref, row):
    return jnp.broadcast_to(ref[pl.ds(row, 1), :], TILE)


def masked(mask, value):
    return jnp.where(mask, value, 0.0)


def pack_kernel(levels, t, s, u, v, depth, prior, to_north, to_south, to_sides, to_corners, wide):
    fields = (t, s, u, v)
    groups = -(-levels // GROUP)
    lane = lanes()
    slot = lane // 4
    near = ((lane + 4) & 63) < 8

    def body(g, corner):
        start = jnp.minimum(GROUP * g, levels - GROUP) * ROWS
        packs = []
        for pair in range(2):
            pack = jnp.zeros(TILE, jnp.float32)
            for f in range(2):
                field = 2 * pair + f
                for r in range(ROWS):
                    x = fields[field][pl.ds(start + r, GROUP, stride=ROWS), :]
                    if r < 2:
                        to_south[(r * 4 + field) * groups + g] = x
                    if r >= ROWS - 2:
                        to_north[((r - ROWS + 2) * 4 + field) * groups + g] = x
                    pack = jnp.where(slot == 16 * f + r, turn(x, 64 * f + 4 * r + 2), pack)
            to_sides[pair * groups + g] = pack
            packs.append(pack)
        both = jnp.where(near, packs[0], turn(packs[1], 8))
        place = 16 * (g % 4)
        corner = jnp.where(((lane + 4 - place) & 63) < 16, pltpu.roll(both, place, 1), corner)
        to_corners[g // 4] = corner
        return corner

    lax.fori_loop(0, groups, body, jnp.zeros(TILE, jnp.float32))
    pack = jnp.zeros(TILE, jnp.float32)
    for r in range(ROWS):
        x = row_of(depth, r)
        for f in range(2):
            pack = jnp.where(slot == 16 * f + r, turn(x, 64 * f + 4 * r + 2), pack)
    to_sides[2 * groups] = pack
    to_corners[2] = pack
    for half in range(2):
        for place, plane in ((half, depth), (2 + half, prior)):
            x = plane[GROUP * half : GROUP * (half + 1), :]
            wide[place] = x
            to_north[8 * groups + place] = x
            to_south[8 * groups + place] = x
            to_sides[2 * groups + 1 + place] = x
            to_corners[3 + place] = x


class Depths:
    def __init__(self, groups, store, depth, north, south, east, west, own, ne, nw, se, sw):
        lane = lanes()
        self.store = store
        column = lane & 3
        row = (lane // 4) & 15
        self.column, self.row = column, row
        self.lane = lane
        self.column_2 = column == 2
        self.column_low = column < 2
        d_own, d_east, d_west = own[2 * groups], east[2 * groups], west[2 * groups]
        k_ne, k_nw = turn(ne[2], 60), turn(nw[2], 60)
        k_se, k_sw = turn(se[2], 68), turn(sw[2], 68)
        self.corner_depths = (k_ne, k_nw, k_se, k_sw)
        q_west = jnp.where(self.column_low, d_west, d_own)
        q_east = jnp.where(self.column_low, d_own, d_east)
        self.side_depths = []
        for q, k_north, k_south in ((q_west, k_nw, k_sw), (q_east, k_ne, k_se)):
            self.side_depths.append((q,) + self.around(q, k_north, k_south))
        ring = self.join(q_west, q_east)
        ring_south, ring_north = self.join(k_sw, k_se), self.join(k_nw, k_ne)
        for j in range(-2, ROWS + 2):
            if j < 0:
                d = jnp.broadcast_to(south[8 * groups + 1][8 + j : 9 + j, :], TILE)
            elif j < ROWS:
                d = row_of(depth, j)
            else:
                d = jnp.broadcast_to(north[8 * groups][j - ROWS : j - ROWS + 1, :], TILE)
            store[3 * (j + 2)] = d
            if -1 <= j <= ROWS:
                edge = ring_south if j < 0 else ring_north if j == ROWS else ring
                d_e, d_w = self.sideways(d, edge, 0, min(max(j, 0), ROWS - 1))
                store[3 * (j + 2) + 1] = d_e
                store[3 * (j + 2) + 2] = d_w

    def around(self, q, k_north, k_south):
        north = jnp.where(self.row == ROWS - 1, k_north, turn(q, -4))
        south = jnp.where(self.row == 0, k_south, turn(q, 4))
        return turn(q, -1), turn(q, 1), north, south

    def join(self, q_west, q_east):
        return jnp.where(self.column_2, q_east, turn(q_west, 2))

    def sideways(self, q, edge, f, r):
        edge = turn(edge, 127 - (64 * f + 4 * r + 2))
        east = jnp.where(self.lane == COLS - 1, edge, turn(q, -1))
        west = jnp.where(self.lane == 0, edge, turn(q, 1))
        return east, west

    def of(self, j):
        return self.store[3 * (j + 2)]

    def east(self, j):
        return self.store[3 * (j + 2) + 1]

    def west(self, j):
        return self.store[3 * (j + 2) + 2]


class Edges:
    def __init__(self, dep, g, groups, level, pairs, with_laplacian, own, east, west, ne, nw, se, sw):
        place = 16 * (g % 4)
        corners = []
        for message, base in ((ne, 60), (nw, 60), (se, 68), (sw, 68)):
            tile = message[g // 4]
            corners.append(pltpu.roll(tile, (base + 128 - place) & 127, 1))
        corner_masks = [level < d for d in dep.corner_depths]
        self.ring, self.south, self.north, self.lap = {}, {}, {}, {}
        for pair in pairs:
            k_ne, k_nw, k_se, k_sw = [
                masked(m, turn(k, -8 * pair)) for k, m in zip(corners, corner_masks)
            ]
            tile_own, tile_east, tile_west = [m[pair * groups + g] for m in (own, east, west)]
            sides = []
            laps = []
            for q, d_all, k_north, k_south in (
                (jnp.where(dep.column_low, tile_west, tile_own), dep.side_depths[0], k_nw, k_sw),
                (jnp.where(dep.column_low, tile_own, tile_east), dep.side_depths[1], k_ne, k_se),
            ):
                here = level < d_all[0]
                q = masked(here, q)
                sides.append(q)
                if pair in with_laplacian:
                    e, w, n, s = dep.around(q, k_north, k_south)
                    count = sum(jnp.where(level < d, 1.0, 0.0) for d in d_all[1:])
                    laps.append(masked(here, ((e + w) + n) + s - count * q))
            self.ring[pair] = dep.join(*sides)
            self.south[pair] = dep.join(k_sw, k_se)
            self.north[pair] = dep.join(k_nw, k_ne)
            if laps:
                self.lap[pair] = dep.join(*laps)

    def edge(self, pair, j):
        return self.south[pair] if j < 0 else self.north[pair] if j == ROWS else self.ring[pair]


def field_row(ref, north, south, field, groups, g, start, j):
    if j < 0:
        return south[((j + 2) * 4 + field) * groups + g]
    if j >= ROWS:
        return north[((j - ROWS) * 4 + field) * groups + g]
    return ref[pl.ds(start + j, GROUP, stride=ROWS), :]


def prefix(x, sub):
    for by in (1, 2, 4):
        x = x + jnp.where(sub >= by, turn(x, by, 0), 0.0)
    return x


def momentum_kernel(
    levels, lat_total, row0, t, s, u, v, depth, north, south, east, west, own, ne, nw, se, sw,
    u_next, v_next, transport, store, sum_x, sum_y, sum_u, sum_v,
):
    groups = -(-levels // GROUP)
    dep = Depths(groups, store, depth, north, south, east, west, own, ne, nw, se, sw)
    sub = sublanes()
    zero = jnp.zeros(TILE, jnp.float32)
    for r in range(ROWS):
        for ref in (sum_x, sum_y):
            ref[GROUP * r : GROUP * (r + 1), :] = zero
        for ref in (sum_u, sum_v):
            ref[r] = zero
    first_row = row0[0].astype(jnp.float32)

    def body(g, carry):
        first = jnp.minimum(GROUP * g, levels - GROUP)
        start = first * ROWS
        level = (first + sub).astype(jnp.float32)
        fresh = first + sub >= GROUP * g
        last = jnp.where(g == groups - 1, GROUP * (groups - 1) - (levels - GROUP), 0)
        last = GROUP - 1 - last
        edges = Edges(dep, g, groups, level, (0, 1), (1,), own, east, west, ne, nw, se, sw)
        load = functools.partial(field_row, north=north, south=south, groups=groups, g=g, start=start)
        edge_load = edges.ring[0]
        edge_load = turn(edge_load, 64) - edge_load
        wet, q, lap, dens, dens_raw, side = {}, {}, {}, {}, {}, {}
        for j in range(-2, ROWS + 2):
            wet[j] = level < dep.of(j)
            q[j] = [masked(wet[j], load(u, field=2, j=j)), masked(wet[j], load(v, field=3, j=j))]
            if -1 <= j <= ROWS:
                dens[j] = masked(wet[j], load(s, field=1, j=j) - load(t, field=0, j=j))
            i = j - 1
            if i >= -1:
                count = (
                    jnp.where(level < dep.east(i), 1.0, 0.0) + jnp.where(level < dep.west(i), 1.0, 0.0)
                ) + (jnp.where(wet[i + 1], 1.0, 0.0) + jnp.where(wet[i - 1], 1.0, 0.0))
                lap[i] = []
                for f in range(2):
                    e, w = dep.sideways(
                        q[i][f], edges.edge(1, i), f, min(max(i, 0), ROWS - 1)
                    )
                    total = (e + w) + (q[i + 1][f] + q[i - 1][f])
                    lap[i].append((masked(wet[i], total - count * q[i][f]), count))
            r = j - 2
            if r >= 0:
                mixes = []
                for f in range(2):
                    here, count = lap[r][f]
                    e, w = dep.sideways(here, edges.lap[1], f, r)
                    mixes.append((e + w) + (lap[r + 1][f][0] + lap[r - 1][f][0]) - count * here)
                e, w = dep.sideways(dens[r], edge_load, 0, r)
                grad_x = prefix(e - w, sub) + row_of(sum_x, GROUP * r + last)
                grad_y = prefix(dens[r + 1] - dens[r - 1], sub) + row_of(sum_y, GROUP * r + last)
                sum_x[GROUP * r : GROUP * (r + 1), :] = grad_x
                sum_y[GROUP * r : GROUP * (r + 1), :] = grad_y
                turning = TIME_STEP * CORIOLIS * (2.0 * (first_row + (r + 0.5)) / lat_total - 1.0)
                pull = TIME_STEP * 0.5 * SALT_INDEX
                mix = TIME_STEP * MIX_MOMENTUM
                new_u = masked(
                    wet[r], q[r][0] + ((turning * q[r][1] - pull * grad_x) - mix * mixes[0])
                )
                new_v = masked(
                    wet[r], q[r][1] - ((turning * q[r][0] + pull * grad_y) + mix * mixes[1])
                )
                u_next[pl.ds(start + r, GROUP, stride=ROWS), :] = new_u
                v_next[pl.ds(start + r, GROUP, stride=ROWS), :] = new_v
                sum_u[r] += masked(fresh, new_u)
                sum_v[r] += masked(fresh, new_v)
        return carry

    lax.fori_loop(0, groups, body, 0)
    for r in range(ROWS):
        transport[0, r : r + 1, :] = jnp.sum(sum_u[r], axis=0, keepdims=True)
        transport[1, r : r + 1, :] = jnp.sum(sum_v[r], axis=0, keepdims=True)


def tracer_kernel(
    levels, t, s, u, v, depth, north, south, east, west, own, ne, nw, se, sw, t_next, s_next, store
):
    groups = -(-levels // GROUP)
    dep = Depths(groups, store, depth, north, south, east, west, own, ne, nw, se, sw)
    sub = sublanes()

    def body(g, carry):
        first = jnp.minimum(GROUP * g, levels - GROUP)
        start = first * ROWS
        level = (first + sub).astype(jnp.float32)
        edges = Edges(dep, g, groups, level, (0, 1), (0,), own, east, west, ne, nw, se, sw)
        load = functools.partial(field_row, north=north, south=south, groups=groups, g=g, start=start)
        wet, q, sides, lap, flow = {}, {}, {}, {}, {}
        for j in range(-2, ROWS + 2):
            wet[j] = level < dep.of(j)
            q[j] = [masked(wet[j], load(t, field=0, j=j)), masked(wet[j], load(s, field=1, j=j))]
            if -1 <= j <= ROWS:
                flow[j] = [masked(wet[j], load(u, field=2, j=j)), masked(wet[j], load(v, field=3, j=j))]
            i = j - 1
            if i >= -1:
                count = (
                    jnp.where(level < dep.east(i), 1.0, 0.0) + jnp.where(level < dep.west(i), 1.0, 0.0)
                ) + (jnp.where(wet[i + 1], 1.0, 0.0) + jnp.where(wet[i - 1], 1.0, 0.0))
                lap[i], sides[i] = [], []
                for f in range(2):
                    e, w = dep.sideways(
                        q[i][f], edges.edge(0, i), f, min(max(i, 0), ROWS - 1)
                    )
                    sides[i].append((e, w))
                    total = (e + w) + (q[i + 1][f] + q[i - 1][f])
                    lap[i].append((masked(wet[i], total - count * q[i][f]), count))
            r = j - 2
            if r >= 0:
                e, w = dep.sideways(flow[r][0], edges.ring[1], 0, r)
                u_e = masked(level < dep.east(r), flow[r][0] + e)
                u_w = masked(level < dep.west(r), flow[r][0] + w)
                v_n = masked(wet[r + 1], flow[r][1] + flow[r + 1][1])
                v_s = masked(wet[r - 1], flow[r][1] + flow[r - 1][1])
                for f, out in ((0, t_next), (1, s_next)):
                    here, count = lap[r][f]
                    e, w = dep.sideways(here, edges.lap[0], f, r)
                    mix = (e + w) + (lap[r + 1][f][0] + lap[r - 1][f][0]) - count * here
                    mid = q[r][f]
                    e, w = sides[r][f]
                    advected = (u_e * (mid + e) - u_w * (mid + w)) + (
                        v_n * (mid + q[r + 1][f]) - v_s * (mid + q[r - 1][f])
                    )
                    out[pl.ds(start + r, GROUP, stride=ROWS), :] = masked(
                        wet[r],
                        mid - (0.25 * TIME_STEP * advected + TIME_STEP * MIX_TRACER * mix),
                    )
        return carry

    lax.fori_loop(0, groups, body, 0)


PLACES = [(b, c) for b in (-2, -1, 0, 1, 2) for c in (-1, 0, 1)]
STEPS = 5 * ROWS // GROUP


class Plane:
    def __init__(self, own, rim):
        self.own, self.rim = own, rim

    def map(self, other, fn):
        if isinstance(other, Plane):
            return Plane(
                [fn(a, b) for a, b in zip(self.own, other.own)],
                [fn(a, b) for a, b in zip(self.rim, other.rim)],
            )
        return Plane([fn(a, other) for a in self.own], [fn(a, other) for a in self.rim])

    def __add__(self, other):
        return self.map(other, lambda a, b: a + b)

    def __sub__(self, other):
        return self.map(other, lambda a, b: a - b)

    def __mul__(self, other):
        return self.map(other, lambda a, b: a * b)

    def low(self, other):
        return self.map(other, jnp.minimum)

    def side(self, by, lane):
        at = lanes() == lane
        pairs = [(turn(a, by), turn(b, by)) for a, b in zip(self.own, self.rim)]
        return Plane([jnp.where(at, b, a) for a, b in pairs], [jnp.where(at, a, b) for a, b in pairs])

    def east(self):
        return self.side(-1, COLS - 1)

    def west(self):
        return self.side(1, 0)

    def north(self):
        return Plane(*[x[1:] + [turn(x[0], -1, 0)] for x in (self.own, self.rim)])

    def south(self):
        return Plane(*[[turn(x[-1], 1, 0)] + x[:-1] for x in (self.own, self.rim)])


def solve_kernel(levels, *refs):
    count = len(PLACES)
    wide, moved = refs[:count], refs[count : 2 * count]
    offsets = {}
    out = refs[2 * count]
    own_buf, rim_buf = refs[2 * count + 1 :]
    lane = lanes()
    east_half = lane < COLS // 2

    def gather(read):
        for b in range(-2, 3):
            for half in range(2):
                at = ROWS * (b + 2) + GROUP * half
                own_buf[at : at + GROUP, :] = read((b, 0), half)
                rim_buf[at : at + GROUP, :] = jnp.where(
                    east_half, read((b, 1), half), read((b, -1), half)
                )
        return Plane(
            *[[buf[pl.ds(t, GROUP, stride=STEPS), :] for t in range(STEPS)] for buf in (own_buf, rim_buf)]
        )

    def wide_tile(plane):
        def read(place, half):
            ref = wide[PLACES.index(place)]
            return ref[ref.shape[0] - 4 + 2 * plane + half]

        return read

    def moved_tile(plane):
        return lambda place, half: moved[PLACES.index(place)][plane, GROUP * half : GROUP * (half + 1), :]

    depth = gather(wide_tile(0))
    prior = gather(wide_tile(1))
    zonal = gather(moved_tile(0))
    northward = gather(moved_tile(1))

    ocean = depth.map(0.0, lambda a, b: jnp.where(a > b, 1.0, 0.0))
    depth_east, depth_north = depth.low(depth.east()), depth.low(depth.north())
    zonal_flow = zonal.map(depth_east, lambda a, b: masked(b > 0.0, a))
    north_flow = northward.map(depth_north, lambda a, b: masked(b > 0.0, a))
    divergence = (zonal_flow - zonal_flow.west()) + (north_flow - north_flow.south())
    right_side = prior * SURFACE_TERM - divergence * TRANSPORT_SCALE
    east_face, north_face = depth_east * (1.0 / levels), depth_north * (1.0 / levels)
    west_face, south_face = east_face.west(), north_face.south()
    diagonal = (((east_face + west_face) + north_face) + south_face) + SURFACE_TERM
    inverse = diagonal.map(1.0, lambda a, b: b / a)
    right_side, east_face, west_face, north_face, south_face = [
        x * inverse for x in (right_side, east_face, west_face, north_face, south_face)
    ]
    height, change = prior, None
    scales, carries = chebyshev_weights(ITERATIONS)
    for scale, carry in zip(scales, carries):
        spread = (east_face * height.east() + west_face * height.west()) + (
            north_face * height.north() + south_face * height.south()
        )
        residual = (right_side - height) + spread
        step = residual * scale
        change = step if change is None else step + change * carry
        height = height + change
    height = height * ocean
    for t in range(STEPS):
        own_buf[pl.ds(t, GROUP, stride=STEPS), :] = height.own[t]
    out[...] = own_buf[2 * ROWS : 3 * ROWS, :]


def moved_by(value, lat_by, lon_by):
    lat, lon = lax.axis_size("lat"), lax.axis_size("lon")
    pairs = [
        ((i + lat_by) * lon + (j + lon_by) % lon, i * lon + j)
        for i in range(lat)
        if 0 <= i + lat_by < lat
        for j in range(lon)
    ]
    return lax.ppermute(value, ("lat", "lon"), pairs)


def shape(*dims):
    return jax.ShapeDtypeStruct(dims, jnp.float32)


VMEM = pl.BlockSpec(memory_space=pltpu.VMEM)


def call(kernel, outs, scratch, *args, smem=0, cost=0):
    return pl.pallas_call(
        kernel,
        out_shape=outs,
        in_specs=[pl.BlockSpec(memory_space=pltpu.SMEM)] * smem + [VMEM] * (len(args) - smem),
        out_specs=jax.tree.map(lambda _: VMEM, outs),
        scratch_shapes=scratch,
        compiler_params=pltpu.CompilerParams(vmem_limit_bytes=32 * 2**20),
        cost_estimate=pl.CostEstimate(flops=cost, bytes_accessed=4 * 2**20, transcendentals=0),
    )(*args)


def per_device(
    heat_anomaly,
    saltiness_anomaly,
    zonal_current_array,
    meridional_current_array,
    sea_height_prior,
    ocean_layer_number,
):
    levels, rows, cols = heat_anomaly.shape
    groups = -(-levels // GROUP)
    lat_total = rows * lax.axis_size("lat")
    fields = [
        x.reshape(levels * rows, cols)
        for x in (heat_anomaly, saltiness_anomaly, zonal_current_array, meridional_current_array)
    ]
    depth = ocean_layer_number.astype(jnp.float32)
    to_north, to_south, own, corners, wide = call(
        functools.partial(pack_kernel, levels),
        (
            shape(8 * groups + 4, *TILE),
            shape(8 * groups + 4, *TILE),
            shape(2 * groups + 5, *TILE),
            shape(7, *TILE),
            shape(4, *TILE),
        ),
        [],
        *fields,
        depth,
        sea_height_prior,
        cost=10**7,
    )
    north, south = moved_by(to_south, 1, 0), moved_by(to_north, -1, 0)
    east, west = moved_by(own, 0, 1), moved_by(own, 0, -1)
    diagonals = {(i, j): moved_by(corners, i, j) for i in (1, -1) for j in (1, -1)}
    ne, nw, se, sw = (diagonals[p] for p in ((1, 1), (1, -1), (-1, 1), (-1, -1)))
    wides = {(0, 0): wide, (1, 0): north, (-1, 0): south, (0, 1): east, (0, -1): west, **diagonals}
    for i in (2, -2):
        for j in (-1, 0, 1):
            wides[i, j] = moved_by(wide, i, j)

    args = (*fields, depth, north, south, east, west, own, ne, nw, se, sw)
    store = pltpu.VMEM((3 * (ROWS + 4), *TILE), jnp.float32)
    row0 = (lax.axis_index("lat") * rows).astype(jnp.int32).reshape(1)
    u_next, v_next, transport = call(
        functools.partial(momentum_kernel, levels, lat_total),
        (shape(levels * rows, cols), shape(levels * rows, cols), shape(2, rows, cols)),
        [store]
        + [pltpu.VMEM((GROUP * ROWS, COLS), jnp.float32)] * 2
        + [pltpu.VMEM((ROWS, *TILE), jnp.float32)] * 2,
        row0,
        *args,
        smem=1,
        cost=10**7,
    )
    moved = [transport if p == (0, 0) else moved_by(transport, *p) for p in PLACES]
    t_next, s_next = call(
        functools.partial(tracer_kernel, levels),
        (shape(levels * rows, cols), shape(levels * rows, cols)),
        [store],
        *args,
        cost=10**7,
    )
    height = call(
        functools.partial(solve_kernel, levels),
        shape(rows, cols),
        [pltpu.VMEM((5 * ROWS, COLS), jnp.float32)] * 2,
        *[wides[p] for p in PLACES],
        *moved,
        cost=10**7,
    )
    return (
        *[x.reshape(levels, rows, cols) for x in (t_next, s_next, u_next, v_next)],
        height,
    )


def solution(mesh):
    cells, plane = P(None, "lat", "lon"), P("lat", "lon")
    return jax.shard_map(
        per_device,
        mesh=mesh,
        in_specs=(cells,) * 4 + (plane,) * 2,
        out_specs=(cells,) * 4 + (plane,),
        check_vma=False,
    )
```

time: 575 us -> 137 us (0.24)
  the two profiles are of different devices: /device:TPU:1 before, /device:TPU:7 now
where the time goes in v1:
time: 137 us; the launch traced here: 136 us
  starting transfers between devices  94.7 us (69%)
  waiting for transfers between devices  18.5 us (14%)
  Pallas kernels  17.1 us (12%)
  local copies, waits for them, and re-layouts  4.16 us (3%)
    ppermute x28, starting transfers between devices, moved_by(): return lax.ppermute(value, ('lat', 'lon'), pairs)  94.7 us
    ppermute x28, waiting for transfers between devices, moved_by(): return lax.ppermute(value, ('lat', 'lon'), pairs)  18.5 us
    pallas_call x4, Pallas kernels, call(): pl.pallas_call(kernel, out_shape=outs, in_specs=[pl.BlockSpec(memory_spac...  17.1 us
    unnamed x18, local copies, waits for them, and re-layouts  4.16 us
  transfers between devices with their start and end apart: 28, of which 3 were waited for; matrix products, arithmetic and copies ran while one was open for 0% of the time, Pallas kernels for 8%

profile of v1, /device:TPU:7, one launch (start us, length us, event | category | flops | bytes accessed | tf_op | source)
XLA Modules:
  0.0 136.2 jit_solution(4227671775621460579)
XLA Ops:
  5.5 2.1 %shard_map.101 = (f32[68,8,128]{2,1,0:T(8,128)S(1)}, f32[68,8,128]{2,1,0:T(8,128)S(1)}, f32[21,8,128]{2,1,0:T(8,128)S(1)}, f32[7,8,128]{2,1,0:T(8,128)S(1)}, f32[4,8,128]{2,1,0:T(8,128)S(1)}) custom-call(f32[992,128]{1,0:T(8,128)S(1)} %bitcast.9, f32[992,128]{1,0:T(8,128)S(1)} %bitcast.12, f32[992,128]{1,0:T(8,128)S(1)} %bitcast.15, ...), custom_call_target="tpu_custom_call" | custom-call | flops 10000000 | bytes 4194304 | tf_op jit(solution)/shard_map/pallas_call | solution.py:484
  7.6 2.6 %collective-permute-start = (f32[68,8,128]{2,1,0:T(8,128)S(1)}, f32[68,8,128]{2,1,0:T(8,128)S(1)}, u32[]{:S(2)}, u32[]{:S(2)}) collective-permute-start(f32[68,8,128]{2,1,0:T(8,128)S(1)} %get-tuple-element.15), channel_id=1, source_target_pairs={{32,0},{33,1},{34,2},{35,3},{36,4},{37,5},{38,6},{39,7},{40,8},{41... | collective-permute-start | bytes 835592 | tf_op jit(solution)/shard_map/ppermute | solution.py:473
  10.2 1.3 collective-permute-start.1
  11.5 10.9 %collective-permute-start.4 = (f32[7,8,128]{2,1,0:T(8,128)S(1)}, f32[7,8,128]{2,1,0:T(8,128)S(1)}, u32[]{:S(2)}, u32[]{:S(2)}) collective-permute-start(f32[7,8,128]{2,1,0:T(8,128)S(1)} %get-tuple-element.18), channel_id=1, source_target_pairs={{33,0},{34,1},{35,2},{36,3},{37,4},{38,5},{39,6},{40,7},{41,8},{42... | collective-permute-start | bytes 86024 | tf_op jit(solution)/shard_map/ppermute | solution.py:473
  22.4 1.3 collective-permute-start.5
  23.7 6.7 %collective-permute-start.2 = (f32[21,8,128]{2,1,0:T(8,128)S(1)}, f32[21,8,128]{2,1,0:T(8,128)S(1)}, u32[]{:S(2)}, u32[]{:S(2)}) collective-permute-start(f32[21,8,128]{2,1,0:T(8,128)S(1)} %get-tuple-element.17.own), channel_id=1, source_target_pairs={{1,0},{2,1},{3,2},{4,3},{5,4},{6,5},{7,6},{8,7},{9,8},{10,9},{11,1... | collective-permute-start | bytes 258056 | tf_op jit(solution)/shard_map/ppermute | solution.py:473
  30.4 1.3 collective-permute-start.6
  31.7 3.9 %collective-permute-done.6.se.refs_5_ = f32[7,8,128]{2,1,0:T(8,128)S(1)} collective-permute-done((f32[7,8,128]{2,1,0:T(8,128)S(1)}, f32[7,8,128]{2,1,0:T(8,128)S(1)}, u32[]{:S(2)}, u32[]{:S(2)}) %collective-permute-start.6) | collective-permute-done | bytes 28704 | tf_op jit(solution)/shard_map/ppermute | solution.py:473
  35.6 1.3 collective-permute-start.7
  36.9 11.2 %collective-permute-done.7.sw.refs_3_ = f32[7,8,128]{2,1,0:T(8,128)S(1)} collective-permute-done((f32[7,8,128]{2,1,0:T(8,128)S(1)}, f32[7,8,128]{2,1,0:T(8,128)S(1)}, u32[]{:S(2)}, u32[]{:S(2)}) %collective-permute-start.7) | collective-permute-done | bytes 28704 | tf_op jit(solution)/shard_map/ppermute | solution.py:473
  48.1 1.3 collective-permute-start.10
  49.4 4.9 %collective-permute-start.11 = (f32[4,8,128]{2,1,0:T(8,128)S(1)}, f32[4,8,128]{2,1,0:T(8,128)S(1)}, u32[]{:S(2)}, u32[]{:S(2)}) collective-permute-start(f32[4,8,128]{2,1,0:T(8,128)S(1)} %get-tuple-element.23.refs_7_), channel_id=1, source_target_pairs={{95,0},{64,1},{65,2},{66,3},{67,4},{68,5},{69,6},{70,7},{71,8},{72... | collective-permute-start | bytes 49160 | tf_op jit(solution)/shard_map/ppermute | solution.py:473
  54.3 2.2 %collective-permute-start.12 = (f32[4,8,128]{2,1,0:T(8,128)S(1)}, f32[4,8,128]{2,1,0:T(8,128)S(1)}, u32[]{:S(2)}, u32[]{:S(2)}) collective-permute-start(f32[4,8,128]{2,1,0:T(8,128)S(1)} %get-tuple-element.23.refs_7_), channel_id=1, source_target_pairs={{64,0},{65,1},{66,2},{67,3},{68,4},{69,5},{70,6},{71,7},{72,8},{73... | collective-permute-start | bytes 49160 | tf_op jit(solution)/shard_map/ppermute | solution.py:473
  56.5 6.4 %collective-permute-start.13 = (f32[4,8,128]{2,1,0:T(8,128)S(1)}, f32[4,8,128]{2,1,0:T(8,128)S(1)}, u32[]{:S(2)}, u32[]{:S(2)}) collective-permute-start(f32[4,8,128]{2,1,0:T(8,128)S(1)} %get-tuple-element.23.refs_7_), channel_id=1, source_target_pairs={{65,0},{66,1},{67,2},{68,3},{69,4},{70,5},{71,6},{72,7},{73,8},{74... | collective-permute-start | bytes 49160 | tf_op jit(solution)/shard_map/ppermute | solution.py:473
  62.9 1.3 collective-permute-start.8
  64.3 5.5 %shard_map.103 = (f32[992,128]{1,0:T(8,128)}, f32[992,128]{1,0:T(8,128)}, f32[2,16,128]{2,1,0:T(8,128)S(1)}) custom-call(s32[1]{0:T(128)} %bitcast.6.row0, f32[992,128]{1,0:T(8,128)S(1)} %bitcast.10, f32[992,128]{1,0:T(8,128)S(1)} %bitcast.13, f32[992,128]{1,0:T(8,128)S(1)} %bitcast.16, f32[992,128]{1,0:T(8,128)S(1)} %bitcast.19, ...), custom_call_target="tpu_custom_call" | custom-call | flops 10000000 | bytes 4194304 | tf_op jit(solution)/shard_map/pallas_call | solution.py:484
  69.8 1.3 collective-permute-start.9
  71.1 1.3 collective-permute-start.14
  72.4 1.3 collective-permute-start.15
  73.7 1.3 collective-permute-start.16
  75.0 1.3 collective-permute-start.17
  76.3 1.3 collective-permute-start.18
  77.7 3.4 %collective-permute-done.14.refs_15_ = f32[2,16,128]{2,1,0:T(8,128)S(1)} collective-permute-done((f32[2,16,128]{2,1,0:T(8,128)S(1)}, f32[2,16,128]{2,1,0:T(8,128)S(1)}, u32[]{:S(2)}, u32[]{:S(2)}) %collective-permute-start.14) | collective-permute-done | bytes 16416 | tf_op jit(solution)/shard_map/ppermute | solution.py:473
  82.5 4.8 %collective-permute-start.21 = (f32[2,16,128]{2,1,0:T(8,128)S(1)}, f32[2,16,128]{2,1,0:T(8,128)S(1)}, u32[]{:S(2)}, u32[]{:S(2)}) collective-permute-start(f32[2,16,128]{2,1,0:T(8,128)S(1)} %get-tuple-element.24.refs_22_), channel_id=1, source_target_pairs={{1,0},{2,1},{3,2},{4,3},{5,4},{6,5},{7,6},{8,7},{9,8},{10,9},{11,1... | collective-permute-start | bytes 49160 | tf_op jit(solution)/shard_map/ppermute | solution.py:473
  87.2 3.2 %collective-permute-start.22 = (f32[2,16,128]{2,1,0:T(8,128)S(1)}, f32[2,16,128]{2,1,0:T(8,128)S(1)}, u32[]{:S(2)}, u32[]{:S(2)}) collective-permute-start(f32[2,16,128]{2,1,0:T(8,128)S(1)} %get-tuple-element.24.refs_22_), channel_id=1, source_target_pairs={{63,0},{32,1},{33,2},{34,3},{35,4},{36,5},{37,6},{38,7},{39,8},{40... | collective-permute-start | bytes 49160 | tf_op jit(solution)/shard_map/ppermute | solution.py:473
  90.5 5.5 %collective-permute-start.23 = (f32[2,16,128]{2,1,0:T(8,128)S(1)}, f32[2,16,128]{2,1,0:T(8,128)S(1)}, u32[]{:S(2)}, u32[]{:S(2)}) collective-permute-start(f32[2,16,128]{2,1,0:T(8,128)S(1)} %get-tuple-element.24.refs_22_), channel_id=1, source_target_pairs={{32,0},{33,1},{34,2},{35,3},{36,4},{37,5},{38,6},{39,7},{40,8},{41... | collective-permute-start | bytes 49160 | tf_op jit(solution)/shard_map/ppermute | solution.py:473
  96.0 10.4 %collective-permute-start.24 = (f32[2,16,128]{2,1,0:T(8,128)S(1)}, f32[2,16,128]{2,1,0:T(8,128)S(1)}, u32[]{:S(2)}, u32[]{:S(2)}) collective-permute-start(f32[2,16,128]{2,1,0:T(8,128)S(1)} %get-tuple-element.24.refs_22_), channel_id=1, source_target_pairs={{33,0},{34,1},{35,2},{36,3},{37,4},{38,5},{39,6},{40,7},{41,8},{42... | collective-permute-start | bytes 49160 | tf_op jit(solution)/shard_map/ppermute | solution.py:473
  106.5 1.4 %collective-permute-start.25 = (f32[2,16,128]{2,1,0:T(8,128)S(1)}, f32[2,16,128]{2,1,0:T(8,128)S(1)}, u32[]{:S(2)}, u32[]{:S(2)}) collective-permute-start(f32[2,16,128]{2,1,0:T(8,128)S(1)} %get-tuple-element.24.refs_22_), channel_id=1, source_target_pairs={{95,0},{64,1},{65,2},{66,3},{67,4},{68,5},{69,6},{70,7},{71,8},{72... | collective-permute-start | bytes 49160 | tf_op jit(solution)/shard_map/ppermute | solution.py:473
  107.9 6.6 %collective-permute-start.26 = (f32[2,16,128]{2,1,0:T(8,128)S(1)}, f32[2,16,128]{2,1,0:T(8,128)S(1)}, u32[]{:S(2)}, u32[]{:S(2)}) collective-permute-start(f32[2,16,128]{2,1,0:T(8,128)S(1)} %get-tuple-element.24.refs_22_), channel_id=1, source_target_pairs={{64,0},{65,1},{66,2},{67,3},{68,4},{69,5},{70,6},{71,7},{72,8},{73... | collective-permute-start | bytes 49160 | tf_op jit(solution)/shard_map/ppermute | solution.py:473
  114.6 12.1 %collective-permute-start.27 = (f32[2,16,128]{2,1,0:T(8,128)S(1)}, f32[2,16,128]{2,1,0:T(8,128)S(1)}, u32[]{:S(2)}, u32[]{:S(2)}) collective-permute-start(f32[2,16,128]{2,1,0:T(8,128)S(1)} %get-tuple-element.24.refs_22_), channel_id=1, source_target_pairs={{65,0},{66,1},{67,2},{68,3},{69,4},{70,5},{71,6},{72,7},{73,8},{74... | collective-permute-start | bytes 49160 | tf_op jit(solution)/shard_map/ppermute | solution.py:473
  126.7 5.4 %shard_map.102 = (f32[992,128]{1,0:T(8,128)}, f32[992,128]{1,0:T(8,128)}) custom-call(f32[992,128]{1,0:T(8,128)S(1)} %bitcast.11, f32[992,128]{1,0:T(8,128)S(1)} %bitcast.14, f32[992,128]{1,0:T(8,128)S(1)} %bitcast.17, f32[992,128]{1,0:T(8,128)S(1)} %bitcast.20, f32[16,128]{1,0:T(8,128)S(1)} %convert_element_type.3.depth, ...), custom_call_target="tpu_custom_call" | custom-call | flops 10000000 | bytes 4194304 | tf_op jit(solution)/shard_map/pallas_call | solution.py:484
  132.1 4.2 %shard_map.104 = f32[16,128]{1,0:T(8,128)} custom-call(f32[4,8,128]{2,1,0:T(8,128)S(1)} %collective-permute-done.8.refs_0_, f32[4,8,128]{2,1,0:T(8,128)S(1)} %collective-permute-done.9.refs_1_, f32[4,8,128]{2,1,0:T(8,128)S(1)} %collective-permute-done.10.refs_2_, f32[7,8,128]{2,1,0:T(8,128)S(1)} %collective-permute-done.7.sw.refs_3_, ...), custom_call_target="tpu_custom_call" | custom-call | flops 10000000 | bytes 4194304 | tf_op jit(solution)/shard_map/pallas_call | solution.py:484
  (47 shorter events, 6.3 us)
Async XLA Ops:
  5.5 58.7 %copy-start.1 = (f32[62,16,128]{2,1,0:T(8,128)S(1)}, f32[62,16,128]{2,1,0:T(8,128)}, u32[]{:S(2)}) copy-start(f32[62,16,128]{2,1,0:T(8,128)} %param.6) | copy-start | bytes 1523716
  5.5 58.8 %copy-start.3 = (f32[62,16,128]{2,1,0:T(8,128)S(1)}, f32[62,16,128]{2,1,0:T(8,128)}, u32[]{:S(2)}) copy-start(f32[62,16,128]{2,1,0:T(8,128)} %param.7) | copy-start | bytes 1523716
  5.5 58.8 %copy-start.5 = (f32[62,16,128]{2,1,0:T(8,128)S(1)}, f32[62,16,128]{2,1,0:T(8,128)}, u32[]{:S(2)}) copy-start(f32[62,16,128]{2,1,0:T(8,128)} %param.8) | copy-start | bytes 1523716
  5.5 58.8 %copy-start.7 = (f32[62,16,128]{2,1,0:T(8,128)S(1)}, f32[62,16,128]{2,1,0:T(8,128)}, u32[]{:S(2)}) copy-start(f32[62,16,128]{2,1,0:T(8,128)} %param.9) | copy-start | bytes 1523716
  7.6 48.9 %collective-permute-start = (f32[68,8,128]{2,1,0:T(8,128)S(1)}, f32[68,8,128]{2,1,0:T(8,128)S(1)}, u32[]{:S(2)}, u32[]{:S(2)}) collective-permute-start(f32[68,8,128]{2,1,0:T(8,128)S(1)} %get-tuple-element.15), channel_id=1, source_target_pairs={{32,0},{33,1},{34,2},{35,3},{36,4},{37,5},{38,6},{39,7},{40,8},{41... | collective-permute-start | bytes 835592 | tf_op jit(solution)/shard_map/ppermute | solution.py:473
  10.2 52.7 %collective-permute-start.1 = (f32[68,8,128]{2,1,0:T(8,128)S(1)}, f32[68,8,128]{2,1,0:T(8,128)S(1)}, u32[]{:S(2)}, u32[]{:S(2)}) collective-permute-start(f32[68,8,128]{2,1,0:T(8,128)S(1)} %get-tuple-element.16), channel_id=1, source_target_pairs={{0,32},{1,33},{2,34},{3,35},{4,36},{5,37},{6,38},{7,39},{8,40},{9,... | collective-permute-start | bytes 835592 | tf_op jit(solution)/shard_map/ppermute | solution.py:473
  11.5 18.9 %collective-permute-start.4 = (f32[7,8,128]{2,1,0:T(8,128)S(1)}, f32[7,8,128]{2,1,0:T(8,128)S(1)}, u32[]{:S(2)}, u32[]{:S(2)}) collective-permute-start(f32[7,8,128]{2,1,0:T(8,128)S(1)} %get-tuple-element.18), channel_id=1, source_target_pairs={{33,0},{34,1},{35,2},{36,3},{37,4},{38,5},{39,6},{40,7},{41,8},{42... | collective-permute-start | bytes 86024 | tf_op jit(solution)/shard_map/ppermute | solution.py:473
  22.4 8.0 %collective-permute-start.5 = (f32[7,8,128]{2,1,0:T(8,128)S(1)}, f32[7,8,128]{2,1,0:T(8,128)S(1)}, u32[]{:S(2)}, u32[]{:S(2)}) collective-permute-start(f32[7,8,128]{2,1,0:T(8,128)S(1)} %get-tuple-element.18), channel_id=1, source_target_pairs={{63,0},{32,1},{33,2},{34,3},{35,4},{36,5},{37,6},{38,7},{39,8},{40... | collective-permute-start | bytes 86024 | tf_op jit(solution)/shard_map/ppermute | solution.py:473
  23.7 25.6 %collective-permute-start.2 = (f32[21,8,128]{2,1,0:T(8,128)S(1)}, f32[21,8,128]{2,1,0:T(8,128)S(1)}, u32[]{:S(2)}, u32[]{:S(2)}) collective-permute-start(f32[21,8,128]{2,1,0:T(8,128)S(1)} %get-tuple-element.17.own), channel_id=1, source_target_pairs={{1,0},{2,1},{3,2},{4,3},{5,4},{6,5},{7,6},{8,7},{9,8},{10,9},{11,1... | collective-permute-start | bytes 258056 | tf_op jit(solution)/shard_map/ppermute | solution.py:473
  30.4 23.9 %collective-permute-start.3 = (f32[21,8,128]{2,1,0:T(8,128)S(1)}, f32[21,8,128]{2,1,0:T(8,128)S(1)}, u32[]{:S(2)}, u32[]{:S(2)}) collective-permute-start(f32[21,8,128]{2,1,0:T(8,128)S(1)} %get-tuple-element.17.own), channel_id=1, source_target_pairs={{31,0},{0,1},{1,2},{2,3},{3,4},{4,5},{5,6},{6,7},{7,8},{8,9},{9,10... | collective-permute-start | bytes 258056 | tf_op jit(solution)/shard_map/ppermute | solution.py:473
  30.4 5.2 %collective-permute-start.6 = (f32[7,8,128]{2,1,0:T(8,128)S(1)}, f32[7,8,128]{2,1,0:T(8,128)S(1)}, u32[]{:S(2)}, u32[]{:S(2)}) collective-permute-start(f32[7,8,128]{2,1,0:T(8,128)S(1)} %get-tuple-element.18), channel_id=1, source_target_pairs={{1,32},{2,33},{3,34},{4,35},{5,36},{6,37},{7,38},{8,39},{9,40},{10... | collective-permute-start | bytes 86024 | tf_op jit(solution)/shard_map/ppermute | solution.py:473
  35.6 12.5 %collective-permute-start.7 = (f32[7,8,128]{2,1,0:T(8,128)S(1)}, f32[7,8,128]{2,1,0:T(8,128)S(1)}, u32[]{:S(2)}, u32[]{:S(2)}) collective-permute-start(f32[7,8,128]{2,1,0:T(8,128)S(1)} %get-tuple-element.18), channel_id=1, source_target_pairs={{31,32},{0,33},{1,34},{2,35},{3,36},{4,37},{5,38},{6,39},{7,40},{8... | collective-permute-start | bytes 86024 | tf_op jit(solution)/shard_map/ppermute | solution.py:473
  48.1 21.7 %collective-permute-start.10 = (f32[4,8,128]{2,1,0:T(8,128)S(1)}, f32[4,8,128]{2,1,0:T(8,128)S(1)}, u32[]{:S(2)}, u32[]{:S(2)}) collective-permute-start(f32[4,8,128]{2,1,0:T(8,128)S(1)} %get-tuple-element.23.refs_7_), channel_id=1, source_target_pairs={{1,64},{2,65},{3,66},{4,67},{5,68},{6,69},{7,70},{8,71},{9,72},{10... | collective-permute-start | bytes 49160 | tf_op jit(solution)/shard_map/ppermute | solution.py:473
  49.4 21.7 %collective-permute-start.11 = (f32[4,8,128]{2,1,0:T(8,128)S(1)}, f32[4,8,128]{2,1,0:T(8,128)S(1)}, u32[]{:S(2)}, u32[]{:S(2)}) collective-permute-start(f32[4,8,128]{2,1,0:T(8,128)S(1)} %get-tuple-element.23.refs_7_), channel_id=1, source_target_pairs={{95,0},{64,1},{65,2},{66,3},{67,4},{68,5},{69,6},{70,7},{71,8},{72... | collective-permute-start | bytes 49160 | tf_op jit(solution)/shard_map/ppermute | solution.py:473
  54.3 18.1 %collective-permute-start.12 = (f32[4,8,128]{2,1,0:T(8,128)S(1)}, f32[4,8,128]{2,1,0:T(8,128)S(1)}, u32[]{:S(2)}, u32[]{:S(2)}) collective-permute-start(f32[4,8,128]{2,1,0:T(8,128)S(1)} %get-tuple-element.23.refs_7_), channel_id=1, source_target_pairs={{64,0},{65,1},{66,2},{67,3},{68,4},{69,5},{70,6},{71,7},{72,8},{73... | collective-permute-start | bytes 49160 | tf_op jit(solution)/shard_map/ppermute | solution.py:473
  56.5 17.2 %collective-permute-start.13 = (f32[4,8,128]{2,1,0:T(8,128)S(1)}, f32[4,8,128]{2,1,0:T(8,128)S(1)}, u32[]{:S(2)}, u32[]{:S(2)}) collective-permute-start(f32[4,8,128]{2,1,0:T(8,128)S(1)} %get-tuple-element.23.refs_7_), channel_id=1, source_target_pairs={{65,0},{66,1},{67,2},{68,3},{69,4},{70,5},{71,6},{72,7},{73,8},{74... | collective-permute-start | bytes 49160 | tf_op jit(solution)/shard_map/ppermute | solution.py:473
  62.9 12.1 %collective-permute-start.8 = (f32[4,8,128]{2,1,0:T(8,128)S(1)}, f32[4,8,128]{2,1,0:T(8,128)S(1)}, u32[]{:S(2)}, u32[]{:S(2)}) collective-permute-start(f32[4,8,128]{2,1,0:T(8,128)S(1)} %get-tuple-element.23.refs_7_), channel_id=1, source_target_pairs={{31,64},{0,65},{1,66},{2,67},{3,68},{4,69},{5,70},{6,71},{7,72},{8... | collective-permute-start | bytes 49160 | tf_op jit(solution)/shard_map/ppermute | solution.py:473
  69.8 6.5 %collective-permute-start.9 = (f32[4,8,128]{2,1,0:T(8,128)S(1)}, f32[4,8,128]{2,1,0:T(8,128)S(1)}, u32[]{:S(2)}, u32[]{:S(2)}) collective-permute-start(f32[4,8,128]{2,1,0:T(8,128)S(1)} %get-tuple-element.23.refs_7_), channel_id=1, source_target_pairs={{0,64},{1,65},{2,66},{3,67},{4,68},{5,69},{6,70},{7,71},{8,72},{9,... | collective-permute-start | bytes 49160 | tf_op jit(solution)/shard_map/ppermute | solution.py:473
  71.1 10.0 %collective-permute-start.14 = (f32[2,16,128]{2,1,0:T(8,128)S(1)}, f32[2,16,128]{2,1,0:T(8,128)S(1)}, u32[]{:S(2)}, u32[]{:S(2)}) collective-permute-start(f32[2,16,128]{2,1,0:T(8,128)S(1)} %get-tuple-element.24.refs_22_), channel_id=1, source_target_pairs={{31,64},{0,65},{1,66},{2,67},{3,68},{4,69},{5,70},{6,71},{7,72},{8... | collective-permute-start | bytes 49160 | tf_op jit(solution)/shard_map/ppermute | solution.py:473
  72.4 9.9 %collective-permute-start.15 = (f32[2,16,128]{2,1,0:T(8,128)S(1)}, f32[2,16,128]{2,1,0:T(8,128)S(1)}, u32[]{:S(2)}, u32[]{:S(2)}) collective-permute-start(f32[2,16,128]{2,1,0:T(8,128)S(1)} %get-tuple-element.24.refs_22_), channel_id=1, source_target_pairs={{0,64},{1,65},{2,66},{3,67},{4,68},{5,69},{6,70},{7,71},{8,72},{9,... | collective-permute-start | bytes 49160 | tf_op jit(solution)/shard_map/ppermute | solution.py:473
  73.7 8.7 %collective-permute-start.16 = (f32[2,16,128]{2,1,0:T(8,128)S(1)}, f32[2,16,128]{2,1,0:T(8,128)S(1)}, u32[]{:S(2)}, u32[]{:S(2)}) collective-permute-start(f32[2,16,128]{2,1,0:T(8,128)S(1)} %get-tuple-element.24.refs_22_), channel_id=1, source_target_pairs={{1,64},{2,65},{3,66},{4,67},{5,68},{6,69},{7,70},{8,71},{9,72},{10... | collective-permute-start | bytes 49160 | tf_op jit(solution)/shard_map/ppermute | solution.py:473
  75.0 12.2 %collective-permute-start.17 = (f32[2,16,128]{2,1,0:T(8,128)S(1)}, f32[2,16,128]{2,1,0:T(8,128)S(1)}, u32[]{:S(2)}, u32[]{:S(2)}) collective-permute-start(f32[2,16,128]{2,1,0:T(8,128)S(1)} %get-tuple-element.24.refs_22_), channel_id=1, source_target_pairs={{31,32},{0,33},{1,34},{2,35},{3,36},{4,37},{5,38},{6,39},{7,40},{8... | collective-permute-start | bytes 49160 | tf_op jit(solution)/shard_map/ppermute | solution.py:473
  76.3 14.1 %collective-permute-start.18 = (f32[2,16,128]{2,1,0:T(8,128)S(1)}, f32[2,16,128]{2,1,0:T(8,128)S(1)}, u32[]{:S(2)}, u32[]{:S(2)}) collective-permute-start(f32[2,16,128]{2,1,0:T(8,128)S(1)} %get-tuple-element.24.refs_22_), channel_id=1, source_target_pairs={{0,32},{1,33},{2,34},{3,35},{4,36},{5,37},{6,38},{7,39},{8,40},{9,... | collective-permute-start | bytes 49160 | tf_op jit(solution)/shard_map/ppermute | solution.py:473
  81.1 15.0 %collective-permute-start.19 = (f32[2,16,128]{2,1,0:T(8,128)S(1)}, f32[2,16,128]{2,1,0:T(8,128)S(1)}, u32[]{:S(2)}, u32[]{:S(2)}) collective-permute-start(f32[2,16,128]{2,1,0:T(8,128)S(1)} %get-tuple-element.24.refs_22_), channel_id=1, source_target_pairs={{1,32},{2,33},{3,34},{4,35},{5,36},{6,37},{7,38},{8,39},{9,40},{10... | collective-permute-start | bytes 49160 | tf_op jit(solution)/shard_map/ppermute | solution.py:473
  82.4 24.1 %collective-permute-start.20 = (f32[2,16,128]{2,1,0:T(8,128)S(1)}, f32[2,16,128]{2,1,0:T(8,128)S(1)}, u32[]{:S(2)}, u32[]{:S(2)}) collective-permute-start(f32[2,16,128]{2,1,0:T(8,128)S(1)} %get-tuple-element.24.refs_22_), channel_id=1, source_target_pairs={{31,0},{0,1},{1,2},{2,3},{3,4},{4,5},{5,6},{6,7},{7,8},{8,9},{9,10... | collective-permute-start | bytes 49160 | tf_op jit(solution)/shard_map/ppermute | solution.py:473
  82.5 25.5 %collective-permute-start.21 = (f32[2,16,128]{2,1,0:T(8,128)S(1)}, f32[2,16,128]{2,1,0:T(8,128)S(1)}, u32[]{:S(2)}, u32[]{:S(2)}) collective-permute-start(f32[2,16,128]{2,1,0:T(8,128)S(1)} %get-tuple-element.24.refs_22_), channel_id=1, source_target_pairs={{1,0},{2,1},{3,2},{4,3},{5,4},{6,5},{7,6},{8,7},{9,8},{10,9},{11,1... | collective-permute-start | bytes 49160 | tf_op jit(solution)/shard_map/ppermute | solution.py:473
  87.2 27.3 %collective-permute-start.22 = (f32[2,16,128]{2,1,0:T(8,128)S(1)}, f32[2,16,128]{2,1,0:T(8,128)S(1)}, u32[]{:S(2)}, u32[]{:S(2)}) collective-permute-start(f32[2,16,128]{2,1,0:T(8,128)S(1)} %get-tuple-element.24.refs_22_), channel_id=1, source_target_pairs={{63,0},{32,1},{33,2},{34,3},{35,4},{36,5},{37,6},{38,7},{39,8},{40... | collective-permute-start | bytes 49160 | tf_op jit(solution)/shard_map/ppermute | solution.py:473
  90.5 41.6 %collective-permute-start.23 = (f32[2,16,128]{2,1,0:T(8,128)S(1)}, f32[2,16,128]{2,1,0:T(8,128)S(1)}, u32[]{:S(2)}, u32[]{:S(2)}) collective-permute-start(f32[2,16,128]{2,1,0:T(8,128)S(1)} %get-tuple-element.24.refs_22_), channel_id=1, source_target_pairs={{32,0},{33,1},{34,2},{35,3},{36,4},{37,5},{38,6},{39,7},{40,8},{41... | collective-permute-start | bytes 49160 | tf_op jit(solution)/shard_map/ppermute | solution.py:473
  96.0 36.0 %collective-permute-start.24 = (f32[2,16,128]{2,1,0:T(8,128)S(1)}, f32[2,16,128]{2,1,0:T(8,128)S(1)}, u32[]{:S(2)}, u32[]{:S(2)}) collective-permute-start(f32[2,16,128]{2,1,0:T(8,128)S(1)} %get-tuple-element.24.refs_22_), channel_id=1, source_target_pairs={{33,0},{34,1},{35,2},{36,3},{37,4},{38,5},{39,6},{40,7},{41,8},{42... | collective-permute-start | bytes 49160 | tf_op jit(solution)/shard_map/ppermute | solution.py:473
  106.5 25.6 %collective-permute-start.25 = (f32[2,16,128]{2,1,0:T(8,128)S(1)}, f32[2,16,128]{2,1,0:T(8,128)S(1)}, u32[]{:S(2)}, u32[]{:S(2)}) collective-permute-start(f32[2,16,128]{2,1,0:T(8,128)S(1)} %get-tuple-element.24.refs_22_), channel_id=1, source_target_pairs={{95,0},{64,1},{65,2},{66,3},{67,4},{68,5},{69,6},{70,7},{71,8},{72... | collective-permute-start | bytes 49160 | tf_op jit(solution)/shard_map/ppermute | solution.py:473
  107.9 24.1 %collective-permute-start.26 = (f32[2,16,128]{2,1,0:T(8,128)S(1)}, f32[2,16,128]{2,1,0:T(8,128)S(1)}, u32[]{:S(2)}, u32[]{:S(2)}) collective-permute-start(f32[2,16,128]{2,1,0:T(8,128)S(1)} %get-tuple-element.24.refs_22_), channel_id=1, source_target_pairs={{64,0},{65,1},{66,2},{67,3},{68,4},{69,5},{70,6},{71,7},{72,8},{73... | collective-permute-start | bytes 49160 | tf_op jit(solution)/shard_map/ppermute | solution.py:473
  114.6 17.5 %collective-permute-start.27 = (f32[2,16,128]{2,1,0:T(8,128)S(1)}, f32[2,16,128]{2,1,0:T(8,128)S(1)}, u32[]{:S(2)}, u32[]{:S(2)}) collective-permute-start(f32[2,16,128]{2,1,0:T(8,128)S(1)} %get-tuple-element.24.refs_22_), channel_id=1, source_target_pairs={{65,0},{66,1},{67,2},{68,3},{69,4},{70,5},{71,6},{72,7},{73,8},{74... | collective-permute-start | bytes 49160 | tf_op jit(solution)/shard_map/ppermute | solution.py:473
  (5 other events, 4.9 us)

commit v2 on v1

v2 whole, which is shorter than its diff:
```python
import functools

import jax
import jax.numpy as jnp
from jax import lax
from jax.experimental import pallas as pl
from jax.experimental.pallas import tpu as pltpu
from jax.sharding import PartitionSpec as P

ITERATIONS = 32

TIME_STEP = 0.1
MIX_TRACER = 0.05
MIX_MOMENTUM = 0.05
HEAT_INDEX = 0.2
SALT_INDEX = 0.2
CORIOLIS = 2.0
SURFACE_TERM = 0.0005
TRANSPORT_SCALE = 0.05

ROWS = 16
COLS = 128
GROUP = 8
GROUPS = 8
TILE = (GROUP, COLS)
PADDED = GROUPS * GROUP * ROWS
HALO = 2 * 4 * GROUPS
PACKS = 2 * GROUPS
SIDE = PACKS + 4
BLOCK = 8
STRIP = 2


def chebyshev_weights(total_steps):
    low_bound = SURFACE_TERM / (SURFACE_TERM + 4.0)
    high_bound = 2.0 - low_bound
    spread_ratio = (high_bound - low_bound) / (high_bound + low_bound)
    middle = 0.5 * (high_bound + low_bound)
    weights = [1.0]
    for number in range(1, total_steps):
        if number == 1:
            weights.append(2.0 / (2.0 - spread_ratio * spread_ratio))
        else:
            weights.append(1.0 / (1.0 - spread_ratio * spread_ratio * weights[-1] / 4.0))
    return [weight / middle for weight in weights], [weight - 1.0 for weight in weights]


def lanes():
    return lax.broadcasted_iota(jnp.int32, TILE, 1)


def sublanes():
    return lax.broadcasted_iota(jnp.int32, TILE, 0)


def turn(value, by, axis=1):
    size = value.shape[axis]
    by = by % size
    return value if by == 0 else pltpu.roll(value, by, axis)


def row_of(ref, row):
    return jnp.broadcast_to(ref[pl.ds(row, 1), :], TILE)


def masked(mask, value):
    return jnp.where(mask, value, 0.0)


def evens():
    return lax.axis_index("lat") % 2 == 0, lax.axis_index("lon") % 2 == 0


def load_kernel(levels, t, s, u, v, depth, t_out, s_out, u_out, v_out, swap_0, swap_1, depth_out, sems):
    lat_even, _ = evens()
    fields, kept = (t, s, u, v), (t_out, s_out, u_out, v_out)
    copies = []
    for part in range(GROUPS // 2):
        first = 2 * GROUP * ROWS * part
        size = min(2 * GROUP * ROWS, levels * ROWS - first)
        for field in range(4):
            span = pl.ds(first, size)
            copies.append(
                pltpu.make_async_copy(
                    fields[field].at[span, :], kept[field].at[span, :], sems.at[4 * part + field]
                )
            )
            copies[-1].start()
    outer = jnp.where(lat_even, ROWS - 2, 0)
    for half in range(2):
        x = depth[GROUP * half : GROUP * (half + 1), :].astype(jnp.float32)
        depth_out[GROUP * half : GROUP * (half + 1), :] = x
        swap_0[HALO + half] = x
        swap_1[HALO + half] = x
    for part in range(GROUPS // 2):
        for field in range(4):
            copies[4 * part + field].wait()
            for g in (2 * part, 2 * part + 1):
                for r in range(2):
                    for swap, row in ((swap_0, outer), (swap_1, ROWS - 2 - outer)):
                        swap[(r * 4 + field) * GROUPS + g] = kept[field][
                            pl.ds(GROUP * ROWS * g + row + r, GROUP, stride=ROWS), :
                        ]


def side_kernel(t, s, u, v, depth, side):
    fields = (t, s, u, v)
    slot = lanes() // 4

    def body(g, carry):
        for pair in range(2):
            pack = jnp.zeros(TILE, jnp.float32)
            for f in range(2):
                for r in range(ROWS):
                    x = fields[2 * pair + f][pl.ds(GROUP * ROWS * g + r, GROUP, stride=ROWS), :]
                    pack = jnp.where(slot == 16 * f + r, turn(x, 64 * f + 4 * r + 2), pack)
            side[pair * GROUPS + g] = pack
        return carry

    lax.fori_loop(0, GROUPS, body, 0)
    pack = jnp.zeros(TILE, jnp.float32)
    for r in range(ROWS):
        x = row_of(depth, r)
        for f in range(2):
            pack = jnp.where(slot == 16 * f + r, turn(x, 64 * f + 4 * r + 2), pack)
    side[PACKS] = pack


def halo_depth(lat_even, swap_0, swap_1, j):
    if j < 0:
        tile, row, first, second = HALO + 1, GROUP + j, swap_1, swap_0
    else:
        tile, row, first, second = HALO, j - ROWS, swap_0, swap_1
    x = jnp.where(lat_even, first[tile, row : row + 1, :], second[tile, row : row + 1, :])
    return jnp.broadcast_to(x, TILE)


def halo_row(lat_even, swap_0, swap_1, field, g, j):
    if j < 0:
        at, first, second = j + 2, swap_1, swap_0
    else:
        at, first, second = j - ROWS, swap_0, swap_1
    index = (at * 4 + field) * GROUPS + g
    return jnp.where(lat_even, first[index], second[index])


def corner_kernel(swap_0, swap_1, side_in, side):
    lat_even, _ = evens()
    slot = lanes() // 4
    side[: PACKS + 1] = side_in[...]
    ends = ((-1, 0), (ROWS, 60))
    for half in range(2):
        pack = jnp.zeros(TILE, jnp.float32)
        for place in range(4):
            for field in range(4):
                for j, end in ends:
                    x = halo_row(lat_even, swap_0, swap_1, field, 4 * half + place, j)
                    base = (16 * place + 8 * (field // 2) + 64 * (field % 2) + end) % COLS
                    pack = jnp.where(slot == base // 4, turn(x, base + 2), pack)
        side[PACKS + 1 + half] = pack
    pack = jnp.zeros(TILE, jnp.float32)
    for j, end in ends:
        x = halo_depth(lat_even, swap_0, swap_1, j)
        for f in range(2):
            base = 64 * f + end
            pack = jnp.where(slot == base // 4, turn(x, base + 2), pack)
    side[PACKS + 3] = pack


class Depths:
    def __init__(self, store, depth, swap_0, swap_1, own, side_0, side_1):
        lane = lanes()
        self.lat_even, self.lon_even = evens()
        self.store, self.lane = store, lane
        self.swaps, self.sides = (swap_0, swap_1), (own, side_0, side_1)
        self.row = (lane // 4) & 15
        self.column_2, self.column_low = (lane & 3) == 2, (lane & 3) < 2
        d_own = own[PACKS]
        d_east, d_west = self.beside(PACKS)
        self.corner_depths = self.beside(PACKS + 3)
        q_west = jnp.where(self.column_low, d_west, d_own)
        q_east = jnp.where(self.column_low, d_own, d_east)
        k_east, k_west = self.corner_depths
        self.side_depths = [
            (q, *self.around(q, k)) for q, k in ((q_west, k_west), (q_east, k_east))
        ]
        ring, corner = self.join(q_west, q_east), self.join(k_west, k_east)
        for j in range(-2, ROWS + 2):
            if 0 <= j < ROWS:
                d = row_of(depth, j)
            else:
                d = halo_depth(self.lat_even, swap_0, swap_1, j)
            store[3 * (j + 2)] = d
            if -1 <= j <= ROWS:
                edge = ring if 0 <= j < ROWS else corner
                d_e, d_w = self.sideways(d, edge, 0, min(max(j, 0), ROWS - 1))
                store[3 * (j + 2) + 1] = d_e
                store[3 * (j + 2) + 2] = d_w

    def beside(self, tile):
        _, first, second = self.sides
        a, b = first[tile], second[tile]
        return jnp.where(self.lon_even, a, b), jnp.where(self.lon_even, b, a)

    def around(self, q, corner):
        north = jnp.where(self.row == ROWS - 1, corner, turn(q, -4))
        south = jnp.where(self.row == 0, corner, turn(q, 4))
        return turn(q, -1), turn(q, 1), north, south

    def join(self, q_west, q_east):
        return jnp.where(self.column_2, q_east, turn(q_west, 2))

    def sideways(self, q, edge, f, r):
        edge = turn(edge, 127 - (64 * f + 4 * r + 2))
        east = jnp.where(self.lane == COLS - 1, edge, turn(q, -1))
        west = jnp.where(self.lane == 0, edge, turn(q, 1))
        return east, west

    def of(self, j):
        return self.store[3 * (j + 2)]

    def east(self, j):
        return self.store[3 * (j + 2) + 1]

    def west(self, j):
        return self.store[3 * (j + 2) + 2]


class Edges:
    def __init__(self, dep, g, level, pairs, with_laplacian):
        place = 16 * (g % 4)
        corners = dep.beside(PACKS + 1 + g // 4)
        corner_masks = [level < d for d in dep.corner_depths]
        self.ring, self.corner, self.lap = {}, {}, {}
        for pair in pairs:
            k_east, k_west = [
                masked(m, pltpu.roll(k, COLS - 8 * pair - place, 1))
                for k, m in zip(corners, corner_masks)
            ]
            tile_own = dep.sides[0][pair * GROUPS + g]
            tile_east, tile_west = dep.beside(pair * GROUPS + g)
            sides, laps = [], []
            for q, d_all, corner in (
                (jnp.where(dep.column_low, tile_west, tile_own), dep.side_depths[0], k_west),
                (jnp.where(dep.column_low, tile_own, tile_east), dep.side_depths[1], k_east),
            ):
                here = level < d_all[0]
                q = masked(here, q)
                sides.append(q)
                if pair in with_laplacian:
                    e, w, n, s = dep.around(q, corner)
                    count = sum(jnp.where(level < d, 1.0, 0.0) for d in d_all[1:])
                    laps.append(masked(here, ((e + w) + n) + s - count * q))
            self.ring[pair] = dep.join(*sides)
            self.corner[pair] = dep.join(k_west, k_east)
            if laps:
                self.lap[pair] = dep.join(*laps)

    def edge(self, pair, j):
        return self.ring[pair] if 0 <= j < ROWS else self.corner[pair]


def field_row(dep, g, ref, field, j):
    if 0 <= j < ROWS:
        return ref[pl.ds(GROUP * ROWS * g + j, GROUP, stride=ROWS), :]
    return halo_row(dep.lat_even, *dep.swaps, field, g, j)


def prefix(x, sub):
    for by in (1, 2, 4):
        x = x + jnp.where(sub >= by, turn(x, by, 0), 0.0)
    return x


def momentum_kernel(
    lat_total, t, s, u, v, depth, prior, swap_0, swap_1, own, side_0, side_1,
    u_next, v_next, block, strip_0, strip_1, store, sum_x, sum_y, sum_u, sum_v,
):
    dep = Depths(store, depth, swap_0, swap_1, own, side_0, side_1)
    sub = sublanes()
    zero = jnp.zeros(TILE, jnp.float32)
    for r in range(ROWS):
        for ref in (sum_x, sum_y):
            ref[GROUP * r : GROUP * (r + 1), :] = zero
        for ref in (sum_u, sum_v):
            ref[r] = zero
    first_row = (lax.axis_index("lat") * ROWS).astype(jnp.float32)

    def body(g, carry):
        start = GROUP * ROWS * g
        level = (GROUP * g + sub).astype(jnp.float32)
        edges = Edges(dep, g, level, (0, 1), (1,))
        load = functools.partial(field_row, dep, g)
        edge_load = edges.ring[0]
        edge_load = turn(edge_load, 64) - edge_load
        wet, q, lap, dens = {}, {}, {}, {}
        for j in range(-2, ROWS + 2):
            wet[j] = level < dep.of(j)
            q[j] = [masked(wet[j], load(u, 2, j)), masked(wet[j], load(v, 3, j))]
            if -1 <= j <= ROWS:
                dens[j] = masked(wet[j], load(s, 1, j) - load(t, 0, j))
            i = j - 1
            if i >= -1:
                count = (
                    jnp.where(level < dep.east(i), 1.0, 0.0) + jnp.where(level < dep.west(i), 1.0, 0.0)
                ) + (jnp.where(wet[i + 1], 1.0, 0.0) + jnp.where(wet[i - 1], 1.0, 0.0))
                lap[i] = []
                for f in range(2):
                    e, w = dep.sideways(q[i][f], edges.edge(1, i), f, min(max(i, 0), ROWS - 1))
                    total = (e + w) + (q[i + 1][f] + q[i - 1][f])
                    lap[i].append((masked(wet[i], total - count * q[i][f]), count))
            r = j - 2
            if r >= 0:
                mixes = []
                for f in range(2):
                    here, count = lap[r][f]
                    e, w = dep.sideways(here, edges.lap[1], f, r)
                    mixes.append((e + w) + (lap[r + 1][f][0] + lap[r - 1][f][0]) - count * here)
                e, w = dep.sideways(dens[r], edge_load, 0, r)
                last = GROUP * r + GROUP - 1
                grad_x = prefix(e - w, sub) + row_of(sum_x, last)
                grad_y = prefix(dens[r + 1] - dens[r - 1], sub) + row_of(sum_y, last)
                sum_x[GROUP * r : GROUP * (r + 1), :] = grad_x
                sum_y[GROUP * r : GROUP * (r + 1), :] = grad_y
                turning = TIME_STEP * CORIOLIS * (2.0 * (first_row + (r + 0.5)) / lat_total - 1.0)
                pull = TIME_STEP * 0.5 * SALT_INDEX
                mix = TIME_STEP * MIX_MOMENTUM
                new_u = masked(
                    wet[r], q[r][0] + ((turning * q[r][1] - pull * grad_x) - mix * mixes[0])
                )
                new_v = masked(
                    wet[r], q[r][1] - ((turning * q[r][0] + pull * grad_y) + mix * mixes[1])
                )
                u_next[pl.ds(start + r, GROUP, stride=ROWS), :] = new_u
                v_next[pl.ds(start + r, GROUP, stride=ROWS), :] = new_v
                sum_u[r] += new_u
                sum_v[r] += new_v
        return carry

    lax.fori_loop(0, GROUPS, body, 0)
    for r in range(ROWS):
        half, row = divmod(r, GROUP)
        block[4 + half, row : row + 1, :] = jnp.sum(sum_u[r], axis=0, keepdims=True)
        block[6 + half, row : row + 1, :] = jnp.sum(sum_v[r], axis=0, keepdims=True)
    quarter = lanes() // 32
    for half in range(2):
        rows = slice(GROUP * half, GROUP * (half + 1))
        block[half] = depth[rows, :]
        block[2 + half] = prior[rows, :]
        planes = [block[2 * plane + half] for plane in range(4)]
        strips = []
        for first in (96, 0):
            strip = zero
            for plane, x in enumerate(planes):
                strip = jnp.where(quarter == plane, turn(x, 32 * plane - first), strip)
            strips.append(strip)
        strip_0[half] = jnp.where(dep.lon_even, strips[0], strips[1])
        strip_1[half] = jnp.where(dep.lon_even, strips[1], strips[0])


def tracer_kernel(
    levels, t, s, u, v, depth, swap_0, swap_1, own, side_0, side_1, u_next, v_next,
    t_out, s_out, u_out, v_out, store, t_next, s_next, sems, sems_flow,
):
    flows = [
        pltpu.make_async_copy(src.at[pl.ds(0, levels * ROWS), :], dst, sems_flow.at[i])
        for i, (src, dst) in enumerate(((u_next, u_out), (v_next, v_out)))
    ]
    for copy in flows:
        copy.start()
    dep = Depths(store, depth, swap_0, swap_1, own, side_0, side_1)
    sub = sublanes()

    def body(g, carry):
        start = GROUP * ROWS * g
        level = (GROUP * g + sub).astype(jnp.float32)
        edges = Edges(dep, g, level, (0, 1), (0,))
        load = functools.partial(field_row, dep, g)
        wet, q, sides, lap, flow = {}, {}, {}, {}, {}
        for j in range(-2, ROWS + 2):
            wet[j] = level < dep.of(j)
            q[j] = [masked(wet[j], load(t, 0, j)), masked(wet[j], load(s, 1, j))]
            if -1 <= j <= ROWS:
                flow[j] = [masked(wet[j], load(u, 2, j)), masked(wet[j], load(v, 3, j))]
            i = j - 1
            if i >= -1:
                count = (
                    jnp.where(level < dep.east(i), 1.0, 0.0) + jnp.where(level < dep.west(i), 1.0, 0.0)
                ) + (jnp.where(wet[i + 1], 1.0, 0.0) + jnp.where(wet[i - 1], 1.0, 0.0))
                lap[i], sides[i] = [], []
                for f in range(2):
                    e, w = dep.sideways(q[i][f], edges.edge(0, i), f, min(max(i, 0), ROWS - 1))
                    sides[i].append((e, w))
                    total = (e + w) + (q[i + 1][f] + q[i - 1][f])
                    lap[i].append((masked(wet[i], total - count * q[i][f]), count))
            r = j - 2
            if r >= 0:
                e, w = dep.sideways(flow[r][0], edges.ring[1], 0, r)
                u_e = masked(level < dep.east(r), flow[r][0] + e)
                u_w = masked(level < dep.west(r), flow[r][0] + w)
                v_n = masked(wet[r + 1], flow[r][1] + flow[r + 1][1])
                v_s = masked(wet[r - 1], flow[r][1] + flow[r - 1][1])
                for f, out in ((0, t_next), (1, s_next)):
                    here, count = lap[r][f]
                    e, w = dep.sideways(here, edges.lap[0], f, r)
                    mix = (e + w) + (lap[r + 1][f][0] + lap[r - 1][f][0]) - count * here
                    mid = q[r][f]
                    e, w = sides[r][f]
                    advected = (u_e * (mid + e) - u_w * (mid + w)) + (
                        v_n * (mid + q[r + 1][f]) - v_s * (mid + q[r - 1][f])
                    )
                    out[pl.ds(start + r, GROUP, stride=ROWS), :] = masked(
                        wet[r],
                        mid - (0.25 * TIME_STEP * advected + TIME_STEP * MIX_TRACER * mix),
                    )
        return carry

    copies = []
    for part in range(GROUPS // 2):
        lax.fori_loop(2 * part, 2 * part + 2, body, 0)
        first = 2 * GROUP * ROWS * part
        span = pl.ds(first, min(2 * GROUP * ROWS, levels * ROWS - first))
        for i, (src, dst) in enumerate(((t_next, t_out), (s_next, s_out))):
            copies.append(
                pltpu.make_async_copy(src.at[span, :], dst.at[span, :], sems.at[2 * part + i])
            )
            copies[-1].start()
    for copy in flows + copies:
        copy.wait()


STEPS = 5 * ROWS // GROUP


class Plane:
    def __init__(self, own, rim):
        self.own, self.rim = own, rim

    def map(self, other, fn):
        if isinstance(other, Plane):
            return Plane(
                [fn(a, b) for a, b in zip(self.own, other.own)],
                [fn(a, b) for a, b in zip(self.rim, other.rim)],
            )
        return Plane([fn(a, other) for a in self.own], [fn(a, other) for a in self.rim])

    def __add__(self, other):
        return self.map(other, lambda a, b: a + b)

    def __sub__(self, other):
        return self.map(other, lambda a, b: a - b)

    def __mul__(self, other):
        return self.map(other, lambda a, b: a * b)

    def low(self, other):
        return self.map(other, jnp.minimum)

    def side(self, by, lane):
        at = lanes() == lane
        pairs = [(turn(a, by), turn(b, by)) for a, b in zip(self.own, self.rim)]
        return Plane([jnp.where(at, b, a) for a, b in pairs], [jnp.where(at, a, b) for a, b in pairs])

    def east(self):
        return self.side(-1, COLS - 1)

    def west(self):
        return self.side(1, 0)

    def north(self):
        return Plane(*[x[1:] + [turn(x[0], -1, 0)] for x in (self.own, self.rim)])

    def south(self):
        return Plane(*[[turn(x[-1], 1, 0)] + x[:-1] for x in (self.own, self.rim)])


def solve_kernel(levels, own, core, chip_0, chip_1, out, own_buf, rim_buf):
    lat_even, lon_even = evens()
    chip_even = lax.axis_index("lat") // 2 % 2 == 0
    lane = lanes()

    def tile(b, index):
        if b == 0:
            return own[index]
        message = BLOCK + 2 * STRIP
        to_first = chip_even if b > 0 else jnp.logical_not(chip_even)
        if abs(b) == 2:
            return jnp.where(to_first, chip_0[index], chip_1[index])
        far = jnp.where(to_first, chip_0[message + index], chip_1[message + index])
        return jnp.where(lat_even if b > 0 else jnp.logical_not(lat_even), core[index], far)

    def gather(plane):
        for b in range(-2, 3):
            for half in range(2):
                at = ROWS * (b + 2) + GROUP * half
                own_buf[at : at + GROUP, :] = tile(b, 2 * plane + half)
                first, second = tile(b, BLOCK + half), tile(b, BLOCK + STRIP + half)
                east = turn(jnp.where(lon_even, first, second), -32 * plane)
                west = turn(jnp.where(lon_even, second, first), 96 - 32 * plane)
                rim_buf[at : at + GROUP, :] = jnp.where(
                    lane < 32, east, jnp.where(lane >= 96, west, 0.0)
                )
        return Plane(
            *[[buf[pl.ds(t, GROUP, stride=STEPS), :] for t in range(STEPS)] for buf in (own_buf, rim_buf)]
        )

    depth, prior, zonal, northward = [gather(plane) for plane in range(4)]

    ocean = depth.map(0.0, lambda a, b: jnp.where(a > b, 1.0, 0.0))
    depth_east, depth_north = depth.low(depth.east()), depth.low(depth.north())
    zonal_flow = zonal.map(depth_east, lambda a, b: masked(b > 0.0, a))
    north_flow = northward.map(depth_north, lambda a, b: masked(b > 0.0, a))
    divergence = (zonal_flow - zonal_flow.west()) + (north_flow - north_flow.south())
    right_side = prior * SURFACE_TERM - divergence * TRANSPORT_SCALE
    east_face, north_face = depth_east * (1.0 / levels), depth_north * (1.0 / levels)
    west_face, south_face = east_face.west(), north_face.south()
    diagonal = (((east_face + west_face) + north_face) + south_face) + SURFACE_TERM
    inverse = diagonal.map(1.0, lambda a, b: b / a)
    right_side, east_face, west_face, north_face, south_face = [
        x * inverse for x in (right_side, east_face, west_face, north_face, south_face)
    ]
    height, change = prior, None
    scales, carries = chebyshev_weights(ITERATIONS)
    for scale, carry in zip(scales, carries):
        spread = (east_face * height.east() + west_face * height.west()) + (
            north_face * height.north() + south_face * height.south()
        )
        residual = (right_side - height) + spread
        step = residual * scale
        change = step if change is None else step + change * carry
        height = height + change
    height = height * ocean
    for t in range(STEPS):
        own_buf[pl.ds(t, GROUP, stride=STEPS), :] = height.own[t]
    out[...] = own_buf[2 * ROWS : 3 * ROWS, :]


def swap(value, axis, partner):
    count = lax.axis_size(axis)
    pairs = [(i, partner(i) % count) for i in range(count) if axis == "lon" or 0 <= partner(i) < count]
    return lax.ppermute(value, axis, pairs)


def even_first(i):
    return i + 1 if i % 2 == 0 else i - 1


def odd_first(i):
    return i - 1 if i % 2 == 0 else i + 1


def chip_even_first(i):
    return i + 2 if i // 2 % 2 == 0 else i - 2


def chip_odd_first(i):
    return i - 2 if i // 2 % 2 == 0 else i + 2


def shape(*dims):
    return jax.ShapeDtypeStruct(dims, jnp.float32)


VMEM = pl.BlockSpec(memory_space=pltpu.VMEM)
HBM = pl.BlockSpec(memory_space=pltpu.HBM)


def call(kernel, outs, scratch, *args, ins=None, out_specs=None, cost=0):
    return pl.pallas_call(
        kernel,
        out_shape=outs,
        in_specs=ins or [VMEM] * len(args),
        out_specs=out_specs or jax.tree.map(lambda _: VMEM, outs),
        scratch_shapes=scratch,
        compiler_params=pltpu.CompilerParams(vmem_limit_bytes=32 * 2**20),
        cost_estimate=pl.CostEstimate(flops=cost, bytes_accessed=4 * 2**20, transcendentals=0),
    )(*args)


def per_device(
    heat_anomaly,
    saltiness_anomaly,
    zonal_current_array,
    meridional_current_array,
    sea_height_prior,
    ocean_layer_number,
):
    levels, rows, cols = heat_anomaly.shape
    lat_total = rows * lax.axis_size("lat")
    fields = [
        x.reshape(levels * rows, cols)
        for x in (heat_anomaly, saltiness_anomaly, zonal_current_array, meridional_current_array)
    ]
    padded, tiles = shape(PADDED, cols), lambda n: shape(n, *TILE)
    *kept, to_0, to_1, depth = call(
        functools.partial(load_kernel, levels),
        (padded,) * 4 + (tiles(HALO + 2), tiles(HALO + 2), shape(rows, cols)),
        [pltpu.SemaphoreType.DMA((2 * GROUPS,))],
        *[pltpu.with_memory_space_constraint(x, pltpu.HBM) for x in fields],
        ocean_layer_number,
        ins=[HBM] * 4 + [VMEM],
        cost=10**6,
    )
    swap_0, swap_1 = swap(to_0, "lat", even_first), swap(to_1, "lat", odd_first)
    side = call(side_kernel, tiles(PACKS + 1), [], *kept, depth, cost=10**7)
    side = call(corner_kernel, tiles(SIDE), [], swap_0, swap_1, side, cost=10**6)
    side_0, side_1 = swap(side, "lon", even_first), swap(side, "lon", odd_first)

    around = (swap_0, swap_1, side, side_0, side_1)
    store = pltpu.VMEM((3 * (ROWS + 4), *TILE), jnp.float32)
    u_next, v_next, block, strip_0, strip_1 = call(
        functools.partial(momentum_kernel, lat_total),
        (padded, padded, tiles(BLOCK), tiles(STRIP), tiles(STRIP)),
        [store]
        + [pltpu.VMEM((GROUP * ROWS, COLS), jnp.float32)] * 2
        + [pltpu.VMEM((ROWS, *TILE), jnp.float32)] * 2,
        *kept,
        depth,
        sea_height_prior,
        *around,
        cost=10**7,
    )
    strips = [swap(strip_0, "lon", even_first), swap(strip_1, "lon", odd_first)]
    own = jnp.concatenate([block, *strips])
    core = swap(own, "lat", even_first)
    chip = jnp.concatenate([own, core])
    chip_0, chip_1 = swap(chip, "lat", chip_even_first), swap(chip, "lat", chip_odd_first)
    out = shape(levels * rows, cols)
    results = call(
        functools.partial(tracer_kernel, levels),
        (out,) * 4,
        [
            store,
            pltpu.VMEM((PADDED, COLS), jnp.float32),
            pltpu.VMEM((PADDED, COLS), jnp.float32),
            pltpu.SemaphoreType.DMA((GROUPS,)),
            pltpu.SemaphoreType.DMA((2,)),
        ],
        *kept,
        depth,
        *around,
        u_next,
        v_next,
        out_specs=(HBM,) * 4,
        cost=10**7,
    )
    height = call(
        functools.partial(solve_kernel, levels),
        shape(rows, cols),
        [pltpu.VMEM((5 * ROWS, COLS), jnp.float32)] * 2,
        own,
        core,
        chip_0,
        chip_1,
        cost=10**7,
    )
    return *[x.reshape(levels, rows, cols) for x in results], height


def solution(mesh):
    cells, plane = P(None, "lat", "lon"), P("lat", "lon")
    return jax.shard_map(
        per_device,
        mesh=mesh,
        in_specs=(cells,) * 4 + (plane,) * 2,
        out_specs=(cells,) * 4 + (plane,),
        check_vma=False,
    )
```

time: 137 us -> 49.5 us (0.36)
  the two profiles are of different devices: /device:TPU:7 before, /device:TPU:2 now
where the time goes in v2:
time: 49.5 us; the launch traced here: 49.3 us
  starting transfers between devices  22.3 us (45%)
  Pallas kernels  16.7 us (34%)
  waiting for transfers between devices  8.81 us (18%)
  between operations  0.75 us (2%)
  local copies, waits for them, and re-layouts  0.71 us (1%)
    ppermute x9, starting transfers between devices, swap(): return lax.ppermute(value, axis, pairs)  22.3 us
    pallas_call x6, Pallas kernels, call(): pl.pallas_call(kernel, out_shape=outs, in_specs=ins or [VMEM] * len(args)...  16.7 us
    ppermute x9, waiting for transfers between devices, swap(): return lax.ppermute(value, axis, pairs)  8.81 us
  transfers between devices with their start and end apart: 9, of which 4 were waited for; matrix products, arithmetic and copies ran while one was open for 0% of the time, Pallas kernels for 13%

profile of v2, /device:TPU:2, one launch (start us, length us, event | category | flops | bytes accessed | tf_op | source)
XLA Modules:
  0.0 49.3 jit_solution(16328524048892010310)
XLA Ops:
  0.6 0.0 copy-start
  0.6 0.7 %copy-done = s32[16,128]{1,0:T(8,128)S(1)} copy-done((s32[16,128]{1,0:T(8,128)S(1)}, s32[16,128]{1,0:T(8,128)}, u32[]{:S(2)}) %copy-start) | copy-done | bytes 8216
  1.3 1.7 %shard_map.101 = (f32[1024,128]{1,0:T(8,128)S(1)}, f32[1024,128]{1,0:T(8,128)S(1)}, f32[1024,128]{1,0:T(8,128)S(1)}, f32[1024,128]{1,0:T(8,128)S(1)}, f32[66,8,1...) custom-call(f32[992,128]{1,0:T(8,128)} %bitcast.8, f32[992,128]{1,0:T(8,128)} %bitcast.9, ...), custom_call_target="tpu_custom_call" | custom-call | flops 1000000 | bytes 4194304 | tf_op jit(solution)/shard_map/pallas_call | solution.py:569
  3.1 0.1 collective-permute-start
  3.2 4.3 %collective-permute-start.1 = (f32[66,8,128]{2,1,0:T(8,128)S(1)}, f32[66,8,128]{2,1,0:T(8,128)S(1)}, u32[]{:S(2)}, u32[]{:S(2)}) collective-permute-start(f32[66,8,128]{2,1,0:T(8,128)S(1)} %get-tuple-element.27), channel_id=1, source_target_pairs={{32,64},{64,32},{96,128},{128,96},{160,192},{192,160},{33,65},{65,... | collective-permute-start | bytes 811016 | tf_op jit(solution)/shard_map/ppermute | solution.py:541
  7.4 1.2 %shard_map.102.side_in = f32[17,8,128]{2,1,0:T(8,128)S(1)} custom-call(f32[1024,128]{1,0:T(8,128)S(1)} %get-tuple-element.21.t, f32[1024,128]{1,0:T(8,128)S(1)} %get-tuple-element.22.s, f32[1024,128]{1,0:T(8,128)S(1)} %get-tuple-element.23.u, f32[1024,128]{1,0:T(8,128)S(1)} %get-tuple-element.24.v, f32[16,128]{1,0:T(8,128)S(1)} %get-tuple-element.25.depth), custom_call_target="tpu_custom_call" | custom-call | flops 10000000 | bytes 4194304 | tf_op jit(solution)/shard_map/pallas_call | solution.py:569
  8.7 0.0 copy-start.1
  8.7 0.0 collective-permute-done.swap_0
  8.7 2.9 %collective-permute-done.1.swap_1 = f32[66,8,128]{2,1,0:T(8,128)S(1)} collective-permute-done((f32[66,8,128]{2,1,0:T(8,128)S(1)}, f32[66,8,128]{2,1,0:T(8,128)S(1)}, u32[]{:S(2)}, u32[]{:S(2)}) %collective-permute-start.1) | collective-permute-done | bytes 270368 | tf_op jit(solution)/shard_map/ppermute | solution.py:541
  11.6 0.1 shard_map.103.own
  11.7 1.0 %collective-permute-start.2 = (f32[20,8,128]{2,1,0:T(8,128)S(1)}, f32[20,8,128]{2,1,0:T(8,128)S(1)}, u32[]{:S(2)}, u32[]{:S(2)}) collective-permute-start(f32[20,8,128]{2,1,0:T(8,128)S(1)} %shard_map.103.own), channel_id=1, source_target_pairs={{0,1},{1,0},{2,3},{3,2},{4,5},{5,4},{6,7},{7,6},{8,9},{9,8},{10,11... | collective-permute-start | bytes 245768 | tf_op jit(solution)/shard_map/ppermute | solution.py:541
  12.8 7.5 %collective-permute-start.3 = (f32[20,8,128]{2,1,0:T(8,128)S(1)}, f32[20,8,128]{2,1,0:T(8,128)S(1)}, u32[]{:S(2)}, u32[]{:S(2)}) collective-permute-start(f32[20,8,128]{2,1,0:T(8,128)S(1)} %shard_map.103.own), channel_id=1, source_target_pairs={{0,31},{1,2},{2,1},{3,4},{4,3},{5,6},{6,5},{7,8},{8,7},{9,10},{10,... | collective-permute-start | bytes 245768 | tf_op jit(solution)/shard_map/ppermute | solution.py:541
  20.2 0.0 collective-permute-done.2.side_0
  20.2 2.8 %collective-permute-done.3.side_1 = f32[20,8,128]{2,1,0:T(8,128)S(1)} collective-permute-done((f32[20,8,128]{2,1,0:T(8,128)S(1)}, f32[20,8,128]{2,1,0:T(8,128)S(1)}, u32[]{:S(2)}, u32[]{:S(2)}) %collective-permute-start.3) | collective-permute-done | bytes 81952 | tf_op jit(solution)/shard_map/ppermute | solution.py:541
  23.0 0.0 copy-done.1
  23.0 4.4 %shard_map.104 = (f32[1024,128]{1,0:T(8,128)S(1)}, f32[1024,128]{1,0:T(8,128)S(1)}, f32[8,8,128]{2,1,0:T(8,128)S(1)}, f32[2,8,128]{2,1,0:T(8,128)S(1)}, f32[2,8,128]{2,1,0:T(8,128)S(1)}) custom-call(f32[1024,128]{1,0:T(8,128)S(1)} %get-tuple-element.21.t, f32[1024,128]{1,0:T(8,128)S(1)} %get-tuple-element.22.s, f32[1024,128]{1,0:T(8,128)S(1)} %get-tuple-element.23.u, ...), custom_call_target="tpu_custom_call" | custom-call | flops 10000000 | bytes 4194304 | tf_op jit(solution)/shard_map/pallas_call | solution.py:569
  27.4 0.1 collective-permute-start.4
  27.5 5.1 %collective-permute-start.5 = (f32[2,8,128]{2,1,0:T(8,128)S(1)}, f32[2,8,128]{2,1,0:T(8,128)S(1)}, u32[]{:S(2)}, u32[]{:S(2)}) collective-permute-start(f32[2,8,128]{2,1,0:T(8,128)S(1)} %get-tuple-element.36), channel_id=1, source_target_pairs={{0,31},{1,2},{2,1},{3,4},{4,3},{5,6},{6,5},{7,8},{8,7},{9,10},{10,... | collective-permute-start | bytes 24584 | tf_op jit(solution)/shard_map/ppermute | solution.py:541
  32.7 0.0 collective-permute-done.4
  32.7 1.9 %collective-permute-done.5 = f32[2,8,128]{2,1,0:T(8,128)S(1)} collective-permute-done((f32[2,8,128]{2,1,0:T(8,128)S(1)}, f32[2,8,128]{2,1,0:T(8,128)S(1)}, u32[]{:S(2)}, u32[]{:S(2)}) %collective-permute-start.5) | collective-permute-done | bytes 8224 | tf_op jit(solution)/shard_map/ppermute | solution.py:541
  34.6 0.0 collective-permute-start.6
  34.6 1.2 %collective-permute-done.6.core = f32[12,8,128]{2,1,0:T(8,128)S(1)} collective-permute-done((f32[12,8,128]{2,1,0:T(8,128)S(1)}, f32[12,8,128]{2,1,0:T(8,128)S(1)}, u32[]{:S(2)}, u32[]{:S(2)}) %collective-permute-start.6) | collective-permute-done | bytes 49184 | tf_op jit(solution)/shard_map/ppermute | solution.py:541
  35.8 0.0 collective-permute-start.7
  35.8 4.2 %collective-permute-start.8 = (f32[24,8,128]{2,1,0:T(8,128)S(1)}, f32[24,8,128]{2,1,0:T(8,128)S(1)}, u32[]{:S(2)}, u32[]{:S(2)}) collective-permute-start(f32[24,8,128]{2,1,0:T(8,128)S(1)} %constant_dynamic-update-slice_fusion.3), channel_id=1, source_target_pairs={{64,128},{96,160},{128,64},{160,96},{65,129},{97,161},{129,65},{16... | collective-permute-start | bytes 294920 | tf_op jit(solution)/shard_map/ppermute | solution.py:541
  40.0 5.1 %shard_map.105 = (f32[992,128]{1,0:T(8,128)}, f32[992,128]{1,0:T(8,128)}, f32[992,128]{1,0:T(8,128)}, f32[992,128]{1,0:T(8,128)}) custom-call(f32[1024,128]{1,0:T(8,128)S(1)} %get-tuple-element.21.t, f32[1024,128]{1,0:T(8,128)S(1)} %get-tuple-element.22.s, f32[1024,128]{1,0:T(8,128)S(1)} %get-tuple-element.23.u, f32[1024,128]{1,0:T(8,128)S(1)} %get-tuple-element.24.v, ...), custom_call_target="tpu_custom_call" | custom-call | flops 10000000 | bytes 4194304 | tf_op jit(solution)/shard_map/pallas_call | solution.py:569
  45.1 0.0 collective-permute-done.7.chip_0
  45.1 0.0 collective-permute-done.8.chip_1
  45.1 4.2 %shard_map.106 = f32[16,128]{1,0:T(8,128)} custom-call(f32[12,8,128]{2,1,0:T(8,128)S(1)} %get-tuple-element.40.own, f32[12,8,128]{2,1,0:T(8,128)S(1)} %collective-permute-done.6.core, f32[24,8,128]{2,1,0:T(8,128)S(1)} %collective-permute-done.7.chip_0, f32[24,8,128]{2,1,0:T(8,128)S(1)} %collective-permute-done.8.chip_1), custom_call_target="tpu_custom_call" | custom-call | flops 10000000 | bytes 4194304 | tf_op jit(solution)/shard_map/pallas_call | solution.py:569
  (4 shorter events, 0.0 us)
Async XLA Ops:
  0.6 0.7 %copy-start = (s32[16,128]{1,0:T(8,128)S(1)}, s32[16,128]{1,0:T(8,128)}, u32[]{:S(2)}) copy-start(s32[16,128]{1,0:T(8,128)} %depth.1) | copy-start | bytes 24580
  3.1 5.6 %collective-permute-start = (f32[66,8,128]{2,1,0:T(8,128)S(1)}, f32[66,8,128]{2,1,0:T(8,128)S(1)}, u32[]{:S(2)}, u32[]{:S(2)}) collective-permute-start(f32[66,8,128]{2,1,0:T(8,128)S(1)} %get-tuple-element.26), channel_id=1, source_target_pairs={{0,32},{32,0},{64,96},{96,64},{128,160},{160,128},{192,224},{224,1... | collective-permute-start | bytes 811016 | tf_op jit(solution)/shard_map/ppermute | solution.py:541
  3.2 8.4 %collective-permute-start.1 = (f32[66,8,128]{2,1,0:T(8,128)S(1)}, f32[66,8,128]{2,1,0:T(8,128)S(1)}, u32[]{:S(2)}, u32[]{:S(2)}) collective-permute-start(f32[66,8,128]{2,1,0:T(8,128)S(1)} %get-tuple-element.27), channel_id=1, source_target_pairs={{32,64},{64,32},{96,128},{128,96},{160,192},{192,160},{33,65},{65,... | collective-permute-start | bytes 811016 | tf_op jit(solution)/shard_map/ppermute | solution.py:541
  8.7 14.4 %copy-start.1 = (f32[16,128]{1,0:T(8,128)S(1)}, f32[16,128]{1,0:T(8,128)}, u32[]{:S(2)}) copy-start(f32[16,128]{1,0:T(8,128)} %prior.1) | copy-start | bytes 24580
  11.7 8.5 %collective-permute-start.2 = (f32[20,8,128]{2,1,0:T(8,128)S(1)}, f32[20,8,128]{2,1,0:T(8,128)S(1)}, u32[]{:S(2)}, u32[]{:S(2)}) collective-permute-start(f32[20,8,128]{2,1,0:T(8,128)S(1)} %shard_map.103.own), channel_id=1, source_target_pairs={{0,1},{1,0},{2,3},{3,2},{4,5},{5,4},{6,7},{7,6},{8,9},{9,8},{10,11... | collective-permute-start | bytes 245768 | tf_op jit(solution)/shard_map/ppermute | solution.py:541
  12.8 10.3 %collective-permute-start.3 = (f32[20,8,128]{2,1,0:T(8,128)S(1)}, f32[20,8,128]{2,1,0:T(8,128)S(1)}, u32[]{:S(2)}, u32[]{:S(2)}) collective-permute-start(f32[20,8,128]{2,1,0:T(8,128)S(1)} %shard_map.103.own), channel_id=1, source_target_pairs={{0,31},{1,2},{2,1},{3,4},{4,3},{5,6},{6,5},{7,8},{8,7},{9,10},{10,... | collective-permute-start | bytes 245768 | tf_op jit(solution)/shard_map/ppermute | solution.py:541
  27.4 5.2 %collective-permute-start.4 = (f32[2,8,128]{2,1,0:T(8,128)S(1)}, f32[2,8,128]{2,1,0:T(8,128)S(1)}, u32[]{:S(2)}, u32[]{:S(2)}) collective-permute-start(f32[2,8,128]{2,1,0:T(8,128)S(1)} %get-tuple-element.35), channel_id=1, source_target_pairs={{0,1},{1,0},{2,3},{3,2},{4,5},{5,4},{6,7},{7,6},{8,9},{9,8},{10,11... | collective-permute-start | bytes 24584 | tf_op jit(solution)/shard_map/ppermute | solution.py:541
  27.5 7.1 %collective-permute-start.5 = (f32[2,8,128]{2,1,0:T(8,128)S(1)}, f32[2,8,128]{2,1,0:T(8,128)S(1)}, u32[]{:S(2)}, u32[]{:S(2)}) collective-permute-start(f32[2,8,128]{2,1,0:T(8,128)S(1)} %get-tuple-element.36), channel_id=1, source_target_pairs={{0,31},{1,2},{2,1},{3,4},{4,3},{5,6},{6,5},{7,8},{8,7},{9,10},{10,... | collective-permute-start | bytes 24584 | tf_op jit(solution)/shard_map/ppermute | solution.py:541
  34.6 1.2 %collective-permute-start.6 = (f32[12,8,128]{2,1,0:T(8,128)S(1)}, f32[12,8,128]{2,1,0:T(8,128)S(1)}, u32[]{:S(2)}, u32[]{:S(2)}) collective-permute-start(f32[12,8,128]{2,1,0:T(8,128)S(1)} %get-tuple-element.40.own), channel_id=1, source_target_pairs={{0,32},{32,0},{64,96},{96,64},{128,160},{160,128},{192,224},{224,1... | collective-permute-start | bytes 147464 | tf_op jit(solution)/shard_map/ppermute | solution.py:541
  35.8 9.3 %collective-permute-start.7 = (f32[24,8,128]{2,1,0:T(8,128)S(1)}, f32[24,8,128]{2,1,0:T(8,128)S(1)}, u32[]{:S(2)}, u32[]{:S(2)}) collective-permute-start(f32[24,8,128]{2,1,0:T(8,128)S(1)} %constant_dynamic-update-slice_fusion.3), channel_id=1, source_target_pairs={{0,64},{32,96},{64,0},{96,32},{128,192},{160,224},{192,128},{224,1... | collective-permute-start | bytes 294920 | tf_op jit(solution)/shard_map/ppermute | solution.py:541
  35.8 9.3 %collective-permute-start.8 = (f32[24,8,128]{2,1,0:T(8,128)S(1)}, f32[24,8,128]{2,1,0:T(8,128)S(1)}, u32[]{:S(2)}, u32[]{:S(2)}) collective-permute-start(f32[24,8,128]{2,1,0:T(8,128)S(1)} %constant_dynamic-update-slice_fusion.3), channel_id=1, source_target_pairs={{64,128},{96,160},{128,64},{160,96},{65,129},{97,161},{129,65},{16... | collective-permute-start | bytes 294920 | tf_op jit(solution)/shard_map/ppermute | solution.py:541

commit v3 on v2

--- a/solution.py
+++ b/solution.py
@@ -24,6 +24,8 @@
 GROUPS = 8
 TILE = (GROUP, COLS)
 PADDED = GROUPS * GROUP * ROWS
+PARTS = 4
+PART = PADDED // PARTS
 HALO = 2 * 4 * GROUPS
 PACKS = 2 * GROUPS
 SIDE = PACKS + 4
@@ -71,10 +73,19 @@
     return lax.axis_index("lat") % 2 == 0, lax.axis_index("lon") % 2 == 0
 
 
-def load_kernel(levels, t, s, u, v, depth, t_out, s_out, u_out, v_out, swap_0, swap_1, depth_out, sems):
+def load_kernel(
+    levels, t, s, u, v, depth_in, prior_in, t_out, s_out, u_out, v_out, swap_0, swap_1, depth_out, prior,
+    depth, sems, sems_plane,
+):
     lat_even, _ = evens()
     fields, kept = (t, s, u, v), (t_out, s_out, u_out, v_out)
     copies = []
+    planes = [
+        pltpu.make_async_copy(src, dst, sems_plane.at[i])
+        for i, (src, dst) in enumerate(((depth_in, depth), (prior_in, prior)))
+    ]
+    for copy in planes:
+        copy.start()
     for part in range(GROUPS // 2):
         first = 2 * GROUP * ROWS * part
         size = min(2 * GROUP * ROWS, levels * ROWS - first)
@@ -87,6 +98,8 @@
             )
             copies[-1].start()
     outer = jnp.where(lat_even, ROWS - 2, 0)
+    for copy in planes:
+        copy.wait()
     for half in range(2):
         x = depth[GROUP * half : GROUP * (half + 1), :].astype(jnp.float32)
         depth_out[GROUP * half : GROUP * (half + 1), :] = x
@@ -168,7 +181,7 @@
 
 
 class Depths:
-    def __init__(self, store, depth, swap_0, swap_1, own, side_0, side_1):
+    def __init__(self, store, depth, swap_0, swap_1, own, side_0, side_1, build=True):
         lane = lanes()
         self.lat_even, self.lon_even = evens()
         self.store, self.lane = store, lane
@@ -184,6 +197,8 @@
         self.side_depths = [
             (q, *self.around(q, k)) for q, k in ((q_west, k_west), (q_east, k_east))
         ]
+        if not build:
+            return
         ring, corner = self.join(q_west, q_east), self.join(k_west, k_east)
         for j in range(-2, ROWS + 2):
             if 0 <= j < ROWS:
@@ -359,16 +374,9 @@
 
 
 def tracer_kernel(
-    levels, t, s, u, v, depth, swap_0, swap_1, own, side_0, side_1, u_next, v_next,
-    t_out, s_out, u_out, v_out, store, t_next, s_next, sems, sems_flow,
+    part, t, s, u, v, depth, swap_0, swap_1, own, side_0, side_1, store, t_next, s_next
 ):
-    flows = [
-        pltpu.make_async_copy(src.at[pl.ds(0, levels * ROWS), :], dst, sems_flow.at[i])
-        for i, (src, dst) in enumerate(((u_next, u_out), (v_next, v_out)))
-    ]
-    for copy in flows:
-        copy.start()
-    dep = Depths(store, depth, swap_0, swap_1, own, side_0, side_1)
+    dep = Depths(store, depth, swap_0, swap_1, own, side_0, side_1, build=False)
     sub = sublanes()
 
     def body(g, carry):
@@ -409,24 +417,13 @@
                     advected = (u_e * (mid + e) - u_w * (mid + w)) + (
                         v_n * (mid + q[r + 1][f]) - v_s * (mid + q[r - 1][f])
                     )
-                    out[pl.ds(start + r, GROUP, stride=ROWS), :] = masked(
+                    out[pl.ds(start - PART * part + r, GROUP, stride=ROWS), :] = masked(
                         wet[r],
                         mid - (0.25 * TIME_STEP * advected + TIME_STEP * MIX_TRACER * mix),
                     )
         return carry
 
-    copies = []
-    for part in range(GROUPS // 2):
-        lax.fori_loop(2 * part, 2 * part + 2, body, 0)
-        first = 2 * GROUP * ROWS * part
-        span = pl.ds(first, min(2 * GROUP * ROWS, levels * ROWS - first))
-        for i, (src, dst) in enumerate(((t_next, t_out), (s_next, s_out))):
-            copies.append(
-                pltpu.make_async_copy(src.at[span, :], dst.at[span, :], sems.at[2 * part + i])
-            )
-            copies[-1].start()
-    for copy in flows + copies:
-        copy.wait()
+    lax.fori_loop(2 * part, 2 * part + 2, body, 0)
 
 
 STEPS = 5 * ROWS // GROUP
@@ -474,7 +471,25 @@
         return Plane(*[[turn(x[-1], 1, 0)] + x[:-1] for x in (self.own, self.rim)])
 
 
-def solve_kernel(levels, own, core, chip_0, chip_1, out, own_buf, rim_buf):
+def solve_kernel(levels, own, core, chip_0, chip_1, u_next, v_next, *refs):
+    pieces, (t_out, s_out, u_out, v_out, out, own_buf, rim_buf, sems, sems_flow) = refs[:-9], refs[-9:]
+    copies = []
+    for part in range(PARTS):
+        size = min(PART, levels * ROWS - PART * part)
+        for i, dst in enumerate((t_out, s_out)):
+            copies.append(
+                pltpu.make_async_copy(
+                    pieces[2 * part + i].at[pl.ds(0, size), :],
+                    dst.at[pl.ds(PART * part, size), :],
+                    sems.at[2 * part + i],
+                )
+            )
+    for i, (src, dst) in enumerate(((u_next, u_out), (v_next, v_out))):
+        copies.append(
+            pltpu.make_async_copy(src.at[pl.ds(0, levels * ROWS), :], dst, sems_flow.at[i])
+        )
+    for copy in copies:
+        copy.start()
     lat_even, lon_even = evens()
     chip_even = lax.axis_index("lat") // 2 % 2 == 0
     lane = lanes()
@@ -533,6 +548,15 @@
     for t in range(STEPS):
         own_buf[pl.ds(t, GROUP, stride=STEPS), :] = height.own[t]
     out[...] = own_buf[2 * ROWS : 3 * ROWS, :]
+    for copy in copies:
+        copy.wait()
+
+
+def join_kernel(count, *refs):
+    at = 0
+    for ref in refs[:count]:
+        refs[-1][at : at + ref.shape[0]] = ref[...]
+        at += ref.shape[0]
 
 
 def swap(value, axis, partner):
@@ -562,10 +586,11 @@
 
 
 VMEM = pl.BlockSpec(memory_space=pltpu.VMEM)
+ANY = pl.BlockSpec(memory_space=pl.ANY)
 HBM = pl.BlockSpec(memory_space=pltpu.HBM)
 
 
-def call(kernel, outs, scratch, *args, ins=None, out_specs=None, cost=0):
+def call(kernel, outs, scratch, *args, ins=None, out_specs=None):
     return pl.pallas_call(
         kernel,
         out_shape=outs,
@@ -573,7 +598,7 @@
         out_specs=out_specs or jax.tree.map(lambda _: VMEM, outs),
         scratch_shapes=scratch,
         compiler_params=pltpu.CompilerParams(vmem_limit_bytes=32 * 2**20),
-        cost_estimate=pl.CostEstimate(flops=cost, bytes_accessed=4 * 2**20, transcendentals=0),
+        cost_estimate=pl.CostEstimate(flops=0, bytes_accessed=4 * 2**20, transcendentals=0),
     )(*args)
 
 
@@ -592,67 +617,78 @@
         for x in (heat_anomaly, saltiness_anomaly, zonal_current_array, meridional_current_array)
     ]
     padded, tiles = shape(PADDED, cols), lambda n: shape(n, *TILE)
-    *kept, to_0, to_1, depth = call(
+    *kept, to_0, to_1, depth, prior = call(
         functools.partial(load_kernel, levels),
-        (padded,) * 4 + (tiles(HALO + 2), tiles(HALO + 2), shape(rows, cols)),
-        [pltpu.SemaphoreType.DMA((2 * GROUPS,))],
-        *[pltpu.with_memory_space_constraint(x, pltpu.HBM) for x in fields],
-        ocean_layer_number,
-        ins=[HBM] * 4 + [VMEM],
-        cost=10**6,
+        (padded,) * 4 + (tiles(HALO + 2), tiles(HALO + 2), shape(rows, cols), shape(rows, cols)),
+        [
+            pltpu.VMEM((rows, cols), jnp.int32),
+            pltpu.SemaphoreType.DMA((2 * GROUPS,)),
+            pltpu.SemaphoreType.DMA((2,)),
+        ],
+        *[
+            pltpu.with_memory_space_constraint(x, pltpu.HBM)
+            for x in (*fields, ocean_layer_number, sea_height_prior)
+        ],
+        ins=[HBM] * 6,
     )
     swap_0, swap_1 = swap(to_0, "lat", even_first), swap(to_1, "lat", odd_first)
-    side = call(side_kernel, tiles(PACKS + 1), [], *kept, depth, cost=10**7)
-    side = call(corner_kernel, tiles(SIDE), [], swap_0, swap_1, side, cost=10**6)
+    side = call(side_kernel, tiles(PACKS + 1), [], *kept, depth)
+    side = call(corner_kernel, tiles(SIDE), [], swap_0, swap_1, side)
     side_0, side_1 = swap(side, "lon", even_first), swap(side, "lon", odd_first)
 
     around = (swap_0, swap_1, side, side_0, side_1)
-    store = pltpu.VMEM((3 * (ROWS + 4), *TILE), jnp.float32)
-    u_next, v_next, block, strip_0, strip_1 = call(
+    u_next, v_next, block, strip_0, strip_1, store = call(
         functools.partial(momentum_kernel, lat_total),
-        (padded, padded, tiles(BLOCK), tiles(STRIP), tiles(STRIP)),
-        [store]
-        + [pltpu.VMEM((GROUP * ROWS, COLS), jnp.float32)] * 2
+        (padded, padded, tiles(BLOCK), tiles(STRIP), tiles(STRIP), tiles(3 * (ROWS + 4))),
+        [pltpu.VMEM((GROUP * ROWS, COLS), jnp.float32)] * 2
         + [pltpu.VMEM((ROWS, *TILE), jnp.float32)] * 2,
         *kept,
         depth,
-        sea_height_prior,
+        prior,
         *around,
-        cost=10**7,
     )
+    pieces = []
+    for part in range(PARTS):
+        pieces += call(
+            functools.partial(tracer_kernel, part),
+            (shape(PART, cols),) * 2,
+            [],
+            *kept,
+            depth,
+            *around,
+            store,
+        )
+
+    def join(messages, parts):
+        made = [piece for part in parts for piece in pieces[2 * part : 2 * part + 2]]
+        return call(
+            functools.partial(join_kernel, len(messages)),
+            tiles(sum(x.shape[0] for x in messages)),
+            [],
+            *messages,
+            *made,
+            ins=[VMEM] * len(messages) + [ANY] * len(made),
+        )
+
     strips = [swap(strip_0, "lon", even_first), swap(strip_1, "lon", odd_first)]
-    own = jnp.concatenate([block, *strips])
+    own = join([block, *strips], (0, 1))
     core = swap(own, "lat", even_first)
-    chip = jnp.concatenate([own, core])
+    chip = join([own, core], (2,))
     chip_0, chip_1 = swap(chip, "lat", chip_even_first), swap(chip, "lat", chip_odd_first)
     out = shape(levels * rows, cols)
-    results = call(
-        functools.partial(tracer_kernel, levels),
-        (out,) * 4,
-        [
-            store,
-            pltpu.VMEM((PADDED, COLS), jnp.float32),
-            pltpu.VMEM((PADDED, COLS), jnp.float32),
-            pltpu.SemaphoreType.DMA((GROUPS,)),
-            pltpu.SemaphoreType.DMA((2,)),
-        ],
-        *kept,
-        depth,
-        *around,
-        u_next,
-        v_next,
-        out_specs=(HBM,) * 4,
-        cost=10**7,
-    )
-    height = call(
+    *results, height = call(
         functools.partial(solve_kernel, levels),
-        shape(rows, cols),
-        [pltpu.VMEM((5 * ROWS, COLS), jnp.float32)] * 2,
+        (out,) * 4 + (shape(rows, cols),),
+        [pltpu.VMEM((5 * ROWS, COLS), jnp.float32)] * 2
+        + [pltpu.SemaphoreType.DMA((2 * PARTS,)), pltpu.SemaphoreType.DMA((2,))],
         own,
         core,
         chip_0,
         chip_1,
-        cost=10**7,
+        u_next,
+        v_next,
+        *pieces,
+        out_specs=(HBM,) * 4 + (VMEM,),
     )
     return *[x.reshape(levels, rows, cols) for x in results], height
 

time: 49.5 us -> 50.4 us (1.018)
  the two profiles are of different devices: /device:TPU:2 before, /device:TPU:1 now
where the time goes in v3:
time: 50.4 us; the launch traced here: 50.3 us
  starting transfers between devices  22.3 us (44%)
  Pallas kernels  17.2 us (34%)
  waiting for transfers between devices  9.95 us (20%)
  between operations  0.74 us (1%)
    ppermute x9, starting transfers between devices, swap(): return lax.ppermute(value, axis, pairs)  22.3 us
    pallas_call x11, Pallas kernels, call(): pl.pallas_call(kernel, out_shape=outs, in_specs=ins or [VMEM] * len(args)...  17.2 us
    ppermute x9, waiting for transfers between devices, swap(): return lax.ppermute(value, axis, pairs)  9.95 us
  transfers between devices with their start and end apart: 9, of which 6 were waited for; matrix products, arithmetic and copies ran while one was open for 0% of the time, Pallas kernels for 11%

profile of v3, /device:TPU:1, one launch (start us, length us, event | category | flops | bytes accessed | tf_op | source)
XLA Modules:
  0.0 50.3 jit_solution(6962593988081501728)
XLA Ops:
  0.6 1.8 %shard_map.101 = (f32[1024,128]{1,0:T(8,128)S(1)}, f32[1024,128]{1,0:T(8,128)S(1)}, f32[1024,128]{1,0:T(8,128)S(1)}, f32[1024,128]{1,0:T(8,128)S(1)}, f32[66,8,1...) custom-call(f32[992,128]{1,0:T(8,128)} %bitcast.8, ...), custom_call_target="tpu_custom_call" | custom-call | bytes 4194304 | tf_op jit(solution)/shard_map/pallas_call | solution.py:594
  2.5 3.3 %collective-permute-start = (f32[66,8,128]{2,1,0:T(8,128)S(1)}, f32[66,8,128]{2,1,0:T(8,128)S(1)}, u32[]{:S(2)}, u32[]{:S(2)}) collective-permute-start(f32[66,8,128]{2,1,0:T(8,128)S(1)} %get-tuple-element.38), channel_id=1, source_target_pairs={{0,32},{32,0},{64,96},{96,64},{128,160},{160,128},{192,224},{224,1... | collective-permute-start | bytes 811016 | tf_op jit(solution)/shard_map/ppermute | solution.py:565
  5.8 1.9 %collective-permute-start.1 = (f32[66,8,128]{2,1,0:T(8,128)S(1)}, f32[66,8,128]{2,1,0:T(8,128)S(1)}, u32[]{:S(2)}, u32[]{:S(2)}) collective-permute-start(f32[66,8,128]{2,1,0:T(8,128)S(1)} %get-tuple-element.39), channel_id=1, source_target_pairs={{32,64},{64,32},{96,128},{128,96},{160,192},{192,160},{33,65},{65,... | collective-permute-start | bytes 811016 | tf_op jit(solution)/shard_map/ppermute | solution.py:565
  7.7 1.2 %shard_map.102.side_in = f32[17,8,128]{2,1,0:T(8,128)S(1)} custom-call(f32[1024,128]{1,0:T(8,128)S(1)} %get-tuple-element.32.t, f32[1024,128]{1,0:T(8,128)S(1)} %get-tuple-element.33.s, f32[1024,128]{1,0:T(8,128)S(1)} %get-tuple-element.34.u, f32[1024,128]{1,0:T(8,128)S(1)} %get-tuple-element.35.v, f32[16,128]{1,0:T(8,128)S(1)} %get-tuple-element.36.depth), custom_call_target="tpu_custom_call" | custom-call | bytes 4194304 | tf_op jit(solution)/shard_map/pallas_call | solution.py:594
  9.0 0.0 collective-permute-done.swap_0
  9.0 4.6 %collective-permute-done.1.swap_1 = f32[66,8,128]{2,1,0:T(8,128)S(1)} collective-permute-done((f32[66,8,128]{2,1,0:T(8,128)S(1)}, f32[66,8,128]{2,1,0:T(8,128)S(1)}, u32[]{:S(2)}, u32[]{:S(2)}) %collective-permute-start.1) | collective-permute-done | bytes 270368 | tf_op jit(solution)/shard_map/ppermute | solution.py:565
  13.6 0.2 shard_map.103.own
  13.7 6.7 %collective-permute-start.3 = (f32[20,8,128]{2,1,0:T(8,128)S(1)}, f32[20,8,128]{2,1,0:T(8,128)S(1)}, u32[]{:S(2)}, u32[]{:S(2)}) collective-permute-start(f32[20,8,128]{2,1,0:T(8,128)S(1)} %shard_map.103.own), channel_id=1, source_target_pairs={{0,31},{1,2},{2,1},{3,4},{4,3},{5,6},{6,5},{7,8},{8,7},{9,10},{10,... | collective-permute-start | bytes 245768 | tf_op jit(solution)/shard_map/ppermute | solution.py:565
  20.4 0.0 collective-permute-start.2
  20.4 1.8 %collective-permute-done.3.side_1 = f32[20,8,128]{2,1,0:T(8,128)S(1)} collective-permute-done((f32[20,8,128]{2,1,0:T(8,128)S(1)}, f32[20,8,128]{2,1,0:T(8,128)S(1)}, u32[]{:S(2)}, u32[]{:S(2)}) %collective-permute-start.3) | collective-permute-done | bytes 81952 | tf_op jit(solution)/shard_map/ppermute | solution.py:565
  22.2 1.5 %collective-permute-done.2.side_0 = f32[20,8,128]{2,1,0:T(8,128)S(1)} collective-permute-done((f32[20,8,128]{2,1,0:T(8,128)S(1)}, f32[20,8,128]{2,1,0:T(8,128)S(1)}, u32[]{:S(2)}, u32[]{:S(2)}) %collective-permute-start.2) | collective-permute-done | bytes 81952 | tf_op jit(solution)/shard_map/ppermute | solution.py:565
  23.7 4.4 %shard_map.104 = (f32[1024,128]{1,0:T(8,128)S(1)}, f32[1024,128]{1,0:T(8,128)S(1)}, f32[8,8,128]{2,1,0:T(8,128)S(1)}, f32[2,8,128]{2,1,0:T(8,128)S(1)}, f32[2,8,...) custom-call(f32[1024,128]{1,0:T(8,128)S(1)} %get-tuple-element.32.t, f32[1024,128]{1,0:T(8,128)S(1)} %get-tuple-element.33.s, ...), custom_call_target="tpu_custom_call" | custom-call | bytes 4194304 | tf_op jit(solution)/shard_map/pallas_call | solution.py:594
  28.1 0.1 collective-permute-start.4
  28.2 3.4 %collective-permute-start.5 = (f32[2,8,128]{2,1,0:T(8,128)S(1)}, f32[2,8,128]{2,1,0:T(8,128)S(1)}, u32[]{:S(2)}, u32[]{:S(2)}) collective-permute-start(f32[2,8,128]{2,1,0:T(8,128)S(1)} %get-tuple-element.42), channel_id=1, source_target_pairs={{0,31},{1,2},{2,1},{3,4},{4,3},{5,6},{6,5},{7,8},{8,7},{9,10},{10,... | collective-permute-start | bytes 24584 | tf_op jit(solution)/shard_map/ppermute | solution.py:565
  31.6 1.1 %shard_map.106 = (f32[256,128]{1,0:T(8,128)S(1)}, f32[256,128]{1,0:T(8,128)S(1)}) custom-call(f32[1024,128]{1,0:T(8,128)S(1)} %get-tuple-element.32.t, f32[1024,128]{1,0:T(8,128)S(1)} %get-tuple-element.33.s, f32[1024,128]{1,0:T(8,128)S(1)} %get-tuple-element.34.u, f32[1024,128]{1,0:T(8,128)S(1)} %get-tuple-element.35.v, ...), custom_call_target="tpu_custom_call" | custom-call | bytes 4194304 | tf_op jit(solution)/shard_map/pallas_call | solution.py:594
  32.7 1.1 %shard_map.105 = (f32[256,128]{1,0:T(8,128)S(1)}, f32[256,128]{1,0:T(8,128)S(1)}) custom-call(f32[1024,128]{1,0:T(8,128)S(1)} %get-tuple-element.32.t, f32[1024,128]{1,0:T(8,128)S(1)} %get-tuple-element.33.s, f32[1024,128]{1,0:T(8,128)S(1)} %get-tuple-element.34.u, f32[1024,128]{1,0:T(8,128)S(1)} %get-tuple-element.35.v, ...), custom_call_target="tpu_custom_call" | custom-call | bytes 4194304 | tf_op jit(solution)/shard_map/pallas_call | solution.py:594
  33.8 0.0 collective-permute-done.4.refs_1_
  33.9 0.2 collective-permute-done.5.refs_2_
  34.1 0.0 collective-permute-start.6
  34.1 1.1 %shard_map.108 = (f32[256,128]{1,0:T(8,128)S(1)}, f32[256,128]{1,0:T(8,128)S(1)}) custom-call(f32[1024,128]{1,0:T(8,128)S(1)} %get-tuple-element.32.t, f32[1024,128]{1,0:T(8,128)S(1)} %get-tuple-element.33.s, f32[1024,128]{1,0:T(8,128)S(1)} %get-tuple-element.34.u, f32[1024,128]{1,0:T(8,128)S(1)} %get-tuple-element.35.v, ...), custom_call_target="tpu_custom_call" | custom-call | bytes 4194304 | tf_op jit(solution)/shard_map/pallas_call | solution.py:594
  35.2 0.1 collective-permute-done.6.refs_1_.core
  35.3 0.7 %collective-permute-start.8 = (f32[24,8,128]{2,1,0:T(8,128)S(1)}, f32[24,8,128]{2,1,0:T(8,128)S(1)}, u32[]{:S(2)}, u32[]{:S(2)}) collective-permute-start(f32[24,8,128]{2,1,0:T(8,128)S(1)} %shard_map.109), channel_id=1, source_target_pairs={{64,128},{96,160},{128,64},{160,96},{65,129},{97,161},{129,65},{16... | collective-permute-start | bytes 294920 | tf_op jit(solution)/shard_map/ppermute | solution.py:565
  36.0 6.3 %collective-permute-start.7 = (f32[24,8,128]{2,1,0:T(8,128)S(1)}, f32[24,8,128]{2,1,0:T(8,128)S(1)}, u32[]{:S(2)}, u32[]{:S(2)}) collective-permute-start(f32[24,8,128]{2,1,0:T(8,128)S(1)} %shard_map.109), channel_id=1, source_target_pairs={{0,64},{32,96},{64,0},{96,32},{128,192},{160,224},{192,128},{224,1... | collective-permute-start | bytes 294920 | tf_op jit(solution)/shard_map/ppermute | solution.py:565
  42.3 1.1 %shard_map.110 = (f32[256,128]{1,0:T(8,128)S(1)}, f32[256,128]{1,0:T(8,128)S(1)}) custom-call(f32[1024,128]{1,0:T(8,128)S(1)} %get-tuple-element.32.t, f32[1024,128]{1,0:T(8,128)S(1)} %get-tuple-element.33.s, f32[1024,128]{1,0:T(8,128)S(1)} %get-tuple-element.34.u, f32[1024,128]{1,0:T(8,128)S(1)} %get-tuple-element.35.v, ...), custom_call_target="tpu_custom_call" | custom-call | bytes 4194304 | tf_op jit(solution)/shard_map/pallas_call | solution.py:594
  43.4 0.0 collective-permute-done.8.chip_1
  43.4 1.7 %collective-permute-done.7.chip_0 = f32[24,8,128]{2,1,0:T(8,128)S(1)} collective-permute-done((f32[24,8,128]{2,1,0:T(8,128)S(1)}, f32[24,8,128]{2,1,0:T(8,128)S(1)}, u32[]{:S(2)}, u32[]{:S(2)}) %collective-permute-start.7) | collective-permute-done | bytes 98336 | tf_op jit(solution)/shard_map/ppermute | solution.py:565
  45.2 5.1 %shard_map.111 = (f32[992,128]{1,0:T(8,128)}, f32[992,128]{1,0:T(8,128)}, f32[992,128]{1,0:T(8,128)}, f32[992,128]{1,0:T(8,128)}, f32[16,128]{1,0:T(8,128)}) custom-call(f32[12,8,128]{2,1,0:T(8,128)S(1)} %shard_map.107.refs_0_.own, f32[12,8,128]{2,1,0:T(8,128)S(1)} %collective-permute-done.6.refs_1_.core, f32[24,8,128]{2,1,0:T(8,128)S(1)} %collective-permute-done.7.chip_0, ...), custom_call_target="tpu_custom_call" | custom-call | bytes 4194304 | tf_op jit(solution)/shard_map/pallas_call | solution.py:594
  (2 shorter events, 0.0 us)
Async XLA Ops:
  2.5 6.5 %collective-permute-start = (f32[66,8,128]{2,1,0:T(8,128)S(1)}, f32[66,8,128]{2,1,0:T(8,128)S(1)}, u32[]{:S(2)}, u32[]{:S(2)}) collective-permute-start(f32[66,8,128]{2,1,0:T(8,128)S(1)} %get-tuple-element.38), channel_id=1, source_target_pairs={{0,32},{32,0},{64,96},{96,64},{128,160},{160,128},{192,224},{224,1... | collective-permute-start | bytes 811016 | tf_op jit(solution)/shard_map/ppermute | solution.py:565
  5.8 7.8 %collective-permute-start.1 = (f32[66,8,128]{2,1,0:T(8,128)S(1)}, f32[66,8,128]{2,1,0:T(8,128)S(1)}, u32[]{:S(2)}, u32[]{:S(2)}) collective-permute-start(f32[66,8,128]{2,1,0:T(8,128)S(1)} %get-tuple-element.39), channel_id=1, source_target_pairs={{32,64},{64,32},{96,128},{128,96},{160,192},{192,160},{33,65},{65,... | collective-permute-start | bytes 811016 | tf_op jit(solution)/shard_map/ppermute | solution.py:565
  13.7 8.5 %collective-permute-start.3 = (f32[20,8,128]{2,1,0:T(8,128)S(1)}, f32[20,8,128]{2,1,0:T(8,128)S(1)}, u32[]{:S(2)}, u32[]{:S(2)}) collective-permute-start(f32[20,8,128]{2,1,0:T(8,128)S(1)} %shard_map.103.own), channel_id=1, source_target_pairs={{0,31},{1,2},{2,1},{3,4},{4,3},{5,6},{6,5},{7,8},{8,7},{9,10},{10,... | collective-permute-start | bytes 245768 | tf_op jit(solution)/shard_map/ppermute | solution.py:565
  20.4 3.3 %collective-permute-start.2 = (f32[20,8,128]{2,1,0:T(8,128)S(1)}, f32[20,8,128]{2,1,0:T(8,128)S(1)}, u32[]{:S(2)}, u32[]{:S(2)}) collective-permute-start(f32[20,8,128]{2,1,0:T(8,128)S(1)} %shard_map.103.own), channel_id=1, source_target_pairs={{0,1},{1,0},{2,3},{3,2},{4,5},{5,4},{6,7},{7,6},{8,9},{9,8},{10,11... | collective-permute-start | bytes 245768 | tf_op jit(solution)/shard_map/ppermute | solution.py:565
  28.1 5.8 %collective-permute-start.4 = (f32[2,8,128]{2,1,0:T(8,128)S(1)}, f32[2,8,128]{2,1,0:T(8,128)S(1)}, u32[]{:S(2)}, u32[]{:S(2)}) collective-permute-start(f32[2,8,128]{2,1,0:T(8,128)S(1)} %get-tuple-element.41), channel_id=1, source_target_pairs={{0,1},{1,0},{2,3},{3,2},{4,5},{5,4},{6,7},{7,6},{8,9},{9,8},{10,11... | collective-permute-start | bytes 24584 | tf_op jit(solution)/shard_map/ppermute | solution.py:565
  28.2 5.9 %collective-permute-start.5 = (f32[2,8,128]{2,1,0:T(8,128)S(1)}, f32[2,8,128]{2,1,0:T(8,128)S(1)}, u32[]{:S(2)}, u32[]{:S(2)}) collective-permute-start(f32[2,8,128]{2,1,0:T(8,128)S(1)} %get-tuple-element.42), channel_id=1, source_target_pairs={{0,31},{1,2},{2,1},{3,4},{4,3},{5,6},{6,5},{7,8},{8,7},{9,10},{10,... | collective-permute-start | bytes 24584 | tf_op jit(solution)/shard_map/ppermute | solution.py:565
  34.1 1.2 %collective-permute-start.6 = (f32[12,8,128]{2,1,0:T(8,128)S(1)}, f32[12,8,128]{2,1,0:T(8,128)S(1)}, u32[]{:S(2)}, u32[]{:S(2)}) collective-permute-start(f32[12,8,128]{2,1,0:T(8,128)S(1)} %shard_map.107.refs_0_.own), channel_id=1, source_target_pairs={{0,32},{32,0},{64,96},{96,64},{128,160},{160,128},{192,224},{224,1... | collective-permute-start | bytes 147464 | tf_op jit(solution)/shard_map/ppermute | solution.py:565
  35.3 8.1 %collective-permute-start.8 = (f32[24,8,128]{2,1,0:T(8,128)S(1)}, f32[24,8,128]{2,1,0:T(8,128)S(1)}, u32[]{:S(2)}, u32[]{:S(2)}) collective-permute-start(f32[24,8,128]{2,1,0:T(8,128)S(1)} %shard_map.109), channel_id=1, source_target_pairs={{64,128},{96,160},{128,64},{160,96},{65,129},{97,161},{129,65},{16... | collective-permute-start | bytes 294920 | tf_op jit(solution)/shard_map/ppermute | solution.py:565
  36.0 9.2 %collective-permute-start.7 = (f32[24,8,128]{2,1,0:T(8,128)S(1)}, f32[24,8,128]{2,1,0:T(8,128)S(1)}, u32[]{:S(2)}, u32[]{:S(2)}) collective-permute-start(f32[24,8,128]{2,1,0:T(8,128)S(1)} %shard_map.109), channel_id=1, source_target_pairs={{0,64},{32,96},{64,0},{96,32},{128,192},{160,224},{192,128},{224,1... | collective-permute-start | bytes 294920 | tf_op jit(solution)/shard_map/ppermute | solution.py:565

commit v4 on v3

v4 whole, which is shorter than its diff:
```python
import functools

import jax
import jax.numpy as jnp
from jax import lax
from jax.experimental import pallas as pl
from jax.experimental.pallas import tpu as pltpu
from jax.sharding import PartitionSpec as P

ITERATIONS = 32

TIME_STEP = 0.1
MIX_TRACER = 0.05
MIX_MOMENTUM = 0.05
HEAT_INDEX = 0.2
SALT_INDEX = 0.2
CORIOLIS = 2.0
SURFACE_TERM = 0.0005
TRANSPORT_SCALE = 0.05

ROWS = 16
COLS = 128
GROUP = 8
GROUPS = 8
TILE = (GROUP, COLS)
PADDED = GROUPS * GROUP * ROWS
PARTS = 4
PART = PADDED // PARTS
LOADS = 2
HALO = 2 * 4 * GROUPS
PACKS = 2 * GROUPS
SIDE = GROUPS + 1
ROWS_OUT = HALO + 4
BLOCK = 8
STRIP = 2


def chebyshev_weights(total_steps):
    low_bound = SURFACE_TERM / (SURFACE_TERM + 4.0)
    high_bound = 2.0 - low_bound
    spread_ratio = (high_bound - low_bound) / (high_bound + low_bound)
    middle = 0.5 * (high_bound + low_bound)
    weights = [1.0]
    for number in range(1, total_steps):
        if number == 1:
            weights.append(2.0 / (2.0 - spread_ratio * spread_ratio))
        else:
            weights.append(1.0 / (1.0 - spread_ratio * spread_ratio * weights[-1] / 4.0))
    return [weight / middle for weight in weights], [weight - 1.0 for weight in weights]


def lanes():
    return lax.broadcasted_iota(jnp.int32, TILE, 1)


def sublanes():
    return lax.broadcasted_iota(jnp.int32, TILE, 0)


def turn(value, by, axis=1):
    size = value.shape[axis]
    by = by % size
    return value if by == 0 else pltpu.roll(value, by, axis)


def row_of(ref, row):
    return jnp.broadcast_to(ref[pl.ds(row, 1), :], TILE)


def masked(mask, value):
    return jnp.where(mask, value, 0.0)


def place():
    return lax.axis_index("lat"), lax.axis_index("lon")


def evens():
    lat, lon = place()
    return lat % 2 == 0, lon % 2 == 0


def load_kernel(
    levels, t, s, u, v, depth_in, prior_in, t_out, s_out, u_out, v_out, own, side_0, side_1, depth_out,
    prior, depth, sems, sems_plane,
):
    _, lon_even = evens()
    fields, kept = (t, s, u, v), (t_out, s_out, u_out, v_out)
    planes = [
        pltpu.make_async_copy(src, dst, sems_plane.at[i])
        for i, (src, dst) in enumerate(((depth_in, depth), (prior_in, prior)))
    ]
    copies = []
    for part in range(LOADS):
        first = PADDED // LOADS * part
        span = pl.ds(first, min(PADDED // LOADS, levels * ROWS - first))
        for field in range(4):
            copies.append(
                pltpu.make_async_copy(
                    fields[field].at[span, :], kept[field].at[span, :], sems.at[4 * part + field]
                )
            )
    for copy in planes + copies:
        copy.start()
    for copy in planes:
        copy.wait()
    for half in range(2):
        rows = slice(GROUP * half, GROUP * (half + 1))
        depth_out[rows, :] = depth[rows, :].astype(jnp.float32)
    lane = lanes()
    slot, low = lane // 4, (lane & 3) < 2
    pack = jnp.zeros(TILE, jnp.float32)
    for r in range(ROWS):
        x = row_of(depth_out, r)
        for f in range(2):
            pack = jnp.where(slot == 16 * f + r, turn(x, 64 * f + 4 * r + 2), pack)
    own[PACKS] = pack
    side_0[GROUPS] = pack
    side_1[GROUPS] = pack

    def body(g, carry):
        packs = []
        for pair in range(2):
            pack = jnp.zeros(TILE, jnp.float32)
            for f in range(2):
                for r in range(ROWS):
                    x = kept[2 * pair + f][pl.ds(GROUP * ROWS * g + r, GROUP, stride=ROWS), :]
                    pack = jnp.where(slot == 16 * f + r, turn(x, 64 * f + 4 * r + 2), pack)
            own[pair * GROUPS + g] = pack
            packs.append(pack)
        to_east = jnp.where(low, packs[0], turn(packs[1], 2))
        to_west = jnp.where(low, turn(packs[1], -2), packs[0])
        side_0[g] = jnp.where(lon_even, to_east, to_west)
        side_1[g] = jnp.where(lon_even, to_west, to_east)
        return carry

    for part in range(LOADS):
        for copy in copies[4 * part : 4 * part + 4]:
            copy.wait()
        lax.fori_loop(GROUPS // LOADS * part, GROUPS // LOADS * (part + 1), body, 0)


def rows_kernel(t, s, u, v, depth, swap_0, swap_1):
    lat_even, _ = evens()
    fields = (t, s, u, v)
    outer = jnp.where(lat_even, ROWS - 2, 0)

    def body(g, carry):
        for field in range(4):
            for r in range(2):
                for swap, row in ((swap_0, outer), (swap_1, ROWS - 2 - outer)):
                    swap[(r * 4 + field) * GROUPS + g] = fields[field][
                        pl.ds(GROUP * ROWS * g + row + r, GROUP, stride=ROWS), :
                    ]
        return carry

    lax.fori_loop(0, GROUPS, body, 0)
    for half in range(2):
        x = depth[GROUP * half : GROUP * (half + 1), :]
        swap_0[HALO + half] = x
        swap_1[HALO + half] = x


class Around:
    def __init__(self, own, side_0, side_1, swap_0=None, swap_1=None):
        lat, _ = place()
        self.lat_even, self.lon_even = evens()
        self.first, self.final = lat == 0, lat == lax.axis_size("lat") - 1
        lane = lanes()
        self.lane, self.column, self.row = lane, lane & 3, (lane // 4) & 15
        self.low, self.column_2 = self.column < 2, self.column == 2
        self.own, self.sides, self.swaps = own, (side_0, side_1), (swap_0, swap_1)

    def beside(self, tile):
        a, b = self.sides[0][tile], self.sides[1][tile]
        return jnp.where(self.lon_even, a, b), jnp.where(self.lon_even, b, a)

    def beyond(self, north, index):
        a, b = self.swaps if north else self.swaps[::-1]
        return jnp.where(self.lat_even, a[index], b[index])

    def columns(self, pair, g):
        east, west = self.beside(g)
        if pair == 1:
            east, west = turn(east, 2), turn(west, -2)
        own = self.own[pair * GROUPS + g]
        return jnp.where(self.low, west, own), jnp.where(self.low, own, east)

    def depth_columns(self):
        east, west = self.beside(GROUPS)
        own = self.own[PACKS]
        return jnp.where(self.low, west, own), jnp.where(self.low, own, east)

    def corner(self, pair, g):
        at = 4 * (g + GROUPS * pair)
        south = pltpu.roll(self.beyond(False, HALO + 2), (COLS - at) % COLS, 1)
        north = pltpu.roll(self.beyond(True, HALO + 2), (COLS + 60 - at) % COLS, 1)
        return jnp.where(self.row == 0, south, north)

    def corner_depth(self):
        south = jnp.where(self.first, 0.0, self.beyond(False, HALO + 3))
        north = jnp.where(self.final, 0.0, self.beyond(True, HALO + 3))
        return jnp.where(self.row == 0, south, north)

    def row_depth(self, j):
        if j < 0:
            x, outside = self.beyond(False, HALO + 1)[GROUP + j : GROUP + j + 1, :], self.first
        else:
            x, outside = self.beyond(True, HALO)[j - ROWS : j - ROWS + 1, :], self.final
        return jnp.where(outside, 0.0, jnp.broadcast_to(x, TILE))

    def level_row(self, ref, field, g, j):
        if 0 <= j < ROWS:
            return ref[pl.ds(GROUP * ROWS * g + j, GROUP, stride=ROWS), :]
        return self.beyond(j >= ROWS, ((j - ROWS if j >= ROWS else j + 2) * 4 + field) * GROUPS + g)

    def neighbours(self, q, corner):
        north = jnp.where(self.row == ROWS - 1, corner, turn(q, -4))
        south = jnp.where(self.row == 0, corner, turn(q, 4))
        return turn(q, -1), turn(q, 1), north, south

    def join(self, west, east):
        return jnp.where(self.column_2, east, turn(west, 2))

    def sideways(self, q, edge, f, r):
        edge = turn(edge, 127 - (64 * f + 4 * r + 2))
        east = jnp.where(self.lane == COLS - 1, edge, turn(q, -1))
        west = jnp.where(self.lane == 0, edge, turn(q, 1))
        return east, west


def corner_kernel(rows_0, rows_1, own, side_0, side_1, swap_0, swap_1):
    near = Around(own, side_0, side_1)
    slot = near.row
    for swap, rows, upper in (
        (swap_0, rows_0, near.lat_even),
        (swap_1, rows_1, jnp.logical_not(near.lat_even)),
    ):
        swap[: HALO + 2] = rows[...]
        from_row = jnp.where(upper, 4 * (ROWS - 1), 0)
        tile = jnp.zeros(TILE, jnp.float32)
        for pair in range(2):
            for g in range(GROUPS):
                west, east = near.columns(pair, g)
                at = g + GROUPS * pair
                moved = pltpu.roll(jnp.where(near.low, west, east), (4 * at + COLS - from_row) % COLS, 1)
                tile = jnp.where(slot == at, moved, tile)
        swap[HALO + 2] = tile
        west, east = near.depth_columns()
        shift = jnp.where(upper, COLS - 60, 60)
        swap[HALO + 3] = pltpu.roll(jnp.where(near.low, west, east), shift, 1)


class Depths:
    def __init__(self, inner, outer=None):
        self.inner, self.outer = inner, outer

    def tile(self, j, which):
        if 0 <= j < ROWS:
            return self.inner[3 * j + which]
        return self.outer[3 * (j + 2 if j < 0 else j - ROWS + 2) + which]

    def build_inner(self, near, depth):
        ring = near.join(*near.depth_columns())
        for j in range(ROWS):
            d = row_of(depth, j)
            self.inner[3 * j] = d
            self.inner[3 * j + 1], self.inner[3 * j + 2] = near.sideways(d, ring, 0, j)

    def build_outer(self, near):
        corner = near.corner_depth()
        ring = near.join(corner, corner)
        for j in (-2, -1, ROWS, ROWS + 1):
            at = 3 * (j + 2 if j < 0 else j - ROWS + 2)
            d = near.row_depth(j)
            self.outer[at] = d
            d_e, d_w = near.sideways(d, ring, 0, 0 if j < 0 else ROWS - 1)
            self.outer[at + 1], self.outer[at + 2] = d_e, d_w


class Edges:
    def __init__(self, near, g, level, with_laplacian, corners):
        self.ring, self.corner, self.lap = {}, {}, {}
        corner_d = near.corner_depth() if corners else jnp.zeros(TILE, jnp.float32)
        depths = [(d, *near.neighbours(d, corner_d)) for d in near.depth_columns()]
        for pair in range(2):
            corner = jnp.zeros(TILE, jnp.float32)
            if corners:
                corner = masked(level < corner_d, near.corner(pair, g))
            sides, laps = [], []
            for q, d_all in zip(near.columns(pair, g), depths):
                here = level < d_all[0]
                q = masked(here, q)
                sides.append(q)
                if pair in with_laplacian:
                    e, w, n, s = near.neighbours(q, corner)
                    count = sum(jnp.where(level < d, 1.0, 0.0) for d in d_all[1:])
                    laps.append(masked(here, ((e + w) + n) + s - count * q))
            self.ring[pair] = near.join(*sides)
            self.corner[pair] = near.join(corner, corner)
            if laps:
                self.lap[pair] = near.join(*laps)

    def edge(self, pair, j):
        return self.ring[pair] if 0 <= j < ROWS else self.corner[pair]


def prefix(x, sub):
    for by in (1, 2, 4):
        x = x + jnp.where(sub >= by, turn(x, by, 0), 0.0)
    return x


def laplace_row(near, dep, level, wet, q, edges, pair, j):
    count = (
        jnp.where(level < dep.tile(j, 1), 1.0, 0.0) + jnp.where(level < dep.tile(j, 2), 1.0, 0.0)
    ) + (jnp.where(wet[j + 1], 1.0, 0.0) + jnp.where(wet[j - 1], 1.0, 0.0))
    laps, sides = [], []
    for f in range(2):
        e, w = near.sideways(q[j][f], edges.edge(pair, j), f, min(max(j, 0), ROWS - 1))
        sides.append((e, w))
        total = (e + w) + (q[j + 1][f] + q[j - 1][f])
        laps.append(masked(wet[j], total - count * q[j][f]))
    return laps, sides, count


def momentum_levels(
    near, dep, lat_total, windows, corners, t, s, u, v, u_next, v_next, sum_x, sum_y, sum_u, sum_v
):
    sub = sublanes()
    zero = jnp.zeros(TILE, jnp.float32)
    for first, last in windows:
        for r in range(first, last + 1):
            for ref in (sum_x, sum_y):
                ref[GROUP * r : GROUP * (r + 1), :] = zero
            for ref in (sum_u, sum_v):
                ref[r] = zero
    first_row = (place()[0] * ROWS).astype(jnp.float32)

    def body(g, carry):
        start = GROUP * ROWS * g
        level = (GROUP * g + sub).astype(jnp.float32)
        edges = Edges(near, g, level, (1,), corners)
        edge_load = turn(edges.ring[0], 64) - edges.ring[0]
        for first, last in windows:
            wet, q, lap, dens, count = {}, {}, {}, {}, {}
            for j in range(first - 2, last + 3):
                wet[j] = level < dep.tile(j, 0)
                q[j] = [masked(wet[j], near.level_row(ref, i, g, j)) for i, ref in ((2, u), (3, v))]
                if first - 1 <= j <= last + 1:
                    dens[j] = masked(wet[j], near.level_row(s, 1, g, j) - near.level_row(t, 0, g, j))
                if j >= first:
                    lap[j - 1], _, count[j - 1] = laplace_row(near, dep, level, wet, q, edges, 1, j - 1)
                r = j - 2
                if r < first:
                    continue
                mixes = []
                for f in range(2):
                    e, w = near.sideways(lap[r][f], edges.lap[1], f, r)
                    mixes.append((e + w) + (lap[r + 1][f] + lap[r - 1][f]) - count[r] * lap[r][f])
                e, w = near.sideways(dens[r], edge_load, 0, r)
                final = GROUP * r + GROUP - 1
                grad_x = prefix(e - w, sub) + row_of(sum_x, final)
                grad_y = prefix(dens[r + 1] - dens[r - 1], sub) + row_of(sum_y, final)
                sum_x[GROUP * r : GROUP * (r + 1), :] = grad_x
                sum_y[GROUP * r : GROUP * (r + 1), :] = grad_y
                turning = TIME_STEP * CORIOLIS * (2.0 * (first_row + (r + 0.5)) / lat_total - 1.0)
                pull = TIME_STEP * 0.5 * SALT_INDEX
                mix = TIME_STEP * MIX_MOMENTUM
                new_u = masked(
                    wet[r], q[r][0] + ((turning * q[r][1] - pull * grad_x) - mix * mixes[0])
                )
                new_v = masked(
                    wet[r], q[r][1] - ((turning * q[r][0] + pull * grad_y) + mix * mixes[1])
                )
                u_next[pl.ds(start + r, GROUP, stride=ROWS), :] = new_u
                v_next[pl.ds(start + r, GROUP, stride=ROWS), :] = new_v
                sum_u[r] += new_u
                sum_v[r] += new_v
        return carry

    lax.fori_loop(0, GROUPS, body, 0)


def write_sums(windows, sum_u, sum_v, block):
    for first, last in windows:
        for r in range(first, last + 1):
            half, row = divmod(r, GROUP)
            block[half, row : row + 1, :] = jnp.sum(sum_u[r], axis=0, keepdims=True)
            block[2 + half, row : row + 1, :] = jnp.sum(sum_v[r], axis=0, keepdims=True)


INNER = ((2, ROWS - 3),)
OUTER = ((0, 1), (ROWS - 2, ROWS - 1))


def inner_kernel(
    lat_total, t, s, u, v, depth, own, side_0, side_1, u_next, v_next, sums, inner,
    sum_x, sum_y, sum_u, sum_v,
):
    near, dep = Around(own, side_0, side_1), Depths(inner)
    dep.build_inner(near, depth)
    momentum_levels(
        near, dep, lat_total, INNER, False, t, s, u, v, u_next, v_next, sum_x, sum_y, sum_u, sum_v
    )
    sums[...] = jnp.zeros(sums.shape, jnp.float32)
    write_sums(INNER, sum_u, sum_v, sums)


def outer_kernel(
    lat_total, t, s, u, v, depth, prior, own, side_0, side_1, swap_0, swap_1, u_inner, v_inner, sums, inner,
    u_next, v_next, block, strip_0, strip_1, outer, sum_x, sum_y, sum_u, sum_v, total,
):
    near, dep = Around(own, side_0, side_1, swap_0, swap_1), Depths(inner, outer)
    dep.build_outer(near)
    u_next[...] = u_inner[...]
    v_next[...] = v_inner[...]
    total[...] = sums[...]
    momentum_levels(
        near, dep, lat_total, OUTER, True, t, s, u, v, u_next, v_next, sum_x, sum_y, sum_u, sum_v
    )
    write_sums(OUTER, sum_u, sum_v, total)
    quarter = lanes() // 32
    for half in range(2):
        rows = slice(GROUP * half, GROUP * (half + 1))
        planes = [depth[rows, :], prior[rows, :], total[half], total[2 + half]]
        for plane, x in enumerate(planes):
            block[2 * plane + half] = x
        strips = []
        for first in (96, 0):
            strip = jnp.zeros(TILE, jnp.float32)
            for plane, x in enumerate(planes):
                strip = jnp.where(quarter == plane, turn(x, 32 * plane - first), strip)
            strips.append(strip)
        strip_0[half] = jnp.where(near.lon_even, strips[0], strips[1])
        strip_1[half] = jnp.where(near.lon_even, strips[1], strips[0])


def tracer_kernel(
    part, t, s, u, v, own, side_0, side_1, swap_0, swap_1, inner, outer, t_next, s_next
):
    near, dep = Around(own, side_0, side_1, swap_0, swap_1), Depths(inner, outer)
    sub = sublanes()

    def body(g, carry):
        start = GROUP * ROWS * g - PART * part
        level = (GROUP * g + sub).astype(jnp.float32)
        edges = Edges(near, g, level, (0,), True)
        wet, q, sides, lap, flow, count = {}, {}, {}, {}, {}, {}
        for j in range(-2, ROWS + 2):
            wet[j] = level < dep.tile(j, 0)
            q[j] = [masked(wet[j], near.level_row(ref, i, g, j)) for i, ref in ((0, t), (1, s))]
            if -1 <= j <= ROWS:
                flow[j] = [masked(wet[j], near.level_row(ref, i, g, j)) for i, ref in ((2, u), (3, v))]
            if j >= 0:
                lap[j - 1], sides[j - 1], count[j - 1] = laplace_row(
                    near, dep, level, wet, q, edges, 0, j - 1
                )
            r = j - 2
            if r < 0:
                continue
            e, w = near.sideways(flow[r][0], edges.ring[1], 0, r)
            u_e = masked(level < dep.tile(r, 1), flow[r][0] + e)
            u_w = masked(level < dep.tile(r, 2), flow[r][0] + w)
            v_n = masked(wet[r + 1], flow[r][1] + flow[r + 1][1])
            v_s = masked(wet[r - 1], flow[r][1] + flow[r - 1][1])
            for f, out in ((0, t_next), (1, s_next)):
                e, w = near.sideways(lap[r][f], edges.lap[0], f, r)
                mix = (e + w) + (lap[r + 1][f] + lap[r - 1][f]) - count[r] * lap[r][f]
                mid = q[r][f]
                e, w = sides[r][f]
                advected = (u_e * (mid + e) - u_w * (mid + w)) + (
                    v_n * (mid + q[r + 1][f]) - v_s * (mid + q[r - 1][f])
                )
                out[pl.ds(start + r, GROUP, stride=ROWS), :] = masked(
                    wet[r],
                    mid - (0.25 * TIME_STEP * advected + TIME_STEP * MIX_TRACER * mix),
                )
        return carry

    lax.fori_loop(2 * part, 2 * part + 2, body, 0)


def store_kernel(levels, u_next, v_next, *refs):
    pieces, (t_out, s_out, u_out, v_out, stored, sems, sems_flow) = refs[:-7], refs[-7:]
    stored[...] = jnp.zeros(TILE, jnp.float32)
    copies = []
    for i, (src, dst) in enumerate(((u_next, u_out), (v_next, v_out))):
        copies.append(
            pltpu.make_async_copy(src.at[pl.ds(0, levels * ROWS), :], dst, sems_flow.at[i])
        )
    for part in range(PARTS):
        size = min(PART, levels * ROWS - PART * part)
        for i, dst in enumerate((t_out, s_out)):
            copies.append(
                pltpu.make_async_copy(
                    pieces[2 * part + i].at[pl.ds(0, size), :],
                    dst.at[pl.ds(PART * part, size), :],
                    sems.at[2 * part + i],
                )
            )
    for copy in copies:
        copy.start()
    for copy in copies:
        copy.wait()


STEPS = 5 * ROWS // GROUP


class Plane:
    def __init__(self, own, rim):
        self.own, self.rim = own, rim

    def map(self, other, fn):
        if isinstance(other, Plane):
            return Plane(
                [fn(a, b) for a, b in zip(self.own, other.own)],
                [fn(a, b) for a, b in zip(self.rim, other.rim)],
            )
        return Plane([fn(a, other) for a in self.own], [fn(a, other) for a in self.rim])

    def __add__(self, other):
        return self.map(other, lambda a, b: a + b)

    def __sub__(self, other):
        return self.map(other, lambda a, b: a - b)

    def __mul__(self, other):
        return self.map(other, lambda a, b: a * b)

    def low(self, other):
        return self.map(other, jnp.minimum)

    def side(self, by, lane):
        at = lanes() == lane
        pairs = [(turn(a, by), turn(b, by)) for a, b in zip(self.own, self.rim)]
        return Plane([jnp.where(at, b, a) for a, b in pairs], [jnp.where(at, a, b) for a, b in pairs])

    def east(self):
        return self.side(-1, COLS - 1)

    def west(self):
        return self.side(1, 0)

    def north(self):
        return Plane(*[x[1:] + [turn(x[0], -1, 0)] for x in (self.own, self.rim)])

    def south(self):
        return Plane(*[[turn(x[-1], 1, 0)] + x[:-1] for x in (self.own, self.rim)])


def solve_kernel(levels, own, core, chip_0, chip_1, passed, stored, out, own_buf, rim_buf):
    del stored
    lat, _ = place()
    lat_even, lon_even = evens()
    chip_even = lat // 2 % 2 == 0
    lane = lanes()

    def tile(b, index):
        if b == 0:
            return own[index]
        if abs(b) == 2:
            to_first = chip_even if b > 0 else jnp.logical_not(chip_even)
            return jnp.where(to_first, chip_0[index], chip_1[index])
        on_chip = lat_even if b > 0 else jnp.logical_not(lat_even)
        return jnp.where(on_chip, core[index], passed[index])

    def gather(plane):
        for b in range(-2, 3):
            inside = (lat + b >= 0) & (lat + b < lax.axis_size("lat"))
            for half in range(2):
                at = ROWS * (b + 2) + GROUP * half
                mid = tile(b, 2 * plane + half)
                first, second = tile(b, BLOCK + half), tile(b, BLOCK + STRIP + half)
                east = turn(jnp.where(lon_even, first, second), -32 * plane)
                west = turn(jnp.where(lon_even, second, first), 96 - 32 * plane)
                rim = jnp.where(lane < 32, east, jnp.where(lane >= 96, west, 0.0))
                if b != 0:
                    mid, rim = jnp.where(inside, mid, 0.0), jnp.where(inside, rim, 0.0)
                own_buf[at : at + GROUP, :] = mid
                rim_buf[at : at + GROUP, :] = rim
        return Plane(
            *[[buf[pl.ds(t, GROUP, stride=STEPS), :] for t in range(STEPS)] for buf in (own_buf, rim_buf)]
        )

    depth, prior, zonal, northward = [gather(plane) for plane in range(4)]

    ocean = depth.map(0.0, lambda a, b: jnp.where(a > b, 1.0, 0.0))
    depth_east, depth_north = depth.low(depth.east()), depth.low(depth.north())
    zonal_flow = zonal.map(depth_east, lambda a, b: masked(b > 0.0, a))
    north_flow = northward.map(depth_north, lambda a, b: masked(b > 0.0, a))
    divergence = (zonal_flow - zonal_flow.west()) + (north_flow - north_flow.south())
    right_side = prior * SURFACE_TERM - divergence * TRANSPORT_SCALE
    east_face, north_face = depth_east * (1.0 / levels), depth_north * (1.0 / levels)
    west_face, south_face = east_face.west(), north_face.south()
    diagonal = (((east_face + west_face) + north_face) + south_face) + SURFACE_TERM
    inverse = diagonal.map(1.0, lambda a, b: b / a)
    right_side, east_face, west_face, north_face, south_face = [
        x * inverse for x in (right_side, east_face, west_face, north_face, south_face)
    ]
    height, change = prior, None
    scales, carries = chebyshev_weights(ITERATIONS)
    for scale, carry in zip(scales, carries):
        spread = (east_face * height.east() + west_face * height.west()) + (
            north_face * height.north() + south_face * height.south()
        )
        residual = (right_side - height) + spread
        step = residual * scale
        change = step if change is None else step + change * carry
        height = height + change
    height = height * ocean
    for t in range(STEPS):
        own_buf[pl.ds(t, GROUP, stride=STEPS), :] = height.own[t]
    out[...] = own_buf[2 * ROWS : 3 * ROWS, :]


def join_kernel(count, *refs):
    at = 0
    for ref in refs[:count]:
        refs[-1][at : at + ref.shape[0]] = ref[...]
        at += ref.shape[0]


def pass_kernel(chip_0, chip_1, *refs):
    lat, _ = place()
    refs[-1][...] = jnp.where((lat % 2 == 0) == (lat // 2 % 2 == 0), chip_0[...], chip_1[...])


def swap(value, axis, partner):
    count = lax.axis_size(axis)
    return lax.ppermute(value, axis, [(i, partner(i) % count) for i in range(count)])


def even_first(i):
    return i + 1 if i % 2 == 0 else i - 1


def odd_first(i):
    return i - 1 if i % 2 == 0 else i + 1


def chip_even_first(i):
    return i + 2 if i // 2 % 2 == 0 else i - 2


def chip_odd_first(i):
    return i - 2 if i // 2 % 2 == 0 else i + 2


def shape(*dims):
    return jax.ShapeDtypeStruct(dims, jnp.float32)


VMEM = pl.BlockSpec(memory_space=pltpu.VMEM)
ANY = pl.BlockSpec(memory_space=pl.ANY)
HBM = pl.BlockSpec(memory_space=pltpu.HBM)


def call(kernel, outs, scratch, *args, ins=None, out_specs=None):
    return pl.pallas_call(
        kernel,
        out_shape=outs,
        in_specs=ins or [VMEM] * len(args),
        out_specs=out_specs or jax.tree.map(lambda _: VMEM, outs),
        scratch_shapes=scratch,
        compiler_params=pltpu.CompilerParams(vmem_limit_bytes=32 * 2**20),
        cost_estimate=pl.CostEstimate(flops=0, bytes_accessed=4 * 2**20, transcendentals=0),
    )(*args)


def per_device(
    heat_anomaly,
    saltiness_anomaly,
    zonal_current_array,
    meridional_current_array,
    sea_height_prior,
    ocean_layer_number,
):
    levels, rows, cols = heat_anomaly.shape
    lat_total = rows * lax.axis_size("lat")
    fields = [
        x.reshape(levels * rows, cols)
        for x in (heat_anomaly, saltiness_anomaly, zonal_current_array, meridional_current_array)
    ]
    padded, plane = shape(PADDED, cols), shape(rows, cols)

    def tiles(n):
        return shape(n, *TILE)

    *kept, own, to_0, to_1, depth, prior = call(
        functools.partial(load_kernel, levels),
        (padded,) * 4 + (tiles(PACKS + 1), tiles(SIDE), tiles(SIDE), plane, plane),
        [
            pltpu.VMEM((rows, cols), jnp.int32),
            pltpu.SemaphoreType.DMA((4 * LOADS,)),
            pltpu.SemaphoreType.DMA((2,)),
        ],
        *[
            pltpu.with_memory_space_constraint(x, pltpu.HBM)
            for x in (*fields, ocean_layer_number, sea_height_prior)
        ],
        ins=[HBM] * 6,
    )
    sides = (own, swap(to_0, "lon", even_first), swap(to_1, "lon", odd_first))
    rows_0, rows_1 = call(rows_kernel, (tiles(HALO + 2),) * 2, [], *kept, depth)
    to_0, to_1 = call(corner_kernel, (tiles(ROWS_OUT),) * 2, [], rows_0, rows_1, *sides)
    swaps = (swap(to_0, "lat", even_first), swap(to_1, "lat", odd_first))

    scratch = [pltpu.VMEM((GROUP * ROWS, COLS), jnp.float32)] * 2
    scratch += [pltpu.VMEM((ROWS, *TILE), jnp.float32)] * 2
    u_inner, v_inner, sums, inner = call(
        functools.partial(inner_kernel, lat_total),
        (padded, padded, tiles(4), tiles(3 * ROWS)),
        scratch,
        *kept,
        depth,
        *sides,
    )
    u_next, v_next, block, strip_0, strip_1, outer = call(
        functools.partial(outer_kernel, lat_total),
        (padded, padded, tiles(BLOCK), tiles(STRIP), tiles(STRIP), tiles(12)),
        scratch + [pltpu.VMEM((4, *TILE), jnp.float32)],
        *kept,
        depth,
        prior,
        *sides,
        *swaps,
        u_inner,
        v_inner,
        sums,
        inner,
    )
    pieces = []
    for part in range(PARTS):
        pieces += call(
            functools.partial(tracer_kernel, part),
            (shape(PART, cols),) * 2,
            [],
            *kept,
            *sides,
            *swaps,
            inner,
            outer,
        )

    strips = [swap(strip_0, "lon", even_first), swap(strip_1, "lon", odd_first)]
    made = pieces[:4]
    block = call(
        functools.partial(join_kernel, 3),
        tiles(BLOCK + 2 * STRIP),
        [],
        block,
        *strips,
        *made,
        ins=[VMEM] * 3 + [ANY] * len(made),
    )
    chip_0, chip_1 = swap(block, "lat", chip_even_first), swap(block, "lat", chip_odd_first)
    core = swap(block, "lat", even_first)
    made = pieces[4:]
    passed = call(
        pass_kernel,
        tiles(BLOCK + 2 * STRIP),
        [],
        chip_0,
        chip_1,
        *made,
        ins=[VMEM] * 2 + [ANY] * len(made),
    )
    passed = swap(passed, "lat", even_first)
    *results, stored = call(
        functools.partial(store_kernel, levels),
        (shape(levels * rows, cols),) * 4 + (shape(*TILE),),
        [pltpu.SemaphoreType.DMA((2 * PARTS,)), pltpu.SemaphoreType.DMA((2,))],
        u_next,
        v_next,
        *pieces,
        out_specs=(HBM,) * 4 + (VMEM,),
    )
    height = call(
        functools.partial(solve_kernel, levels),
        plane,
        [pltpu.VMEM((5 * ROWS, COLS), jnp.float32)] * 2,
        block,
        core,
        chip_0,
        chip_1,
        passed,
        stored,
        ins=[VMEM] * 5 + [ANY],
    )
    return *[x.reshape(levels, rows, cols) for x in results], height


def solution(mesh):
    cells, plane = P(None, "lat", "lon"), P("lat", "lon")
    return jax.shard_map(
        per_device,
        mesh=mesh,
        in_specs=(cells,) * 4 + (plane,) * 2,
        out_specs=(cells,) * 4 + (plane,),
        check_vma=False,
    )
```

time: 50.4 us -> 46.5 us (0.923)
  waiting for transfers between devices: 9.95 us -> 3.8 us
  Pallas kernels: 17.2 us -> 20 us
    ppermute x9 -> x10, waiting for transfers between devices: 9.95 us -> 3.8 us  [swap(): lax.ppermute(value, axis, [(i, partner(i) % count) for i in range(count)])]
    pallas_call x11 -> x13, Pallas kernels: 17.2 us -> 20 us  [call(): pl.pallas_call(kernel, out_shape=outs, in_specs=ins or [VMEM] * len(args)...]
    ppermute x9 -> x10, starting transfers between devices: 22.3 us -> 21.8 us  [swap(): lax.ppermute(value, axis, [(i, partner(i) % count) for i in range(count)])]
  transfers between devices with their start and end apart: 9 -> 10, of which waited for: 6 -> 3; matrix products, arithmetic and copies ran while one was open for 0% -> 0% of each run, Pallas kernels for 11% -> 21%
where the time goes in v4:
time: 46.5 us; the launch traced here: 46.4 us
  starting transfers between devices  21.8 us (47%)
  Pallas kernels  20 us (43%)
  waiting for transfers between devices  3.8 us (8%)
  between operations  0.79 us (2%)
    ppermute x10, starting transfers between devices, swap(): lax.ppermute(value, axis, [(i, partner(i) % count) for i in range(count)])  21.8 us
    pallas_call x13, Pallas kernels, call(): pl.pallas_call(kernel, out_shape=outs, in_specs=ins or [VMEM] * len(args)...  20 us
    ppermute x10, waiting for transfers between devices, swap(): lax.ppermute(value, axis, [(i, partner(i) % count) for i in range(count)])  3.8 us
  transfers between devices with their start and end apart: 10, of which 3 were waited for; matrix products, arithmetic and copies ran while one was open for 0% of the time, Pallas kernels for 21%

profile of v4, /device:TPU:1, one launch (start us, length us, event | category | flops | bytes accessed | tf_op | source)
XLA Modules:
  0.0 46.4 jit_solution(3300311981430179538)
XLA Ops:
  0.6 3.0 %shard_map.101 = (f32[1024,128]{1,0:T(8,128)S(1)}, f32[1024,128]{1,0:T(8,128)S(1)}, f32[1024,128]{1,0:T(8,128)S(1)}, f32[1024,128]{1,0:T(8,128)S(1)}, f32[17,8,1...) custom-call(f32[992,128]{1,0:T(8,128)} %bitcast.8, ...), custom_call_target="tpu_custom_call" | custom-call | bytes 4194304 | tf_op jit(solution)/shard_map/pallas_call | solution.py:661
  3.7 2.2 %collective-permute-start = (f32[9,8,128]{2,1,0:T(8,128)S(1)}, f32[9,8,128]{2,1,0:T(8,128)S(1)}, u32[]{:S(2)}, u32[]{:S(2)}) collective-permute-start(f32[9,8,128]{2,1,0:T(8,128)S(1)} %get-tuple-element.48), channel_id=1, source_target_pairs={{0,1},{1,0},{2,3},{3,2},{4,5},{5,4},{6,7},{7,6},{8,9},{9,8},{10,11... | collective-permute-start | bytes 110600 | tf_op jit(solution)/shard_map/ppermute | solution.py:632
  5.9 7.2 %collective-permute-start.1 = (f32[9,8,128]{2,1,0:T(8,128)S(1)}, f32[9,8,128]{2,1,0:T(8,128)S(1)}, u32[]{:S(2)}, u32[]{:S(2)}) collective-permute-start(f32[9,8,128]{2,1,0:T(8,128)S(1)} %get-tuple-element.49), channel_id=1, source_target_pairs={{0,31},{1,2},{2,1},{3,4},{4,3},{5,6},{6,5},{7,8},{8,7},{9,10},{10,... | collective-permute-start | bytes 110600 | tf_op jit(solution)/shard_map/ppermute | solution.py:632
  13.1 0.2 shard_map.102
  13.3 0.0 collective-permute-done.side_0
  13.3 1.1 %collective-permute-done.1.side_1 = f32[9,8,128]{2,1,0:T(8,128)S(1)} collective-permute-done((f32[9,8,128]{2,1,0:T(8,128)S(1)}, f32[9,8,128]{2,1,0:T(8,128)S(1)}, u32[]{:S(2)}, u32[]{:S(2)}) %collective-permute-start.1) | collective-permute-done | bytes 36896 | tf_op jit(solution)/shard_map/ppermute | solution.py:632
  14.4 0.2 shard_map.103
  14.6 1.9 %collective-permute-start.2 = (f32[68,8,128]{2,1,0:T(8,128)S(1)}, f32[68,8,128]{2,1,0:T(8,128)S(1)}, u32[]{:S(2)}, u32[]{:S(2)}) collective-permute-start(f32[68,8,128]{2,1,0:T(8,128)S(1)} %get-tuple-element.52), channel_id=1, source_target_pairs={{0,32},{32,0},{64,96},{96,64},{128,160},{160,128},{192,224},{224,1... | collective-permute-start | bytes 835592 | tf_op jit(solution)/shard_map/ppermute | solution.py:632
  16.5 1.2 %collective-permute-start.3 = (f32[68,8,128]{2,1,0:T(8,128)S(1)}, f32[68,8,128]{2,1,0:T(8,128)S(1)}, u32[]{:S(2)}, u32[]{:S(2)}) collective-permute-start(f32[68,8,128]{2,1,0:T(8,128)S(1)} %get-tuple-element.53), channel_id=1, source_target_pairs={{0,224},{32,64},{64,32},{96,128},{128,96},{160,192},{192,160},{224... | collective-permute-start | bytes 835592 | tf_op jit(solution)/shard_map/ppermute | solution.py:632
  17.7 3.5 %shard_map.104 = (f32[1024,128]{1,0:T(8,128)S(1)}, f32[1024,128]{1,0:T(8,128)S(1)}, f32[4,8,128]{2,1,0:T(8,128)S(1)}, f32[48,8,128]{2,1,0:T(8,128)S(1)}) custom-call(f32[1024,128]{1,0:T(8,128)S(1)} %get-tuple-element.41.t, f32[1024,128]{1,0:T(8,128)S(1)} %get-tuple-element.42.s, f32[1024,128]{1,0:T(8,128)S(1)} %get-tuple-element.43.u, ...), custom_call_target="tpu_custom_call" | custom-call | bytes 4194304 | tf_op jit(solution)/shard_map/pallas_call | solution.py:661
  21.2 0.0 collective-permute-done.2.swap_0
  21.2 1.5 %collective-permute-done.3.swap_1 = f32[68,8,128]{2,1,0:T(8,128)S(1)} collective-permute-done((f32[68,8,128]{2,1,0:T(8,128)S(1)}, f32[68,8,128]{2,1,0:T(8,128)S(1)}, u32[]{:S(2)}, u32[]{:S(2)}) %collective-permute-start.3) | collective-permute-done | bytes 278560 | tf_op jit(solution)/shard_map/ppermute | solution.py:632
  22.8 2.9 %shard_map.105 = (f32[1024,128]{1,0:T(8,128)S(1)}, f32[1024,128]{1,0:T(8,128)S(1)}, f32[8,8,128]{2,1,0:T(8,128)S(1)}, f32[2,8,128]{2,1,0:T(8,128)S(1)}, f32[2,8,...) custom-call(f32[1024,128]{1,0:T(8,128)S(1)} %get-tuple-element.41.t, f32[1024,128]{1,0:T(8,128)S(1)} %get-tuple-element.42.s, ...), custom_call_target="tpu_custom_call" | custom-call | bytes 4194304 | tf_op jit(solution)/shard_map/pallas_call | solution.py:661
  25.6 0.1 collective-permute-start.4
  25.7 5.1 %collective-permute-start.5 = (f32[2,8,128]{2,1,0:T(8,128)S(1)}, f32[2,8,128]{2,1,0:T(8,128)S(1)}, u32[]{:S(2)}, u32[]{:S(2)}) collective-permute-start(f32[2,8,128]{2,1,0:T(8,128)S(1)} %get-tuple-element.75), channel_id=1, source_target_pairs={{0,31},{1,2},{2,1},{3,4},{4,3},{5,6},{6,5},{7,8},{8,7},{9,10},{10,... | collective-permute-start | bytes 24584 | tf_op jit(solution)/shard_map/ppermute | solution.py:632
  30.9 1.2 %shard_map.107 = (f32[256,128]{1,0:T(8,128)S(1)}, f32[256,128]{1,0:T(8,128)S(1)}) custom-call(f32[1024,128]{1,0:T(8,128)S(1)} %get-tuple-element.41.t, f32[1024,128]{1,0:T(8,128)S(1)} %get-tuple-element.42.s, f32[1024,128]{1,0:T(8,128)S(1)} %get-tuple-element.43.u, f32[1024,128]{1,0:T(8,128)S(1)} %get-tuple-element.44.v, ...), custom_call_target="tpu_custom_call" | custom-call | bytes 4194304 | tf_op jit(solution)/shard_map/pallas_call | solution.py:661
  32.0 1.2 %shard_map.106 = (f32[256,128]{1,0:T(8,128)S(1)}, f32[256,128]{1,0:T(8,128)S(1)}) custom-call(f32[1024,128]{1,0:T(8,128)S(1)} %get-tuple-element.41.t, f32[1024,128]{1,0:T(8,128)S(1)} %get-tuple-element.42.s, f32[1024,128]{1,0:T(8,128)S(1)} %get-tuple-element.43.u, f32[1024,128]{1,0:T(8,128)S(1)} %get-tuple-element.44.v, ...), custom_call_target="tpu_custom_call" | custom-call | bytes 4194304 | tf_op jit(solution)/shard_map/pallas_call | solution.py:661
  33.2 0.0 collective-permute-done.4.refs_1_
  33.2 0.0 collective-permute-done.5.refs_2_
  33.3 3.5 %collective-permute-start.8 = (f32[12,8,128]{2,1,0:T(8,128)S(1)}, f32[12,8,128]{2,1,0:T(8,128)S(1)}, u32[]{:S(2)}, u32[]{:S(2)}) collective-permute-start(f32[12,8,128]{2,1,0:T(8,128)S(1)} %shard_map.111.own), channel_id=1, source_target_pairs={{0,192},{32,224},{64,128},{96,160},{128,64},{160,96},{192,0},{224,... | collective-permute-start | bytes 147464 | tf_op jit(solution)/shard_map/ppermute | solution.py:632
  36.7 0.0 collective-permute-start.7
  36.7 1.2 %shard_map.109 = (f32[256,128]{1,0:T(8,128)S(1)}, f32[256,128]{1,0:T(8,128)S(1)}) custom-call(f32[1024,128]{1,0:T(8,128)S(1)} %get-tuple-element.41.t, f32[1024,128]{1,0:T(8,128)S(1)} %get-tuple-element.42.s, f32[1024,128]{1,0:T(8,128)S(1)} %get-tuple-element.43.u, f32[1024,128]{1,0:T(8,128)S(1)} %get-tuple-element.44.v, ...), custom_call_target="tpu_custom_call" | custom-call | bytes 4194304 | tf_op jit(solution)/shard_map/pallas_call | solution.py:661
  37.9 1.2 %shard_map.108 = (f32[256,128]{1,0:T(8,128)S(1)}, f32[256,128]{1,0:T(8,128)S(1)}) custom-call(f32[1024,128]{1,0:T(8,128)S(1)} %get-tuple-element.41.t, f32[1024,128]{1,0:T(8,128)S(1)} %get-tuple-element.42.s, f32[1024,128]{1,0:T(8,128)S(1)} %get-tuple-element.43.u, f32[1024,128]{1,0:T(8,128)S(1)} %get-tuple-element.44.v, ...), custom_call_target="tpu_custom_call" | custom-call | bytes 4194304 | tf_op jit(solution)/shard_map/pallas_call | solution.py:661
  39.1 0.1 collective-permute-start.6
  39.2 0.0 collective-permute-done.8.chip_1
  39.2 1.1 %collective-permute-done.7.chip_0 = f32[12,8,128]{2,1,0:T(8,128)S(1)} collective-permute-done((f32[12,8,128]{2,1,0:T(8,128)S(1)}, f32[12,8,128]{2,1,0:T(8,128)S(1)}, u32[]{:S(2)}, u32[]{:S(2)}) %collective-permute-start.7) | collective-permute-done | bytes 49184 | tf_op jit(solution)/shard_map/ppermute | solution.py:632
  40.3 0.5 %collective-permute-start.9 = (f32[12,8,128]{2,1,0:T(8,128)S(1)}, f32[12,8,128]{2,1,0:T(8,128)S(1)}, u32[]{:S(2)}, u32[]{:S(2)}) collective-permute-start(f32[12,8,128]{2,1,0:T(8,128)S(1)} %shard_map.112), channel_id=1, source_target_pairs={{0,32},{32,0},{64,96},{96,64},{128,160},{160,128},{192,224},{224,1... | collective-permute-start | bytes 147464 | tf_op jit(solution)/shard_map/ppermute | solution.py:632
  40.8 1.4 %shard_map.110 = (f32[992,128]{1,0:T(8,128)}, f32[992,128]{1,0:T(8,128)}, f32[992,128]{1,0:T(8,128)}, f32[992,128]{1,0:T(8,128)}, f32[8,128]{1,0:T(8,128)S(1)}) custom-call(f32[1024,128]{1,0:T(8,128)S(1)} %get-tuple-element.58.u_next, f32[1024,128]{1,0:T(8,128)S(1)} %get-tuple-element.59.v_next, f32[256,128]{1,0:T(8,128)S(1)} %get-tuple-element.61.refs_0_.refs_3_, ...), custom_call_target="tpu_custom_call" | custom-call | bytes 4194304 | tf_op jit(solution)/shard_map/pallas_call | solution.py:661
  42.2 0.0 collective-permute-done.6.core
  42.2 0.0 collective-permute-done.9.passed
  42.2 4.2 %shard_map.113 = f32[16,128]{1,0:T(8,128)} custom-call(f32[12,8,128]{2,1,0:T(8,128)S(1)} %shard_map.111.own, f32[12,8,128]{2,1,0:T(8,128)S(1)} %collective-permute-done.6.core, f32[12,8,128]{2,1,0:T(8,128)S(1)} %collective-permute-done.7.chip_0, f32[12,8,128]{2,1,0:T(8,128)S(1)} %collective-permute-done.8.chip_1, ...), custom_call_target="tpu_custom_call" | custom-call | bytes 4194304 | tf_op jit(solution)/shard_map/pallas_call | solution.py:661
  (2 shorter events, 0.0 us)
Async XLA Ops:
  3.7 9.6 %collective-permute-start = (f32[9,8,128]{2,1,0:T(8,128)S(1)}, f32[9,8,128]{2,1,0:T(8,128)S(1)}, u32[]{:S(2)}, u32[]{:S(2)}) collective-permute-start(f32[9,8,128]{2,1,0:T(8,128)S(1)} %get-tuple-element.48), channel_id=1, source_target_pairs={{0,1},{1,0},{2,3},{3,2},{4,5},{5,4},{6,7},{7,6},{8,9},{9,8},{10,11... | collective-permute-start | bytes 110600 | tf_op jit(solution)/shard_map/ppermute | solution.py:632
  5.9 8.5 %collective-permute-start.1 = (f32[9,8,128]{2,1,0:T(8,128)S(1)}, f32[9,8,128]{2,1,0:T(8,128)S(1)}, u32[]{:S(2)}, u32[]{:S(2)}) collective-permute-start(f32[9,8,128]{2,1,0:T(8,128)S(1)} %get-tuple-element.49), channel_id=1, source_target_pairs={{0,31},{1,2},{2,1},{3,4},{4,3},{5,6},{6,5},{7,8},{8,7},{9,10},{10,... | collective-permute-start | bytes 110600 | tf_op jit(solution)/shard_map/ppermute | solution.py:632
  14.6 6.6 %collective-permute-start.2 = (f32[68,8,128]{2,1,0:T(8,128)S(1)}, f32[68,8,128]{2,1,0:T(8,128)S(1)}, u32[]{:S(2)}, u32[]{:S(2)}) collective-permute-start(f32[68,8,128]{2,1,0:T(8,128)S(1)} %get-tuple-element.52), channel_id=1, source_target_pairs={{0,32},{32,0},{64,96},{96,64},{128,160},{160,128},{192,224},{224,1... | collective-permute-start | bytes 835592 | tf_op jit(solution)/shard_map/ppermute | solution.py:632
  16.5 6.3 %collective-permute-start.3 = (f32[68,8,128]{2,1,0:T(8,128)S(1)}, f32[68,8,128]{2,1,0:T(8,128)S(1)}, u32[]{:S(2)}, u32[]{:S(2)}) collective-permute-start(f32[68,8,128]{2,1,0:T(8,128)S(1)} %get-tuple-element.53), channel_id=1, source_target_pairs={{0,224},{32,64},{64,32},{96,128},{128,96},{160,192},{192,160},{224... | collective-permute-start | bytes 835592 | tf_op jit(solution)/shard_map/ppermute | solution.py:632
  25.6 7.6 %collective-permute-start.4 = (f32[2,8,128]{2,1,0:T(8,128)S(1)}, f32[2,8,128]{2,1,0:T(8,128)S(1)}, u32[]{:S(2)}, u32[]{:S(2)}) collective-permute-start(f32[2,8,128]{2,1,0:T(8,128)S(1)} %get-tuple-element.74), channel_id=1, source_target_pairs={{0,1},{1,0},{2,3},{3,2},{4,5},{5,4},{6,7},{7,6},{8,9},{9,8},{10,11... | collective-permute-start | bytes 24584 | tf_op jit(solution)/shard_map/ppermute | solution.py:632
  25.7 7.5 %collective-permute-start.5 = (f32[2,8,128]{2,1,0:T(8,128)S(1)}, f32[2,8,128]{2,1,0:T(8,128)S(1)}, u32[]{:S(2)}, u32[]{:S(2)}) collective-permute-start(f32[2,8,128]{2,1,0:T(8,128)S(1)} %get-tuple-element.75), channel_id=1, source_target_pairs={{0,31},{1,2},{2,1},{3,4},{4,3},{5,6},{6,5},{7,8},{8,7},{9,10},{10,... | collective-permute-start | bytes 24584 | tf_op jit(solution)/shard_map/ppermute | solution.py:632
  33.3 6.0 %collective-permute-start.8 = (f32[12,8,128]{2,1,0:T(8,128)S(1)}, f32[12,8,128]{2,1,0:T(8,128)S(1)}, u32[]{:S(2)}, u32[]{:S(2)}) collective-permute-start(f32[12,8,128]{2,1,0:T(8,128)S(1)} %shard_map.111.own), channel_id=1, source_target_pairs={{0,192},{32,224},{64,128},{96,160},{128,64},{160,96},{192,0},{224,... | collective-permute-start | bytes 147464 | tf_op jit(solution)/shard_map/ppermute | solution.py:632
  36.7 3.6 %collective-permute-start.7 = (f32[12,8,128]{2,1,0:T(8,128)S(1)}, f32[12,8,128]{2,1,0:T(8,128)S(1)}, u32[]{:S(2)}, u32[]{:S(2)}) collective-permute-start(f32[12,8,128]{2,1,0:T(8,128)S(1)} %shard_map.111.own), channel_id=1, source_target_pairs={{0,64},{32,96},{64,0},{96,32},{128,192},{160,224},{192,128},{224,1... | collective-permute-start | bytes 147464 | tf_op jit(solution)/shard_map/ppermute | solution.py:632
  39.1 3.1 %collective-permute-start.6 = (f32[12,8,128]{2,1,0:T(8,128)S(1)}, f32[12,8,128]{2,1,0:T(8,128)S(1)}, u32[]{:S(2)}, u32[]{:S(2)}) collective-permute-start(f32[12,8,128]{2,1,0:T(8,128)S(1)} %shard_map.111.own), channel_id=1, source_target_pairs={{0,32},{32,0},{64,96},{96,64},{128,160},{160,128},{192,224},{224,1... | collective-permute-start | bytes 147464 | tf_op jit(solution)/shard_map/ppermute | solution.py:632
  40.3 1.9 %collective-permute-start.9 = (f32[12,8,128]{2,1,0:T(8,128)S(1)}, f32[12,8,128]{2,1,0:T(8,128)S(1)}, u32[]{:S(2)}, u32[]{:S(2)}) collective-permute-start(f32[12,8,128]{2,1,0:T(8,128)S(1)} %shard_map.112), channel_id=1, source_target_pairs={{0,32},{32,0},{64,96},{96,64},{128,160},{160,128},{192,224},{224,1... | collective-permute-start | bytes 147464 | tf_op jit(solution)/shard_map/ppermute | solution.py:632

commit v5 on v4

--- a/solution.py
+++ b/solution.py
@@ -26,7 +26,7 @@
 PADDED = GROUPS * GROUP * ROWS
 PARTS = 4
 PART = PADDED // PARTS
-LOADS = 2
+LOADS = 4
 HALO = 2 * 4 * GROUPS
 PACKS = 2 * GROUPS
 SIDE = GROUPS + 1
@@ -311,10 +311,14 @@
     return x
 
 
-def laplace_row(near, dep, level, wet, q, edges, pair, j):
-    count = (
+def wet_sides(dep, level, wet, j):
+    return (
         jnp.where(level < dep.tile(j, 1), 1.0, 0.0) + jnp.where(level < dep.tile(j, 2), 1.0, 0.0)
     ) + (jnp.where(wet[j + 1], 1.0, 0.0) + jnp.where(wet[j - 1], 1.0, 0.0))
+
+
+def laplace_row(near, dep, level, wet, q, edges, pair, j):
+    count = wet_sides(dep, level, wet, j)
     laps, sides = [], []
     for f in range(2):
         e, w = near.sideways(q[j][f], edges.edge(pair, j), f, min(max(j, 0), ROWS - 1))
@@ -325,7 +329,7 @@
 
 
 def momentum_levels(
-    near, dep, lat_total, windows, corners, t, s, u, v, u_next, v_next, sum_x, sum_y, sum_u, sum_v
+    near, dep, lat_total, windows, corners, t, s, u, v, write, kept, sum_x, sum_y, sum_u, sum_v
 ):
     sub = sublanes()
     zero = jnp.zeros(TILE, jnp.float32)
@@ -338,19 +342,28 @@
     first_row = (place()[0] * ROWS).astype(jnp.float32)
 
     def body(g, carry):
-        start = GROUP * ROWS * g
         level = (GROUP * g + sub).astype(jnp.float32)
         edges = Edges(near, g, level, (1,), corners)
         edge_load = turn(edges.ring[0], 64) - edges.ring[0]
         for first, last in windows:
             wet, q, lap, dens, count = {}, {}, {}, {}, {}
             for j in range(first - 2, last + 3):
-                wet[j] = level < dep.tile(j, 0)
-                q[j] = [masked(wet[j], near.level_row(ref, i, g, j)) for i, ref in ((2, u), (3, v))]
+                if not corners or j not in (3, ROWS - 4):
+                    wet[j] = level < dep.tile(j, 0)
+                    q[j] = [masked(wet[j], near.level_row(ref, i, g, j)) for i, ref in ((2, u), (3, v))]
                 if first - 1 <= j <= last + 1:
                     dens[j] = masked(wet[j], near.level_row(s, 1, g, j) - near.level_row(t, 0, g, j))
+                i = j - 1
                 if j >= first:
-                    lap[j - 1], _, count[j - 1] = laplace_row(near, dep, level, wet, q, edges, 1, j - 1)
+                    if corners and i in KEPT:
+                        lap[i] = [kept[KEPT.index(i) * 2 + f, g] for f in range(2)]
+                        if first <= i <= last:
+                            count[i] = wet_sides(dep, level, wet, i)
+                    else:
+                        lap[i], _, count[i] = laplace_row(near, dep, level, wet, q, edges, 1, i)
+                        if not corners and i in KEPT:
+                            for f in range(2):
+                                kept[KEPT.index(i) * 2 + f, g] = lap[i][f]
                 r = j - 2
                 if r < first:
                     continue
@@ -373,8 +386,7 @@
                 new_v = masked(
                     wet[r], q[r][1] - ((turning * q[r][0] + pull * grad_y) + mix * mixes[1])
                 )
-                u_next[pl.ds(start + r, GROUP, stride=ROWS), :] = new_u
-                v_next[pl.ds(start + r, GROUP, stride=ROWS), :] = new_v
+                write(g, r, new_u, new_v)
                 sum_u[r] += new_u
                 sum_v[r] += new_v
         return carry
@@ -392,32 +404,43 @@
 
 INNER = ((2, ROWS - 3),)
 OUTER = ((0, 1), (ROWS - 2, ROWS - 1))
+OUTER_ROWS = (0, 1, ROWS - 2, ROWS - 1)
+KEPT = (1, 2, ROWS - 3, ROWS - 2)
 
 
 def inner_kernel(
-    lat_total, t, s, u, v, depth, own, side_0, side_1, u_next, v_next, sums, inner,
+    lat_total, t, s, u, v, depth, own, side_0, side_1, u_next, v_next, sums, inner, kept,
     sum_x, sum_y, sum_u, sum_v,
 ):
     near, dep = Around(own, side_0, side_1), Depths(inner)
     dep.build_inner(near, depth)
+
+    def write(g, r, new_u, new_v):
+        rows = pl.ds(GROUP * ROWS * g + r, GROUP, stride=ROWS)
+        u_next[rows, :] = new_u
+        v_next[rows, :] = new_v
+
     momentum_levels(
-        near, dep, lat_total, INNER, False, t, s, u, v, u_next, v_next, sum_x, sum_y, sum_u, sum_v
+        near, dep, lat_total, INNER, False, t, s, u, v, write, kept, sum_x, sum_y, sum_u, sum_v
     )
     sums[...] = jnp.zeros(sums.shape, jnp.float32)
     write_sums(INNER, sum_u, sum_v, sums)
 
 
 def outer_kernel(
-    lat_total, t, s, u, v, depth, prior, own, side_0, side_1, swap_0, swap_1, u_inner, v_inner, sums, inner,
-    u_next, v_next, block, strip_0, strip_1, outer, sum_x, sum_y, sum_u, sum_v, total,
+    lat_total, t, s, u, v, depth, prior, own, side_0, side_1, swap_0, swap_1, sums, inner, kept,
+    u_outer, v_outer, block, strip_0, strip_1, outer, sum_x, sum_y, sum_u, sum_v, total,
 ):
     near, dep = Around(own, side_0, side_1, swap_0, swap_1), Depths(inner, outer)
     dep.build_outer(near)
-    u_next[...] = u_inner[...]
-    v_next[...] = v_inner[...]
     total[...] = sums[...]
+
+    def write(g, r, new_u, new_v):
+        u_outer[OUTER_ROWS.index(r), g] = new_u
+        v_outer[OUTER_ROWS.index(r), g] = new_v
+
     momentum_levels(
-        near, dep, lat_total, OUTER, True, t, s, u, v, u_next, v_next, sum_x, sum_y, sum_u, sum_v
+        near, dep, lat_total, OUTER, True, t, s, u, v, write, kept, sum_x, sum_y, sum_u, sum_v
     )
     write_sums(OUTER, sum_u, sum_v, total)
     quarter = lanes() // 32
@@ -434,6 +457,14 @@
             strips.append(strip)
         strip_0[half] = jnp.where(near.lon_even, strips[0], strips[1])
         strip_1[half] = jnp.where(near.lon_even, strips[1], strips[0])
+
+
+def merge_kernel(u_inner, v_inner, u_outer, v_outer, u_next, v_next):
+    for inner, outer, out in ((u_inner, u_outer, u_next), (v_inner, v_outer, v_next)):
+        out[...] = inner[...]
+        for g in range(GROUPS):
+            for i, r in enumerate(OUTER_ROWS):
+                out[pl.ds(GROUP * ROWS * g + r, GROUP, stride=ROWS), :] = outer[i, g]
 
 
 def tracer_kernel(
@@ -550,7 +581,7 @@
         return Plane(*[[turn(x[-1], 1, 0)] + x[:-1] for x in (self.own, self.rim)])
 
 
-def solve_kernel(levels, own, core, chip_0, chip_1, passed, stored, out, own_buf, rim_buf):
+def solve_kernel(levels, own, core, chip_0, chip_1, passed, stored, out, own_buf, rim_buf, terms, weights):
     del stored
     lat, _ = place()
     lat_even, lon_even = evens()
@@ -595,20 +626,37 @@
     east_face, north_face = depth_east * (1.0 / levels), depth_north * (1.0 / levels)
     west_face, south_face = east_face.west(), north_face.south()
     diagonal = (((east_face + west_face) + north_face) + south_face) + SURFACE_TERM
-    inverse = diagonal.map(1.0, lambda a, b: b / a)
-    right_side, east_face, west_face, north_face, south_face = [
-        x * inverse for x in (right_side, east_face, west_face, north_face, south_face)
-    ]
-    height, change = prior, None
-    scales, carries = chebyshev_weights(ITERATIONS)
-    for scale, carry in zip(scales, carries):
-        spread = (east_face * height.east() + west_face * height.west()) + (
-            north_face * height.north() + south_face * height.south()
+    root = diagonal.map(0.0, lambda a, b: jnp.sqrt(a))
+    inverse = root.map(1.0, lambda a, b: b / a)
+    scaled_side = right_side * inverse
+    east_face = east_face * inverse * inverse.east()
+    north_face = north_face * inverse * inverse.north()
+    for step, (scale, carry) in enumerate(zip(*chebyshev_weights(ITERATIONS))):
+        weights[step : step + 1, :] = jnp.full((1, COLS), scale, jnp.float32)
+        weights[ITERATIONS + step : ITERATIONS + step + 1, :] = jnp.full((1, COLS), carry, jnp.float32)
+    for i, plane in enumerate((scaled_side, east_face, north_face)):
+        for t in range(STEPS):
+            terms[2 * i, t] = plane.own[t]
+            terms[2 * i + 1, t] = plane.rim[t]
+
+    def body(step, state):
+        height, change = [Plane(list(x[:STEPS]), list(x[STEPS:])) for x in state]
+        side, east, north = [
+            Plane([terms[2 * i, t] for t in range(STEPS)], [terms[2 * i + 1, t] for t in range(STEPS)])
+            for i in range(3)
+        ]
+        spread = (east * height.east() + (east * height).west()) + (
+            north * height.north() + (north * height).south()
         )
-        residual = (right_side - height) + spread
-        step = residual * scale
-        change = step if change is None else step + change * carry
+        residual = (side - height) + spread
+        change = residual * row_of(weights, step) + change * row_of(weights, ITERATIONS + step)
         height = height + change
+        return tuple(tuple(x.own + x.rim) for x in (height, change))
+
+    start = prior * root
+    nothing = (jnp.zeros(TILE, jnp.float32),) * (2 * STEPS)
+    height, _ = lax.fori_loop(0, ITERATIONS, body, (tuple(start.own + start.rim), nothing))
+    height = Plane(list(height[:STEPS]), list(height[STEPS:])) * inverse
     height = height * ocean
     for t in range(STEPS):
         own_buf[pl.ds(t, GROUP, stride=STEPS), :] = height.own[t]
@@ -709,28 +757,29 @@
 
     scratch = [pltpu.VMEM((GROUP * ROWS, COLS), jnp.float32)] * 2
     scratch += [pltpu.VMEM((ROWS, *TILE), jnp.float32)] * 2
-    u_inner, v_inner, sums, inner = call(
+    u_inner, v_inner, sums, inner, kept_laps = call(
         functools.partial(inner_kernel, lat_total),
-        (padded, padded, tiles(4), tiles(3 * ROWS)),
+        (padded, padded, tiles(4), tiles(3 * ROWS), shape(2 * len(KEPT), GROUPS, *TILE)),
         scratch,
         *kept,
         depth,
         *sides,
     )
-    u_next, v_next, block, strip_0, strip_1, outer = call(
+    some_rows = shape(len(OUTER_ROWS), GROUPS, *TILE)
+    u_outer, v_outer, block, strip_0, strip_1, outer = call(
         functools.partial(outer_kernel, lat_total),
-        (padded, padded, tiles(BLOCK), tiles(STRIP), tiles(STRIP), tiles(12)),
+        (some_rows, some_rows, tiles(BLOCK), tiles(STRIP), tiles(STRIP), tiles(12)),
         scratch + [pltpu.VMEM((4, *TILE), jnp.float32)],
         *kept,
         depth,
         prior,
         *sides,
         *swaps,
-        u_inner,
-        v_inner,
         sums,
         inner,
-    )
+        kept_laps,
+    )
+    u_next, v_next = call(merge_kernel, (padded, padded), [], u_inner, v_inner, u_outer, v_outer)
     pieces = []
     for part in range(PARTS):
         pieces += call(
@@ -757,7 +806,7 @@
     )
     chip_0, chip_1 = swap(block, "lat", chip_even_first), swap(block, "lat", chip_odd_first)
     core = swap(block, "lat", even_first)
-    made = pieces[4:]
+    made = [*pieces[4:], u_next, v_next]
     passed = call(
         pass_kernel,
         tiles(BLOCK + 2 * STRIP),
@@ -780,7 +829,11 @@
     height = call(
         functools.partial(solve_kernel, levels),
         plane,
-        [pltpu.VMEM((5 * ROWS, COLS), jnp.float32)] * 2,
+        [pltpu.VMEM((5 * ROWS, COLS), jnp.float32)] * 2
+        + [
+            pltpu.VMEM((6, STEPS, *TILE), jnp.float32),
+            pltpu.VMEM((2 * ITERATIONS, COLS), jnp.float32),
+        ],
         block,
         core,
         chip_0,

time: 46.5 us -> 47.2 us (1.015)
  Pallas kernels: 20 us -> 20.9 us
    pallas_call x13 -> x14, Pallas kernels: 20 us -> 20.9 us  [call(): pl.pallas_call(kernel, out_shape=outs, in_specs=ins or [VMEM] * len(args)...]
where the time goes in v5:
time: 47.2 us; the launch traced here: 47.1 us
  starting transfers between devices  21.8 us (46%)
  Pallas kernels  20.9 us (44%)
  waiting for transfers between devices  3.59 us (8%)
  between operations  0.79 us (2%)
    ppermute x10, starting transfers between devices, swap(): lax.ppermute(value, axis, [(i, partner(i) % count) for i in range(count)])  21.8 us
    pallas_call x14, Pallas kernels, call(): pl.pallas_call(kernel, out_shape=outs, in_specs=ins or [VMEM] * len(args)...  20.9 us
    ppermute x10, waiting for transfers between devices, swap(): lax.ppermute(value, axis, [(i, partner(i) % count) for i in range(count)])  3.59 us
  transfers between devices with their start and end apart: 10, of which 3 were waited for; matrix products, arithmetic and copies ran while one was open for 0% of the time, Pallas kernels for 21%

profile of v5, /device:TPU:1, one launch (start us, length us, event | category | flops | bytes accessed | tf_op | source)
XLA Modules:
  0.0 47.1 jit_solution(5698293912761773489)
XLA Ops:
  0.6 3.1 %shard_map.101 = (f32[1024,128]{1,0:T(8,128)S(1)}, f32[1024,128]{1,0:T(8,128)S(1)}, f32[1024,128]{1,0:T(8,128)S(1)}, f32[1024,128]{1,0:T(8,128)S(1)}, f32[17,8,1...) custom-call(f32[992,128]{1,0:T(8,128)} %bitcast.8, ...), custom_call_target="tpu_custom_call" | custom-call | bytes 4194304 | tf_op jit(solution)/shard_map/pallas_call | solution.py:709
  3.8 2.2 %collective-permute-start = (f32[9,8,128]{2,1,0:T(8,128)S(1)}, f32[9,8,128]{2,1,0:T(8,128)S(1)}, u32[]{:S(2)}, u32[]{:S(2)}) collective-permute-start(f32[9,8,128]{2,1,0:T(8,128)S(1)} %get-tuple-element.50), channel_id=1, source_target_pairs={{0,1},{1,0},{2,3},{3,2},{4,5},{5,4},{6,7},{7,6},{8,9},{9,8},{10,11... | collective-permute-start | bytes 110600 | tf_op jit(solution)/shard_map/ppermute | solution.py:680
  6.0 7.2 %collective-permute-start.1 = (f32[9,8,128]{2,1,0:T(8,128)S(1)}, f32[9,8,128]{2,1,0:T(8,128)S(1)}, u32[]{:S(2)}, u32[]{:S(2)}) collective-permute-start(f32[9,8,128]{2,1,0:T(8,128)S(1)} %get-tuple-element.51), channel_id=1, source_target_pairs={{0,31},{1,2},{2,1},{3,4},{4,3},{5,6},{6,5},{7,8},{8,7},{9,10},{10,... | collective-permute-start | bytes 110600 | tf_op jit(solution)/shard_map/ppermute | solution.py:680
  13.2 0.2 shard_map.103
  13.4 0.0 collective-permute-done.side_0
  13.4 1.1 %collective-permute-done.1.side_1 = f32[9,8,128]{2,1,0:T(8,128)S(1)} collective-permute-done((f32[9,8,128]{2,1,0:T(8,128)S(1)}, f32[9,8,128]{2,1,0:T(8,128)S(1)}, u32[]{:S(2)}, u32[]{:S(2)}) %collective-permute-start.1) | collective-permute-done | bytes 36896 | tf_op jit(solution)/shard_map/ppermute | solution.py:680
  14.5 0.2 shard_map.104
  14.7 1.9 %collective-permute-start.2 = (f32[68,8,128]{2,1,0:T(8,128)S(1)}, f32[68,8,128]{2,1,0:T(8,128)S(1)}, u32[]{:S(2)}, u32[]{:S(2)}) collective-permute-start(f32[68,8,128]{2,1,0:T(8,128)S(1)} %get-tuple-element.57), channel_id=1, source_target_pairs={{0,32},{32,0},{64,96},{96,64},{128,160},{160,128},{192,224},{224,1... | collective-permute-start | bytes 835592 | tf_op jit(solution)/shard_map/ppermute | solution.py:680
  16.6 1.2 %collective-permute-start.3 = (f32[68,8,128]{2,1,0:T(8,128)S(1)}, f32[68,8,128]{2,1,0:T(8,128)S(1)}, u32[]{:S(2)}, u32[]{:S(2)}) collective-permute-start(f32[68,8,128]{2,1,0:T(8,128)S(1)} %get-tuple-element.58), channel_id=1, source_target_pairs={{0,224},{32,64},{64,32},{96,128},{128,96},{160,192},{192,160},{224... | collective-permute-start | bytes 835592 | tf_op jit(solution)/shard_map/ppermute | solution.py:680
  17.8 3.6 %shard_map.102 = (f32[1024,128]{1,0:T(8,128)S(1)}, f32[1024,128]{1,0:T(8,128)S(1)}, f32[4,8,128]{2,1,0:T(8,128)S(1)}, f32[48,8,128]{2,1,0:T(8,128)S(1)}, f32[8,8,8,128]{3,2,1,0:T(8,128)S(1)}) custom-call(f32[1024,128]{1,0:T(8,128)S(1)} %get-tuple-element.44.t, f32[1024,128]{1,0:T(8,128)S(1)} %get-tuple-element.45.s, f32[1024,128]{1,0:T(8,128)S(1)} %get-tuple-element.46.u, ...), custom_call_target="tpu_custom_call" | custom-call | bytes 4194304 | tf_op jit(solution)/shard_map/pallas_call | solution.py:709
  21.4 0.0 collective-permute-done.2.swap_0
  21.4 1.5 %collective-permute-done.3.swap_1 = f32[68,8,128]{2,1,0:T(8,128)S(1)} collective-permute-done((f32[68,8,128]{2,1,0:T(8,128)S(1)}, f32[68,8,128]{2,1,0:T(8,128)S(1)}, u32[]{:S(2)}, u32[]{:S(2)}) %collective-permute-start.3) | collective-permute-done | bytes 278560 | tf_op jit(solution)/shard_map/ppermute | solution.py:680
  22.9 2.9 %shard_map.105 = (f32[4,8,8,128]{3,2,1,0:T(8,128)S(1)}, f32[4,8,8,128]{3,2,1,0:T(8,128)S(1)}, f32[8,8,128]{2,1,0:T(8,128)S(1)}, f32[2,8,128]{2,1,0:T(8,128)S(1)}...) custom-call(f32[1024,128]{1,0:T(8,128)S(1)} %get-tuple-element.44.t, f32[1024,128]{1,0:T(8,128)S(1)} %get-tuple-element.45.s, ...), custom_call_target="tpu_custom_call" | custom-call | bytes 4194304 | tf_op jit(solution)/shard_map/pallas_call | solution.py:709
  25.8 0.1 collective-permute-start.4
  25.9 5.1 %collective-permute-start.5 = (f32[2,8,128]{2,1,0:T(8,128)S(1)}, f32[2,8,128]{2,1,0:T(8,128)S(1)}, u32[]{:S(2)}, u32[]{:S(2)}) collective-permute-start(f32[2,8,128]{2,1,0:T(8,128)S(1)} %get-tuple-element.81), channel_id=1, source_target_pairs={{0,31},{1,2},{2,1},{3,4},{4,3},{5,6},{6,5},{7,8},{8,7},{9,10},{10,... | collective-permute-start | bytes 24584 | tf_op jit(solution)/shard_map/ppermute | solution.py:680
  31.0 1.2 %shard_map.108 = (f32[256,128]{1,0:T(8,128)S(1)}, f32[256,128]{1,0:T(8,128)S(1)}) custom-call(f32[1024,128]{1,0:T(8,128)S(1)} %get-tuple-element.44.t, f32[1024,128]{1,0:T(8,128)S(1)} %get-tuple-element.45.s, f32[1024,128]{1,0:T(8,128)S(1)} %get-tuple-element.46.u, f32[1024,128]{1,0:T(8,128)S(1)} %get-tuple-element.47.v, ...), custom_call_target="tpu_custom_call" | custom-call | bytes 4194304 | tf_op jit(solution)/shard_map/pallas_call | solution.py:709
  32.2 1.2 %shard_map.107 = (f32[256,128]{1,0:T(8,128)S(1)}, f32[256,128]{1,0:T(8,128)S(1)}) custom-call(f32[1024,128]{1,0:T(8,128)S(1)} %get-tuple-element.44.t, f32[1024,128]{1,0:T(8,128)S(1)} %get-tuple-element.45.s, f32[1024,128]{1,0:T(8,128)S(1)} %get-tuple-element.46.u, f32[1024,128]{1,0:T(8,128)S(1)} %get-tuple-element.47.v, ...), custom_call_target="tpu_custom_call" | custom-call | bytes 4194304 | tf_op jit(solution)/shard_map/pallas_call | solution.py:709
  33.4 0.0 collective-permute-done.4.refs_1_
  33.4 0.0 collective-permute-done.5.refs_2_
  33.4 3.5 %collective-permute-start.8 = (f32[12,8,128]{2,1,0:T(8,128)S(1)}, f32[12,8,128]{2,1,0:T(8,128)S(1)}, u32[]{:S(2)}, u32[]{:S(2)}) collective-permute-start(f32[12,8,128]{2,1,0:T(8,128)S(1)} %shard_map.112.own), channel_id=1, source_target_pairs={{0,192},{32,224},{64,128},{96,160},{128,64},{160,96},{192,0},{224,... | collective-permute-start | bytes 147464 | tf_op jit(solution)/shard_map/ppermute | solution.py:680
  36.9 0.0 collective-permute-start.7
  36.9 0.1 shard_map.106
  37.0 1.2 %shard_map.110 = (f32[256,128]{1,0:T(8,128)S(1)}, f32[256,128]{1,0:T(8,128)S(1)}) custom-call(f32[1024,128]{1,0:T(8,128)S(1)} %get-tuple-element.44.t, f32[1024,128]{1,0:T(8,128)S(1)} %get-tuple-element.45.s, f32[1024,128]{1,0:T(8,128)S(1)} %get-tuple-element.46.u, f32[1024,128]{1,0:T(8,128)S(1)} %get-tuple-element.47.v, ...), custom_call_target="tpu_custom_call" | custom-call | bytes 4194304 | tf_op jit(solution)/shard_map/pallas_call | solution.py:709
  38.2 1.2 %shard_map.109 = (f32[256,128]{1,0:T(8,128)S(1)}, f32[256,128]{1,0:T(8,128)S(1)}) custom-call(f32[1024,128]{1,0:T(8,128)S(1)} %get-tuple-element.44.t, f32[1024,128]{1,0:T(8,128)S(1)} %get-tuple-element.45.s, f32[1024,128]{1,0:T(8,128)S(1)} %get-tuple-element.46.u, f32[1024,128]{1,0:T(8,128)S(1)} %get-tuple-element.47.v, ...), custom_call_target="tpu_custom_call" | custom-call | bytes 4194304 | tf_op jit(solution)/shard_map/pallas_call | solution.py:709
  39.4 0.1 collective-permute-start.6
  39.5 0.0 collective-permute-done.8.chip_1
  39.5 0.9 %collective-permute-done.7.chip_0 = f32[12,8,128]{2,1,0:T(8,128)S(1)} collective-permute-done((f32[12,8,128]{2,1,0:T(8,128)S(1)}, f32[12,8,128]{2,1,0:T(8,128)S(1)}, u32[]{:S(2)}, u32[]{:S(2)}) %collective-permute-start.7) | collective-permute-done | bytes 49184 | tf_op jit(solution)/shard_map/ppermute | solution.py:680
  40.5 0.5 %collective-permute-start.9 = (f32[12,8,128]{2,1,0:T(8,128)S(1)}, f32[12,8,128]{2,1,0:T(8,128)S(1)}, u32[]{:S(2)}, u32[]{:S(2)}) collective-permute-start(f32[12,8,128]{2,1,0:T(8,128)S(1)} %shard_map.113), channel_id=1, source_target_pairs={{0,32},{32,0},{64,96},{96,64},{128,160},{160,128},{192,224},{224,1... | collective-permute-start | bytes 147464 | tf_op jit(solution)/shard_map/ppermute | solution.py:680
  41.0 1.4 %shard_map.111 = (f32[992,128]{1,0:T(8,128)}, f32[992,128]{1,0:T(8,128)}, f32[992,128]{1,0:T(8,128)}, f32[992,128]{1,0:T(8,128)}, f32[8,128]{1,0:T(8,128)S(1)}) custom-call(f32[1024,128]{1,0:T(8,128)S(1)} %get-tuple-element.64.u_next.refs_4_, f32[1024,128]{1,0:T(8,128)S(1)} %get-tuple-element.65.v_next.refs_5_, ...), custom_call_target="tpu_custom_call" | custom-call | bytes 4194304 | tf_op jit(solution)/shard_map/pallas_call | solution.py:709
  42.3 0.0 collective-permute-done.6.core
  42.3 0.0 collective-permute-done.9.passed
  42.3 4.7 %shard_map.114 = f32[16,128]{1,0:T(8,128)} custom-call(f32[12,8,128]{2,1,0:T(8,128)S(1)} %shard_map.112.own, f32[12,8,128]{2,1,0:T(8,128)S(1)} %collective-permute-done.6.core, f32[12,8,128]{2,1,0:T(8,128)S(1)} %collective-permute-done.7.chip_0, f32[12,8,128]{2,1,0:T(8,128)S(1)} %collective-permute-done.8.chip_1, ...), custom_call_target="tpu_custom_call" | custom-call | bytes 4194304 | tf_op jit(solution)/shard_map/pallas_call | solution.py:709
  (2 shorter events, 0.0 us)
Async XLA Ops:
  3.8 9.6 %collective-permute-start = (f32[9,8,128]{2,1,0:T(8,128)S(1)}, f32[9,8,128]{2,1,0:T(8,128)S(1)}, u32[]{:S(2)}, u32[]{:S(2)}) collective-permute-start(f32[9,8,128]{2,1,0:T(8,128)S(1)} %get-tuple-element.50), channel_id=1, source_target_pairs={{0,1},{1,0},{2,3},{3,2},{4,5},{5,4},{6,7},{7,6},{8,9},{9,8},{10,11... | collective-permute-start | bytes 110600 | tf_op jit(solution)/shard_map/ppermute | solution.py:680
  6.0 8.5 %collective-permute-start.1 = (f32[9,8,128]{2,1,0:T(8,128)S(1)}, f32[9,8,128]{2,1,0:T(8,128)S(1)}, u32[]{:S(2)}, u32[]{:S(2)}) collective-permute-start(f32[9,8,128]{2,1,0:T(8,128)S(1)} %get-tuple-element.51), channel_id=1, source_target_pairs={{0,31},{1,2},{2,1},{3,4},{4,3},{5,6},{6,5},{7,8},{8,7},{9,10},{10,... | collective-permute-start | bytes 110600 | tf_op jit(solution)/shard_map/ppermute | solution.py:680
  14.7 6.7 %collective-permute-start.2 = (f32[68,8,128]{2,1,0:T(8,128)S(1)}, f32[68,8,128]{2,1,0:T(8,128)S(1)}, u32[]{:S(2)}, u32[]{:S(2)}) collective-permute-start(f32[68,8,128]{2,1,0:T(8,128)S(1)} %get-tuple-element.57), channel_id=1, source_target_pairs={{0,32},{32,0},{64,96},{96,64},{128,160},{160,128},{192,224},{224,1... | collective-permute-start | bytes 835592 | tf_op jit(solution)/shard_map/ppermute | solution.py:680
  16.6 6.3 %collective-permute-start.3 = (f32[68,8,128]{2,1,0:T(8,128)S(1)}, f32[68,8,128]{2,1,0:T(8,128)S(1)}, u32[]{:S(2)}, u32[]{:S(2)}) collective-permute-start(f32[68,8,128]{2,1,0:T(8,128)S(1)} %get-tuple-element.58), channel_id=1, source_target_pairs={{0,224},{32,64},{64,32},{96,128},{128,96},{160,192},{192,160},{224... | collective-permute-start | bytes 835592 | tf_op jit(solution)/shard_map/ppermute | solution.py:680
  25.8 7.6 %collective-permute-start.4 = (f32[2,8,128]{2,1,0:T(8,128)S(1)}, f32[2,8,128]{2,1,0:T(8,128)S(1)}, u32[]{:S(2)}, u32[]{:S(2)}) collective-permute-start(f32[2,8,128]{2,1,0:T(8,128)S(1)} %get-tuple-element.80), channel_id=1, source_target_pairs={{0,1},{1,0},{2,3},{3,2},{4,5},{5,4},{6,7},{7,6},{8,9},{9,8},{10,11... | collective-permute-start | bytes 24584 | tf_op jit(solution)/shard_map/ppermute | solution.py:680
  25.9 7.5 %collective-permute-start.5 = (f32[2,8,128]{2,1,0:T(8,128)S(1)}, f32[2,8,128]{2,1,0:T(8,128)S(1)}, u32[]{:S(2)}, u32[]{:S(2)}) collective-permute-start(f32[2,8,128]{2,1,0:T(8,128)S(1)} %get-tuple-element.81), channel_id=1, source_target_pairs={{0,31},{1,2},{2,1},{3,4},{4,3},{5,6},{6,5},{7,8},{8,7},{9,10},{10,... | collective-permute-start | bytes 24584 | tf_op jit(solution)/shard_map/ppermute | solution.py:680
  33.4 6.1 %collective-permute-start.8 = (f32[12,8,128]{2,1,0:T(8,128)S(1)}, f32[12,8,128]{2,1,0:T(8,128)S(1)}, u32[]{:S(2)}, u32[]{:S(2)}) collective-permute-start(f32[12,8,128]{2,1,0:T(8,128)S(1)} %shard_map.112.own), channel_id=1, source_target_pairs={{0,192},{32,224},{64,128},{96,160},{128,64},{160,96},{192,0},{224,... | collective-permute-start | bytes 147464 | tf_op jit(solution)/shard_map/ppermute | solution.py:680
  36.9 3.6 %collective-permute-start.7 = (f32[12,8,128]{2,1,0:T(8,128)S(1)}, f32[12,8,128]{2,1,0:T(8,128)S(1)}, u32[]{:S(2)}, u32[]{:S(2)}) collective-permute-start(f32[12,8,128]{2,1,0:T(8,128)S(1)} %shard_map.112.own), channel_id=1, source_target_pairs={{0,64},{32,96},{64,0},{96,32},{128,192},{160,224},{192,128},{224,1... | collective-permute-start | bytes 147464 | tf_op jit(solution)/shard_map/ppermute | solution.py:680
  39.4 2.9 %collective-permute-start.6 = (f32[12,8,128]{2,1,0:T(8,128)S(1)}, f32[12,8,128]{2,1,0:T(8,128)S(1)}, u32[]{:S(2)}, u32[]{:S(2)}) collective-permute-start(f32[12,8,128]{2,1,0:T(8,128)S(1)} %shard_map.112.own), channel_id=1, source_target_pairs={{0,32},{32,0},{64,96},{96,64},{128,160},{160,128},{192,224},{224,1... | collective-permute-start | bytes 147464 | tf_op jit(solution)/shard_map/ppermute | solution.py:680
  40.5 1.9 %collective-permute-start.9 = (f32[12,8,128]{2,1,0:T(8,128)S(1)}, f32[12,8,128]{2,1,0:T(8,128)S(1)}, u32[]{:S(2)}, u32[]{:S(2)}) collective-permute-start(f32[12,8,128]{2,1,0:T(8,128)S(1)} %shard_map.113), channel_id=1, source_target_pairs={{0,32},{32,0},{64,96},{96,64},{128,160},{160,128},{192,224},{224,1... | collective-permute-start | bytes 147464 | tf_op jit(solution)/shard_map/ppermute | solution.py:680

commit v6 on v5

--- a/solution.py
+++ b/solution.py
@@ -30,7 +30,7 @@
 HALO = 2 * 4 * GROUPS
 PACKS = 2 * GROUPS
 SIDE = GROUPS + 1
-ROWS_OUT = HALO + 4
+CORNER = 2
 BLOCK = 8
 STRIP = 2
 
@@ -137,7 +137,8 @@
     for part in range(LOADS):
         for copy in copies[4 * part : 4 * part + 4]:
             copy.wait()
-        lax.fori_loop(GROUPS // LOADS * part, GROUPS // LOADS * (part + 1), body, 0)
+        for g in range(GROUPS // LOADS * part, GROUPS // LOADS * (part + 1)):
+            body(g, 0)
 
 
 def rows_kernel(t, s, u, v, depth, swap_0, swap_1):
@@ -162,7 +163,7 @@
 
 
 class Around:
-    def __init__(self, own, side_0, side_1, swap_0=None, swap_1=None):
+    def __init__(self, own, side_0, side_1, swap_0=None, swap_1=None, corner_0=None, corner_1=None):
         lat, _ = place()
         self.lat_even, self.lon_even = evens()
         self.first, self.final = lat == 0, lat == lax.axis_size("lat") - 1
@@ -170,6 +171,7 @@
         self.lane, self.column, self.row = lane, lane & 3, (lane // 4) & 15
         self.low, self.column_2 = self.column < 2, self.column == 2
         self.own, self.sides, self.swaps = own, (side_0, side_1), (swap_0, swap_1)
+        self.corners = corner_0, corner_1
 
     def beside(self, tile):
         a, b = self.sides[0][tile], self.sides[1][tile]
@@ -177,6 +179,10 @@
 
     def beyond(self, north, index):
         a, b = self.swaps if north else self.swaps[::-1]
+        return jnp.where(self.lat_even, a[index], b[index])
+
+    def cornered(self, north, index):
+        a, b = self.corners if north else self.corners[::-1]
         return jnp.where(self.lat_even, a[index], b[index])
 
     def columns(self, pair, g):
@@ -193,13 +199,13 @@
 
     def corner(self, pair, g):
         at = 4 * (g + GROUPS * pair)
-        south = pltpu.roll(self.beyond(False, HALO + 2), (COLS - at) % COLS, 1)
-        north = pltpu.roll(self.beyond(True, HALO + 2), (COLS + 60 - at) % COLS, 1)
+        south = pltpu.roll(self.cornered(False, 0), (COLS - at) % COLS, 1)
+        north = pltpu.roll(self.cornered(True, 0), (COLS + 60 - at) % COLS, 1)
         return jnp.where(self.row == 0, south, north)
 
     def corner_depth(self):
-        south = jnp.where(self.first, 0.0, self.beyond(False, HALO + 3))
-        north = jnp.where(self.final, 0.0, self.beyond(True, HALO + 3))
+        south = jnp.where(self.first, 0.0, self.cornered(False, 1))
+        north = jnp.where(self.final, 0.0, self.cornered(True, 1))
         return jnp.where(self.row == 0, south, north)
 
     def row_depth(self, j):
@@ -229,14 +235,10 @@
         return east, west
 
 
-def corner_kernel(rows_0, rows_1, own, side_0, side_1, swap_0, swap_1):
+def corner_kernel(own, side_0, side_1, corner_0, corner_1):
     near = Around(own, side_0, side_1)
     slot = near.row
-    for swap, rows, upper in (
-        (swap_0, rows_0, near.lat_even),
-        (swap_1, rows_1, jnp.logical_not(near.lat_even)),
-    ):
-        swap[: HALO + 2] = rows[...]
+    for corner, upper in ((corner_0, near.lat_even), (corner_1, jnp.logical_not(near.lat_even))):
         from_row = jnp.where(upper, 4 * (ROWS - 1), 0)
         tile = jnp.zeros(TILE, jnp.float32)
         for pair in range(2):
@@ -245,10 +247,10 @@
                 at = g + GROUPS * pair
                 moved = pltpu.roll(jnp.where(near.low, west, east), (4 * at + COLS - from_row) % COLS, 1)
                 tile = jnp.where(slot == at, moved, tile)
-        swap[HALO + 2] = tile
+        corner[0] = tile
         west, east = near.depth_columns()
         shift = jnp.where(upper, COLS - 60, 60)
-        swap[HALO + 3] = pltpu.roll(jnp.where(near.low, west, east), shift, 1)
+        corner[1] = pltpu.roll(jnp.where(near.low, west, east), shift, 1)
 
 
 class Depths:
@@ -391,7 +393,7 @@
                 sum_v[r] += new_v
         return carry
 
-    lax.fori_loop(0, GROUPS, body, 0)
+    lax.fori_loop(0, GROUPS, body, 0, unroll=4 if corners else 2)
 
 
 def write_sums(windows, sum_u, sum_v, block):
@@ -428,10 +430,11 @@
 
 
 def outer_kernel(
-    lat_total, t, s, u, v, depth, prior, own, side_0, side_1, swap_0, swap_1, sums, inner, kept,
-    u_outer, v_outer, block, strip_0, strip_1, outer, sum_x, sum_y, sum_u, sum_v, total,
+    lat_total, t, s, u, v, depth, prior, own, side_0, side_1, swap_0, swap_1, corner_0, corner_1,
+    sums, inner, kept, u_outer, v_outer, block, strip_0, strip_1, outer, sum_x, sum_y, sum_u, sum_v, total,
 ):
-    near, dep = Around(own, side_0, side_1, swap_0, swap_1), Depths(inner, outer)
+    near = Around(own, side_0, side_1, swap_0, swap_1, corner_0, corner_1)
+    dep = Depths(inner, outer)
     dep.build_outer(near)
     total[...] = sums[...]
 
@@ -468,9 +471,10 @@
 
 
 def tracer_kernel(
-    part, t, s, u, v, own, side_0, side_1, swap_0, swap_1, inner, outer, t_next, s_next
+    part, t, s, u, v, own, side_0, side_1, swap_0, swap_1, corner_0, corner_1, inner, outer, t_next, s_next
 ):
-    near, dep = Around(own, side_0, side_1, swap_0, swap_1), Depths(inner, outer)
+    near = Around(own, side_0, side_1, swap_0, swap_1, corner_0, corner_1)
+    dep = Depths(inner, outer)
     sub = sublanes()
 
     def body(g, carry):
@@ -581,7 +585,7 @@
         return Plane(*[[turn(x[-1], 1, 0)] + x[:-1] for x in (self.own, self.rim)])
 
 
-def solve_kernel(levels, own, core, chip_0, chip_1, passed, stored, out, own_buf, rim_buf, terms, weights):
+def solve_kernel(levels, own, core, chip_0, chip_1, passed, stored, out, own_buf, rim_buf):
     del stored
     lat, _ = place()
     lat_even, lon_even = evens()
@@ -626,37 +630,20 @@
     east_face, north_face = depth_east * (1.0 / levels), depth_north * (1.0 / levels)
     west_face, south_face = east_face.west(), north_face.south()
     diagonal = (((east_face + west_face) + north_face) + south_face) + SURFACE_TERM
-    root = diagonal.map(0.0, lambda a, b: jnp.sqrt(a))
-    inverse = root.map(1.0, lambda a, b: b / a)
-    scaled_side = right_side * inverse
-    east_face = east_face * inverse * inverse.east()
-    north_face = north_face * inverse * inverse.north()
-    for step, (scale, carry) in enumerate(zip(*chebyshev_weights(ITERATIONS))):
-        weights[step : step + 1, :] = jnp.full((1, COLS), scale, jnp.float32)
-        weights[ITERATIONS + step : ITERATIONS + step + 1, :] = jnp.full((1, COLS), carry, jnp.float32)
-    for i, plane in enumerate((scaled_side, east_face, north_face)):
-        for t in range(STEPS):
-            terms[2 * i, t] = plane.own[t]
-            terms[2 * i + 1, t] = plane.rim[t]
-
-    def body(step, state):
-        height, change = [Plane(list(x[:STEPS]), list(x[STEPS:])) for x in state]
-        side, east, north = [
-            Plane([terms[2 * i, t] for t in range(STEPS)], [terms[2 * i + 1, t] for t in range(STEPS)])
-            for i in range(3)
-        ]
-        spread = (east * height.east() + (east * height).west()) + (
-            north * height.north() + (north * height).south()
+    inverse = diagonal.map(1.0, lambda a, b: b / a)
+    right_side, east_face, west_face, north_face, south_face = [
+        x * inverse for x in (right_side, east_face, west_face, north_face, south_face)
+    ]
+    height, change = prior, None
+    scales, carries = chebyshev_weights(ITERATIONS)
+    for scale, carry in zip(scales, carries):
+        spread = (east_face * height.east() + west_face * height.west()) + (
+            north_face * height.north() + south_face * height.south()
         )
-        residual = (side - height) + spread
-        change = residual * row_of(weights, step) + change * row_of(weights, ITERATIONS + step)
+        residual = (right_side - height) + spread
+        step = residual * scale
+        change = step if change is None else step + change * carry
         height = height + change
-        return tuple(tuple(x.own + x.rim) for x in (height, change))
-
-    start = prior * root
-    nothing = (jnp.zeros(TILE, jnp.float32),) * (2 * STEPS)
-    height, _ = lax.fori_loop(0, ITERATIONS, body, (tuple(start.own + start.rim), nothing))
-    height = Plane(list(height[:STEPS]), list(height[STEPS:])) * inverse
     height = height * ocean
     for t in range(STEPS):
         own_buf[pl.ds(t, GROUP, stride=STEPS), :] = height.own[t]
@@ -752,8 +739,9 @@
     )
     sides = (own, swap(to_0, "lon", even_first), swap(to_1, "lon", odd_first))
     rows_0, rows_1 = call(rows_kernel, (tiles(HALO + 2),) * 2, [], *kept, depth)
-    to_0, to_1 = call(corner_kernel, (tiles(ROWS_OUT),) * 2, [], rows_0, rows_1, *sides)
-    swaps = (swap(to_0, "lat", even_first), swap(to_1, "lat", odd_first))
+    swaps = (swap(rows_0, "lat", even_first), swap(rows_1, "lat", odd_first))
+    to_0, to_1 = call(corner_kernel, (tiles(CORNER),) * 2, [], *sides)
+    swaps += (swap(to_0, "lat", even_first), swap(to_1, "lat", odd_first))
 
     scratch = [pltpu.VMEM((GROUP * ROWS, COLS), jnp.float32)] * 2
     scratch += [pltpu.VMEM((ROWS, *TILE), jnp.float32)] * 2
@@ -829,11 +817,7 @@
     height = call(
         functools.partial(solve_kernel, levels),
         plane,
-        [pltpu.VMEM((5 * ROWS, COLS), jnp.float32)] * 2
-        + [
-            pltpu.VMEM((6, STEPS, *TILE), jnp.float32),
-            pltpu.VMEM((2 * ITERATIONS, COLS), jnp.float32),
-        ],
+        [pltpu.VMEM((5 * ROWS, COLS), jnp.float32)] * 2,
         block,
         core,
         chip_0,

time: 47.2 us -> 45.7 us (0.968)
  waiting for transfers between devices: 3.59 us -> 2.06 us
  starting transfers between devices: 21.8 us -> 23.1 us
  Pallas kernels: 20.9 us -> 19.7 us
    ppermute x10 -> x12, waiting for transfers between devices: 3.59 us -> 2.06 us  [swap(): lax.ppermute(value, axis, [(i, partner(i) % count) for i in range(count)])]
    ppermute x10 -> x12, starting transfers between devices: 21.8 us -> 23.1 us  [swap(): lax.ppermute(value, axis, [(i, partner(i) % count) for i in range(count)])]
    pallas_call x14, Pallas kernels: 20.9 us -> 19.7 us  [call(): pl.pallas_call(kernel, out_shape=outs, in_specs=ins or [VMEM] * len(args)...]
  transfers between devices with their start and end apart: 10 -> 12, of which waited for: 3 -> 2; matrix products, arithmetic and copies ran while one was open for 0% -> 0% of each run, Pallas kernels for 21% -> 23%
where the time goes in v6:
time: 45.7 us; the launch traced here: 45.6 us
  starting transfers between devices  23.1 us (51%)
  Pallas kernels  19.7 us (43%)
  waiting for transfers between devices  2.06 us (5%)
  between operations  0.81 us (2%)
    ppermute x12, starting transfers between devices, swap(): lax.ppermute(value, axis, [(i, partner(i) % count) for i in range(count)])  23.1 us
    pallas_call x14, Pallas kernels, call(): pl.pallas_call(kernel, out_shape=outs, in_specs=ins or [VMEM] * len(args)...  19.7 us
    ppermute x12, waiting for transfers between devices, swap(): lax.ppermute(value, axis, [(i, partner(i) % count) for i in range(count)])  2.06 us
  transfers between devices with their start and end apart: 12, of which 2 were waited for; matrix products, arithmetic and copies ran while one was open for 0% of the time, Pallas kernels for 23%

profile of v6, /device:TPU:1, one launch (start us, length us, event | category | flops | bytes accessed | tf_op | source)
XLA Modules:
  0.0 45.6 jit_solution(14680037148672387568)
XLA Ops:
  0.6 2.7 %shard_map.101 = (f32[1024,128]{1,0:T(8,128)S(1)}, f32[1024,128]{1,0:T(8,128)S(1)}, f32[1024,128]{1,0:T(8,128)S(1)}, f32[1024,128]{1,0:T(8,128)S(1)}, f32[17,8,1...) custom-call(f32[992,128]{1,0:T(8,128)} %bitcast.8, ...), custom_call_target="tpu_custom_call" | custom-call | bytes 4194304 | tf_op jit(solution)/shard_map/pallas_call | solution.py:696
  3.3 0.2 shard_map.103
  3.6 3.3 %collective-permute-start.2 = (f32[66,8,128]{2,1,0:T(8,128)S(1)}, f32[66,8,128]{2,1,0:T(8,128)S(1)}, u32[]{:S(2)}, u32[]{:S(2)}) collective-permute-start(f32[66,8,128]{2,1,0:T(8,128)S(1)} %get-tuple-element.55), channel_id=1, source_target_pairs={{0,32},{32,0},{64,96},{96,64},{128,160},{160,128},{192,224},{224,1... | collective-permute-start | bytes 811016 | tf_op jit(solution)/shard_map/ppermute | solution.py:667
  6.9 0.0 collective-permute-start.3
  6.9 0.8 %collective-permute-start = (f32[9,8,128]{2,1,0:T(8,128)S(1)}, f32[9,8,128]{2,1,0:T(8,128)S(1)}, u32[]{:S(2)}, u32[]{:S(2)}) collective-permute-start(f32[9,8,128]{2,1,0:T(8,128)S(1)} %get-tuple-element.50), channel_id=1, source_target_pairs={{0,1},{1,0},{2,3},{3,2},{4,5},{5,4},{6,7},{7,6},{8,9},{9,8},{10,11... | collective-permute-start | bytes 110600 | tf_op jit(solution)/shard_map/ppermute | solution.py:667
  7.7 7.2 %collective-permute-start.1 = (f32[9,8,128]{2,1,0:T(8,128)S(1)}, f32[9,8,128]{2,1,0:T(8,128)S(1)}, u32[]{:S(2)}, u32[]{:S(2)}) collective-permute-start(f32[9,8,128]{2,1,0:T(8,128)S(1)} %get-tuple-element.51), channel_id=1, source_target_pairs={{0,31},{1,2},{2,1},{3,4},{4,3},{5,6},{6,5},{7,8},{8,7},{9,10},{10,... | collective-permute-start | bytes 110600 | tf_op jit(solution)/shard_map/ppermute | solution.py:667
  14.8 0.0 collective-permute-done.side_0
  14.8 1.3 %collective-permute-done.1.side_1 = f32[9,8,128]{2,1,0:T(8,128)S(1)} collective-permute-done((f32[9,8,128]{2,1,0:T(8,128)S(1)}, f32[9,8,128]{2,1,0:T(8,128)S(1)}, u32[]{:S(2)}, u32[]{:S(2)}) %collective-permute-start.1) | collective-permute-done | bytes 36896 | tf_op jit(solution)/shard_map/ppermute | solution.py:667
  16.2 0.2 shard_map.104
  16.4 2.9 %collective-permute-start.4 = (f32[2,8,128]{2,1,0:T(8,128)S(1)}, f32[2,8,128]{2,1,0:T(8,128)S(1)}, u32[]{:S(2)}, u32[]{:S(2)}) collective-permute-start(f32[2,8,128]{2,1,0:T(8,128)S(1)} %get-tuple-element.57), channel_id=1, source_target_pairs={{0,32},{32,0},{64,96},{96,64},{128,160},{160,128},{192,224},{224,1... | collective-permute-start | bytes 24584 | tf_op jit(solution)/shard_map/ppermute | solution.py:667
  19.3 0.0 collective-permute-start.5
  19.3 4.3 %shard_map.102 = (f32[1024,128]{1,0:T(8,128)S(1)}, f32[1024,128]{1,0:T(8,128)S(1)}, f32[4,8,128]{2,1,0:T(8,128)S(1)}, f32[48,8,128]{2,1,0:T(8,128)S(1)}, f32[8,8,8,128]{3,2,1,0:T(8,128)S(1)}) custom-call(f32[1024,128]{1,0:T(8,128)S(1)} %get-tuple-element.44.t, f32[1024,128]{1,0:T(8,128)S(1)} %get-tuple-element.45.s, f32[1024,128]{1,0:T(8,128)S(1)} %get-tuple-element.46.u, ...), custom_call_target="tpu_custom_call" | custom-call | bytes 4194304 | tf_op jit(solution)/shard_map/pallas_call | solution.py:696
  23.5 0.0 collective-permute-done.4.corner_0
  23.5 0.0 collective-permute-done.5.corner_1
  23.6 0.0 collective-permute-done.2.swap_0
  23.6 1.9 %shard_map.105 = (f32[4,8,8,128]{3,2,1,0:T(8,128)S(1)}, f32[4,8,8,128]{3,2,1,0:T(8,128)S(1)}, f32[8,8,128]{2,1,0:T(8,128)S(1)}, f32[2,8,128]{2,1,0:T(8,128)S(1)}...) custom-call(f32[1024,128]{1,0:T(8,128)S(1)} %get-tuple-element.44.t, f32[1024,128]{1,0:T(8,128)S(1)} %get-tuple-element.45.s, ...), custom_call_target="tpu_custom_call" | custom-call | bytes 4194304 | tf_op jit(solution)/shard_map/pallas_call | solution.py:696
  25.5 0.1 collective-permute-start.6
  25.6 5.1 %collective-permute-start.7 = (f32[2,8,128]{2,1,0:T(8,128)S(1)}, f32[2,8,128]{2,1,0:T(8,128)S(1)}, u32[]{:S(2)}, u32[]{:S(2)}) collective-permute-start(f32[2,8,128]{2,1,0:T(8,128)S(1)} %get-tuple-element.81), channel_id=1, source_target_pairs={{0,31},{1,2},{2,1},{3,4},{4,3},{5,6},{6,5},{7,8},{8,7},{9,10},{10,... | collective-permute-start | bytes 24584 | tf_op jit(solution)/shard_map/ppermute | solution.py:667
  30.7 1.2 %shard_map.108 = (f32[256,128]{1,0:T(8,128)S(1)}, f32[256,128]{1,0:T(8,128)S(1)}) custom-call(f32[1024,128]{1,0:T(8,128)S(1)} %get-tuple-element.44.t, f32[1024,128]{1,0:T(8,128)S(1)} %get-tuple-element.45.s, f32[1024,128]{1,0:T(8,128)S(1)} %get-tuple-element.46.u, f32[1024,128]{1,0:T(8,128)S(1)} %get-tuple-element.47.v, ...), custom_call_target="tpu_custom_call" | custom-call | bytes 4194304 | tf_op jit(solution)/shard_map/pallas_call | solution.py:696
  31.9 1.2 %shard_map.107 = (f32[256,128]{1,0:T(8,128)S(1)}, f32[256,128]{1,0:T(8,128)S(1)}) custom-call(f32[1024,128]{1,0:T(8,128)S(1)} %get-tuple-element.44.t, f32[1024,128]{1,0:T(8,128)S(1)} %get-tuple-element.45.s, f32[1024,128]{1,0:T(8,128)S(1)} %get-tuple-element.46.u, f32[1024,128]{1,0:T(8,128)S(1)} %get-tuple-element.47.v, ...), custom_call_target="tpu_custom_call" | custom-call | bytes 4194304 | tf_op jit(solution)/shard_map/pallas_call | solution.py:696
  33.1 0.0 collective-permute-done.7.refs_2_
  33.1 2.7 %collective-permute-start.10 = (f32[12,8,128]{2,1,0:T(8,128)S(1)}, f32[12,8,128]{2,1,0:T(8,128)S(1)}, u32[]{:S(2)}, u32[]{:S(2)}) collective-permute-start(f32[12,8,128]{2,1,0:T(8,128)S(1)} %shard_map.112.own), channel_id=1, source_target_pairs={{0,192},{32,224},{64,128},{96,160},{128,64},{160,96},{192,0},{224,... | collective-permute-start | bytes 147464 | tf_op jit(solution)/shard_map/ppermute | solution.py:667
  35.9 0.0 collective-permute-start.9
  35.9 0.1 shard_map.106
  36.0 1.2 %shard_map.110 = (f32[256,128]{1,0:T(8,128)S(1)}, f32[256,128]{1,0:T(8,128)S(1)}) custom-call(f32[1024,128]{1,0:T(8,128)S(1)} %get-tuple-element.44.t, f32[1024,128]{1,0:T(8,128)S(1)} %get-tuple-element.45.s, f32[1024,128]{1,0:T(8,128)S(1)} %get-tuple-element.46.u, f32[1024,128]{1,0:T(8,128)S(1)} %get-tuple-element.47.v, ...), custom_call_target="tpu_custom_call" | custom-call | bytes 4194304 | tf_op jit(solution)/shard_map/pallas_call | solution.py:696
  37.2 1.2 %shard_map.109 = (f32[256,128]{1,0:T(8,128)S(1)}, f32[256,128]{1,0:T(8,128)S(1)}) custom-call(f32[1024,128]{1,0:T(8,128)S(1)} %get-tuple-element.44.t, f32[1024,128]{1,0:T(8,128)S(1)} %get-tuple-element.45.s, f32[1024,128]{1,0:T(8,128)S(1)} %get-tuple-element.46.u, f32[1024,128]{1,0:T(8,128)S(1)} %get-tuple-element.47.v, ...), custom_call_target="tpu_custom_call" | custom-call | bytes 4194304 | tf_op jit(solution)/shard_map/pallas_call | solution.py:696
  38.4 0.1 collective-permute-start.8
  38.5 0.7 %collective-permute-done.9.chip_0 = f32[12,8,128]{2,1,0:T(8,128)S(1)} collective-permute-done((f32[12,8,128]{2,1,0:T(8,128)S(1)}, f32[12,8,128]{2,1,0:T(8,128)S(1)}, u32[]{:S(2)}, u32[]{:S(2)}) %collective-permute-start.9) | collective-permute-done | bytes 49184 | tf_op jit(solution)/shard_map/ppermute | solution.py:667
  39.2 0.8 %collective-permute-start.11 = (f32[12,8,128]{2,1,0:T(8,128)S(1)}, f32[12,8,128]{2,1,0:T(8,128)S(1)}, u32[]{:S(2)}, u32[]{:S(2)}) collective-permute-start(f32[12,8,128]{2,1,0:T(8,128)S(1)} %shard_map.113), channel_id=1, source_target_pairs={{0,32},{32,0},{64,96},{96,64},{128,160},{160,128},{192,224},{224,1... | collective-permute-start | bytes 147464 | tf_op jit(solution)/shard_map/ppermute | solution.py:667
  40.0 1.4 %shard_map.111 = (f32[992,128]{1,0:T(8,128)}, f32[992,128]{1,0:T(8,128)}, f32[992,128]{1,0:T(8,128)}, f32[992,128]{1,0:T(8,128)}, f32[8,128]{1,0:T(8,128)S(1)}) custom-call(f32[1024,128]{1,0:T(8,128)S(1)} %get-tuple-element.64.u_next.refs_4_, f32[1024,128]{1,0:T(8,128)S(1)} %get-tuple-element.65.v_next.refs_5_, ...), custom_call_target="tpu_custom_call" | custom-call | bytes 4194304 | tf_op jit(solution)/shard_map/pallas_call | solution.py:696
  41.4 0.0 collective-permute-done.11.passed
  41.4 4.2 %shard_map.114 = f32[16,128]{1,0:T(8,128)} custom-call(f32[12,8,128]{2,1,0:T(8,128)S(1)} %shard_map.112.own, f32[12,8,128]{2,1,0:T(8,128)S(1)} %collective-permute-done.8.core, f32[12,8,128]{2,1,0:T(8,128)S(1)} %collective-permute-done.9.chip_0, f32[12,8,128]{2,1,0:T(8,128)S(1)} %collective-permute-done.10.chip_1, ...), custom_call_target="tpu_custom_call" | custom-call | bytes 4194304 | tf_op jit(solution)/shard_map/pallas_call | solution.py:696
  (6 shorter events, 0.0 us)
Async XLA Ops:
  3.6 20.0 %collective-permute-start.2 = (f32[66,8,128]{2,1,0:T(8,128)S(1)}, f32[66,8,128]{2,1,0:T(8,128)S(1)}, u32[]{:S(2)}, u32[]{:S(2)}) collective-permute-start(f32[66,8,128]{2,1,0:T(8,128)S(1)} %get-tuple-element.55), channel_id=1, source_target_pairs={{0,32},{32,0},{64,96},{96,64},{128,160},{160,128},{192,224},{224,1... | collective-permute-start | bytes 811016 | tf_op jit(solution)/shard_map/ppermute | solution.py:667
  6.9 16.7 %collective-permute-start.3 = (f32[66,8,128]{2,1,0:T(8,128)S(1)}, f32[66,8,128]{2,1,0:T(8,128)S(1)}, u32[]{:S(2)}, u32[]{:S(2)}) collective-permute-start(f32[66,8,128]{2,1,0:T(8,128)S(1)} %get-tuple-element.56), channel_id=1, source_target_pairs={{0,224},{32,64},{64,32},{96,128},{128,96},{160,192},{192,160},{224... | collective-permute-start | bytes 811016 | tf_op jit(solution)/shard_map/ppermute | solution.py:667
  6.9 8.0 %collective-permute-start = (f32[9,8,128]{2,1,0:T(8,128)S(1)}, f32[9,8,128]{2,1,0:T(8,128)S(1)}, u32[]{:S(2)}, u32[]{:S(2)}) collective-permute-start(f32[9,8,128]{2,1,0:T(8,128)S(1)} %get-tuple-element.50), channel_id=1, source_target_pairs={{0,1},{1,0},{2,3},{3,2},{4,5},{5,4},{6,7},{7,6},{8,9},{9,8},{10,11... | collective-permute-start | bytes 110600 | tf_op jit(solution)/shard_map/ppermute | solution.py:667
  7.7 8.5 %collective-permute-start.1 = (f32[9,8,128]{2,1,0:T(8,128)S(1)}, f32[9,8,128]{2,1,0:T(8,128)S(1)}, u32[]{:S(2)}, u32[]{:S(2)}) collective-permute-start(f32[9,8,128]{2,1,0:T(8,128)S(1)} %get-tuple-element.51), channel_id=1, source_target_pairs={{0,31},{1,2},{2,1},{3,4},{4,3},{5,6},{6,5},{7,8},{8,7},{9,10},{10,... | collective-permute-start | bytes 110600 | tf_op jit(solution)/shard_map/ppermute | solution.py:667
  16.4 7.2 %collective-permute-start.4 = (f32[2,8,128]{2,1,0:T(8,128)S(1)}, f32[2,8,128]{2,1,0:T(8,128)S(1)}, u32[]{:S(2)}, u32[]{:S(2)}) collective-permute-start(f32[2,8,128]{2,1,0:T(8,128)S(1)} %get-tuple-element.57), channel_id=1, source_target_pairs={{0,32},{32,0},{64,96},{96,64},{128,160},{160,128},{192,224},{224,1... | collective-permute-start | bytes 24584 | tf_op jit(solution)/shard_map/ppermute | solution.py:667
  19.3 4.3 %collective-permute-start.5 = (f32[2,8,128]{2,1,0:T(8,128)S(1)}, f32[2,8,128]{2,1,0:T(8,128)S(1)}, u32[]{:S(2)}, u32[]{:S(2)}) collective-permute-start(f32[2,8,128]{2,1,0:T(8,128)S(1)} %get-tuple-element.58), channel_id=1, source_target_pairs={{0,224},{32,64},{64,32},{96,128},{128,96},{160,192},{192,160},{224... | collective-permute-start | bytes 24584 | tf_op jit(solution)/shard_map/ppermute | solution.py:667
  25.5 7.6 %collective-permute-start.6 = (f32[2,8,128]{2,1,0:T(8,128)S(1)}, f32[2,8,128]{2,1,0:T(8,128)S(1)}, u32[]{:S(2)}, u32[]{:S(2)}) collective-permute-start(f32[2,8,128]{2,1,0:T(8,128)S(1)} %get-tuple-element.80), channel_id=1, source_target_pairs={{0,1},{1,0},{2,3},{3,2},{4,5},{5,4},{6,7},{7,6},{8,9},{9,8},{10,11... | collective-permute-start | bytes 24584 | tf_op jit(solution)/shard_map/ppermute | solution.py:667
  25.6 7.5 %collective-permute-start.7 = (f32[2,8,128]{2,1,0:T(8,128)S(1)}, f32[2,8,128]{2,1,0:T(8,128)S(1)}, u32[]{:S(2)}, u32[]{:S(2)}) collective-permute-start(f32[2,8,128]{2,1,0:T(8,128)S(1)} %get-tuple-element.81), channel_id=1, source_target_pairs={{0,31},{1,2},{2,1},{3,4},{4,3},{5,6},{6,5},{7,8},{8,7},{9,10},{10,... | collective-permute-start | bytes 24584 | tf_op jit(solution)/shard_map/ppermute | solution.py:667
  33.1 5.4 %collective-permute-start.10 = (f32[12,8,128]{2,1,0:T(8,128)S(1)}, f32[12,8,128]{2,1,0:T(8,128)S(1)}, u32[]{:S(2)}, u32[]{:S(2)}) collective-permute-start(f32[12,8,128]{2,1,0:T(8,128)S(1)} %shard_map.112.own), channel_id=1, source_target_pairs={{0,192},{32,224},{64,128},{96,160},{128,64},{160,96},{192,0},{224,... | collective-permute-start | bytes 147464 | tf_op jit(solution)/shard_map/ppermute | solution.py:667
  35.9 3.3 %collective-permute-start.9 = (f32[12,8,128]{2,1,0:T(8,128)S(1)}, f32[12,8,128]{2,1,0:T(8,128)S(1)}, u32[]{:S(2)}, u32[]{:S(2)}) collective-permute-start(f32[12,8,128]{2,1,0:T(8,128)S(1)} %shard_map.112.own), channel_id=1, source_target_pairs={{0,64},{32,96},{64,0},{96,32},{128,192},{160,224},{192,128},{224,1... | collective-permute-start | bytes 147464 | tf_op jit(solution)/shard_map/ppermute | solution.py:667
  38.4 3.0 %collective-permute-start.8 = (f32[12,8,128]{2,1,0:T(8,128)S(1)}, f32[12,8,128]{2,1,0:T(8,128)S(1)}, u32[]{:S(2)}, u32[]{:S(2)}) collective-permute-start(f32[12,8,128]{2,1,0:T(8,128)S(1)} %shard_map.112.own), channel_id=1, source_target_pairs={{0,32},{32,0},{64,96},{96,64},{128,160},{160,128},{192,224},{224,1... | collective-permute-start | bytes 147464 | tf_op jit(solution)/shard_map/ppermute | solution.py:667
  39.2 2.2 %collective-permute-start.11 = (f32[12,8,128]{2,1,0:T(8,128)S(1)}, f32[12,8,128]{2,1,0:T(8,128)S(1)}, u32[]{:S(2)}, u32[]{:S(2)}) collective-permute-start(f32[12,8,128]{2,1,0:T(8,128)S(1)} %shard_map.113), channel_id=1, source_target_pairs={{0,32},{32,0},{64,96},{96,64},{128,160},{160,128},{192,224},{224,1... | collective-permute-start | bytes 147464 | tf_op jit(solution)/shard_map/ppermute | solution.py:667

commit v7 on v6

--- a/solution.py
+++ b/solution.py
@@ -82,10 +82,10 @@
 
 def load_kernel(
     levels, t, s, u, v, depth_in, prior_in, t_out, s_out, u_out, v_out, own, side_0, side_1, depth_out,
-    prior, depth, sems, sems_plane,
+    prior, depth, t_buf, s_buf, u_buf, v_buf, sems, sems_plane,
 ):
     _, lon_even = evens()
-    fields, kept = (t, s, u, v), (t_out, s_out, u_out, v_out)
+    fields, outs, kept = (t, s, u, v), (t_out, s_out, u_out, v_out), (t_buf, s_buf, u_buf, v_buf)
     planes = [
         pltpu.make_async_copy(src, dst, sems_plane.at[i])
         for i, (src, dst) in enumerate(((depth_in, depth), (prior_in, prior)))
@@ -125,6 +125,7 @@
             for f in range(2):
                 for r in range(ROWS):
                     x = kept[2 * pair + f][pl.ds(GROUP * ROWS * g + r, GROUP, stride=ROWS), :]
+                    outs[2 * pair + f][GROUPS * r + g] = x
                     pack = jnp.where(slot == 16 * f + r, turn(x, 64 * f + 4 * r + 2), pack)
             own[pair * GROUPS + g] = pack
             packs.append(pack)
@@ -150,9 +151,7 @@
         for field in range(4):
             for r in range(2):
                 for swap, row in ((swap_0, outer), (swap_1, ROWS - 2 - outer)):
-                    swap[(r * 4 + field) * GROUPS + g] = fields[field][
-                        pl.ds(GROUP * ROWS * g + row + r, GROUP, stride=ROWS), :
-                    ]
+                    swap[(r * 4 + field) * GROUPS + g] = fields[field][GROUPS * (row + r) + g]
         return carry
 
     lax.fori_loop(0, GROUPS, body, 0)
@@ -217,7 +216,7 @@
 
     def level_row(self, ref, field, g, j):
         if 0 <= j < ROWS:
-            return ref[pl.ds(GROUP * ROWS * g + j, GROUP, stride=ROWS), :]
+            return ref[GROUPS * j + g]
         return self.beyond(j >= ROWS, ((j - ROWS if j >= ROWS else j + 2) * 4 + field) * GROUPS + g)
 
     def neighbours(self, q, corner):
@@ -393,7 +392,7 @@
                 sum_v[r] += new_v
         return carry
 
-    lax.fori_loop(0, GROUPS, body, 0, unroll=4 if corners else 2)
+    lax.fori_loop(0, GROUPS, body, 0, unroll=GROUPS if corners else 1)
 
 
 def write_sums(windows, sum_u, sum_v, block):
@@ -418,9 +417,8 @@
     dep.build_inner(near, depth)
 
     def write(g, r, new_u, new_v):
-        rows = pl.ds(GROUP * ROWS * g + r, GROUP, stride=ROWS)
-        u_next[rows, :] = new_u
-        v_next[rows, :] = new_v
+        u_next[GROUPS * r + g] = new_u
+        v_next[GROUPS * r + g] = new_v
 
     momentum_levels(
         near, dep, lat_total, INNER, False, t, s, u, v, write, kept, sum_x, sum_y, sum_u, sum_v
@@ -462,12 +460,20 @@
         strip_1[half] = jnp.where(near.lon_even, strips[1], strips[0])
 
 
-def merge_kernel(u_inner, v_inner, u_outer, v_outer, u_next, v_next):
+def merge_kernel(u_inner, v_inner, u_outer, v_outer, u_next, v_next, parting):
     for inner, outer, out in ((u_inner, u_outer, u_next), (v_inner, v_outer, v_next)):
-        out[...] = inner[...]
         for g in range(GROUPS):
-            for i, r in enumerate(OUTER_ROWS):
-                out[pl.ds(GROUP * ROWS * g + r, GROUP, stride=ROWS), :] = outer[i, g]
+            for r in range(ROWS):
+                tile = outer[OUTER_ROWS.index(r), g] if r in OUTER_ROWS else inner[GROUPS * r + g]
+                out[pl.ds(GROUP * ROWS * g + r, GROUP, stride=ROWS), :] = tile
+    source = lax.broadcasted_iota(jnp.int32, parting.shape, 0)
+    target = lax.broadcasted_iota(jnp.int32, parting.shape, 1)
+    rim = source - COLS
+    column = jnp.where(
+        source < COLS, source + 32, jnp.where(rim < 32, rim + 160, jnp.where(rim >= 96, rim - 96, -1))
+    )
+    wanted = jnp.where(target < COLS, 2 * target, 2 * (target - COLS) + 1)
+    parting[...] = jnp.where(column == wanted, 1.0, 0.0).astype(jnp.bfloat16)
 
 
 def tracer_kernel(
@@ -544,16 +550,16 @@
 
 
 class Plane:
-    def __init__(self, own, rim):
-        self.own, self.rim = own, rim
+    def __init__(self, even, odd):
+        self.even, self.odd = even, odd
 
     def map(self, other, fn):
         if isinstance(other, Plane):
             return Plane(
-                [fn(a, b) for a, b in zip(self.own, other.own)],
-                [fn(a, b) for a, b in zip(self.rim, other.rim)],
+                [fn(a, b) for a, b in zip(self.even, other.even)],
+                [fn(a, b) for a, b in zip(self.odd, other.odd)],
             )
-        return Plane([fn(a, other) for a in self.own], [fn(a, other) for a in self.rim])
+        return Plane([fn(a, other) for a in self.even], [fn(a, other) for a in self.odd])
 
     def __add__(self, other):
         return self.map(other, lambda a, b: a + b)
@@ -567,25 +573,32 @@
     def low(self, other):
         return self.map(other, jnp.minimum)
 
-    def side(self, by, lane):
-        at = lanes() == lane
-        pairs = [(turn(a, by), turn(b, by)) for a, b in zip(self.own, self.rim)]
-        return Plane([jnp.where(at, b, a) for a, b in pairs], [jnp.where(at, a, b) for a, b in pairs])
-
     def east(self):
-        return self.side(-1, COLS - 1)
+        return Plane(self.odd, [turn(x, -1) for x in self.even])
 
     def west(self):
-        return self.side(1, 0)
+        return Plane([turn(x, 1) for x in self.odd], self.even)
 
     def north(self):
-        return Plane(*[x[1:] + [turn(x[0], -1, 0)] for x in (self.own, self.rim)])
+        return Plane(*[x[1:] + [turn(x[0], -1, 0)] for x in (self.even, self.odd)])
 
     def south(self):
-        return Plane(*[[turn(x[-1], 1, 0)] + x[:-1] for x in (self.own, self.rim)])
-
-
-def solve_kernel(levels, own, core, chip_0, chip_1, passed, stored, out, own_buf, rim_buf):
+        return Plane(*[[turn(x[-1], 1, 0)] + x[:-1] for x in (self.even, self.odd)])
+
+
+def one_hot(x, matrix, side, terms):
+    total = None
+    for _ in range(terms):
+        term = x.astype(jnp.bfloat16)
+        x = x - term.astype(jnp.float32)
+        product = lax.dot_general(
+            term, matrix, (((1,), (side,)), ((), ())), preferred_element_type=jnp.float32
+        )
+        total = product if total is None else total + product
+    return total
+
+
+def solve_kernel(levels, own, core, chip_0, chip_1, passed, parting, stored, out, own_buf, rim_buf):
     del stored
     lat, _ = place()
     lat_even, lon_even = evens()
@@ -615,6 +628,10 @@
                     mid, rim = jnp.where(inside, mid, 0.0), jnp.where(inside, rim, 0.0)
                 own_buf[at : at + GROUP, :] = mid
                 rim_buf[at : at + GROUP, :] = rim
+        both = one_hot(
+            jnp.concatenate([own_buf[...], rim_buf[...]], axis=1), parting[...], 0, 1 if plane == 0 else 3
+        )
+        own_buf[...], rim_buf[...] = both[:, :COLS], both[:, COLS:]
         return Plane(
             *[[buf[pl.ds(t, GROUP, stride=STEPS), :] for t in range(STEPS)] for buf in (own_buf, rim_buf)]
         )
@@ -646,8 +663,12 @@
         height = height + change
     height = height * ocean
     for t in range(STEPS):
-        own_buf[pl.ds(t, GROUP, stride=STEPS), :] = height.own[t]
-    out[...] = own_buf[2 * ROWS : 3 * ROWS, :]
+        own_buf[pl.ds(t, GROUP, stride=STEPS), :] = height.even[t]
+        rim_buf[pl.ds(t, GROUP, stride=STEPS), :] = height.odd[t]
+    rows = slice(2 * ROWS, 3 * ROWS)
+    out[...] = one_hot(
+        jnp.concatenate([own_buf[rows, :], rim_buf[rows, :]], axis=1), parting[:COLS, :], 1, 3
+    )
 
 
 def join_kernel(count, *refs):
@@ -723,11 +744,14 @@
     def tiles(n):
         return shape(n, *TILE)
 
+    by_rows = tiles(ROWS * GROUPS)
+
     *kept, own, to_0, to_1, depth, prior = call(
         functools.partial(load_kernel, levels),
-        (padded,) * 4 + (tiles(PACKS + 1), tiles(SIDE), tiles(SIDE), plane, plane),
+        (by_rows,) * 4 + (tiles(PACKS + 1), tiles(SIDE), tiles(SIDE), plane, plane),
         [
             pltpu.VMEM((rows, cols), jnp.int32),
+            *[pltpu.VMEM((PADDED, cols), jnp.float32)] * 4,
             pltpu.SemaphoreType.DMA((4 * LOADS,)),
             pltpu.SemaphoreType.DMA((2,)),
         ],
@@ -747,7 +771,7 @@
     scratch += [pltpu.VMEM((ROWS, *TILE), jnp.float32)] * 2
     u_inner, v_inner, sums, inner, kept_laps = call(
         functools.partial(inner_kernel, lat_total),
-        (padded, padded, tiles(4), tiles(3 * ROWS), shape(2 * len(KEPT), GROUPS, *TILE)),
+        (by_rows, by_rows, tiles(4), tiles(3 * ROWS), shape(2 * len(KEPT), GROUPS, *TILE)),
         scratch,
         *kept,
         depth,
@@ -767,7 +791,10 @@
         inner,
         kept_laps,
     )
-    u_next, v_next = call(merge_kernel, (padded, padded), [], u_inner, v_inner, u_outer, v_outer)
+    matrix = jax.ShapeDtypeStruct((2 * COLS, 2 * COLS), jnp.bfloat16)
+    u_next, v_next, parting = call(
+        merge_kernel, (padded, padded, matrix), [], u_inner, v_inner, u_outer, v_outer
+    )
     pieces = []
     for part in range(PARTS):
         pieces += call(
@@ -823,8 +850,9 @@
         chip_0,
         chip_1,
         passed,
+        parting,
         stored,
-        ins=[VMEM] * 5 + [ANY],
+        ins=[VMEM] * 6 + [ANY],
     )
     return *[x.reshape(levels, rows, cols) for x in results], height
 

time: 45.7 us -> 44.3 us (0.969)
  Pallas kernels: 19.7 us -> 18.6 us
    pallas_call x14, Pallas kernels: 19.7 us -> 18.6 us  [call(): pl.pallas_call(kernel, out_shape=outs, in_specs=ins or [VMEM] * len(args)...]
  transfers between devices with their start and end apart: 12 -> 12, of which waited for: 2 -> 2; matrix products, arithmetic and copies ran while one was open for 0% -> 0% of each run, Pallas kernels for 23% -> 22%
where the time goes in v7:
time: 44.3 us; the launch traced here: 44.2 us
  starting transfers between devices  22.9 us (52%)
  Pallas kernels  18.6 us (42%)
  waiting for transfers between devices  1.92 us (4%)
  between operations  0.81 us (2%)
    ppermute x12, starting transfers between devices, swap(): lax.ppermute(value, axis, [(i, partner(i) % count) for i in range(count)])  22.9 us
    pallas_call x14, Pallas kernels, call(): pl.pallas_call(kernel, out_shape=outs, in_specs=ins or [VMEM] * len(args)...  18.6 us
    ppermute x12, waiting for transfers between devices, swap(): lax.ppermute(value, axis, [(i, partner(i) % count) for i in range(count)])  1.92 us
  transfers between devices with their start and end apart: 12, of which 2 were waited for; matrix products, arithmetic and copies ran while one was open for 0% of the time, Pallas kernels for 22%

profile of v7, /device:TPU:1, one launch (start us, length us, event | category | flops | bytes accessed | tf_op | source)
XLA Modules:
  0.0 44.2 jit_solution(7641790671590811214)
XLA Ops:
  0.6 2.8 %shard_map.101 = (f32[128,8,128]{2,1,0:T(8,128)S(1)}, f32[128,8,128]{2,1,0:T(8,128)S(1)}, f32[128,8,128]{2,1,0:T(8,128)S(1)}, f32[128,8,128]{2,1,0:T(8,128)S(1)}...) custom-call(f32[992,128]{1,0:T(8,128)} %bitcast.8, ...), custom_call_target="tpu_custom_call" | custom-call | bytes 4194304 | tf_op jit(solution)/shard_map/pallas_call | solution.py:717
  3.4 0.1 shard_map.103
  3.5 3.3 %collective-permute-start.2 = (f32[66,8,128]{2,1,0:T(8,128)S(1)}, f32[66,8,128]{2,1,0:T(8,128)S(1)}, u32[]{:S(2)}, u32[]{:S(2)}) collective-permute-start(f32[66,8,128]{2,1,0:T(8,128)S(1)} %get-tuple-element.56), channel_id=1, source_target_pairs={{0,32},{32,0},{64,96},{96,64},{128,160},{160,128},{192,224},{224,1... | collective-permute-start | bytes 811016 | tf_op jit(solution)/shard_map/ppermute | solution.py:688
  6.9 0.0 collective-permute-start.3
  6.9 0.8 %collective-permute-start = (f32[9,8,128]{2,1,0:T(8,128)S(1)}, f32[9,8,128]{2,1,0:T(8,128)S(1)}, u32[]{:S(2)}, u32[]{:S(2)}) collective-permute-start(f32[9,8,128]{2,1,0:T(8,128)S(1)} %get-tuple-element.51), channel_id=1, source_target_pairs={{0,1},{1,0},{2,3},{3,2},{4,5},{5,4},{6,7},{7,6},{8,9},{9,8},{10,11... | collective-permute-start | bytes 110600 | tf_op jit(solution)/shard_map/ppermute | solution.py:688
  7.6 7.2 %collective-permute-start.1 = (f32[9,8,128]{2,1,0:T(8,128)S(1)}, f32[9,8,128]{2,1,0:T(8,128)S(1)}, u32[]{:S(2)}, u32[]{:S(2)}) collective-permute-start(f32[9,8,128]{2,1,0:T(8,128)S(1)} %get-tuple-element.52), channel_id=1, source_target_pairs={{0,31},{1,2},{2,1},{3,4},{4,3},{5,6},{6,5},{7,8},{8,7},{9,10},{10,... | collective-permute-start | bytes 110600 | tf_op jit(solution)/shard_map/ppermute | solution.py:688
  14.8 0.0 collective-permute-done.side_0
  14.8 1.3 %collective-permute-done.1.side_1 = f32[9,8,128]{2,1,0:T(8,128)S(1)} collective-permute-done((f32[9,8,128]{2,1,0:T(8,128)S(1)}, f32[9,8,128]{2,1,0:T(8,128)S(1)}, u32[]{:S(2)}, u32[]{:S(2)}) %collective-permute-start.1) | collective-permute-done | bytes 36896 | tf_op jit(solution)/shard_map/ppermute | solution.py:688
  16.2 0.2 shard_map.104
  16.3 2.9 %collective-permute-start.4 = (f32[2,8,128]{2,1,0:T(8,128)S(1)}, f32[2,8,128]{2,1,0:T(8,128)S(1)}, u32[]{:S(2)}, u32[]{:S(2)}) collective-permute-start(f32[2,8,128]{2,1,0:T(8,128)S(1)} %get-tuple-element.58), channel_id=1, source_target_pairs={{0,32},{32,0},{64,96},{96,64},{128,160},{160,128},{192,224},{224,1... | collective-permute-start | bytes 24584 | tf_op jit(solution)/shard_map/ppermute | solution.py:688
  19.2 0.0 collective-permute-start.5
  19.2 3.4 %shard_map.102 = (f32[128,8,128]{2,1,0:T(8,128)S(1)}, f32[128,8,128]{2,1,0:T(8,128)S(1)}, f32[4,8,128]{2,1,0:T(8,128)S(1)}, f32[48,8,128]{2,1,0:T(8,128)S(1)}, f32[8,8,8,128]{3,2,1,0:T(8,128)S(1)}) custom-call(f32[128,8,128]{2,1,0:T(8,128)S(1)} %get-tuple-element.45.t, f32[128,8,128]{2,1,0:T(8,128)S(1)} %get-tuple-element.46.s, ...), custom_call_target="tpu_custom_call" | custom-call | bytes 4194304 | tf_op jit(solution)/shard_map/pallas_call | solution.py:717
  22.6 0.0 collective-permute-done.4.corner_0
  22.6 0.0 collective-permute-done.5.corner_1
  22.7 0.0 collective-permute-done.3.swap_1
  22.7 2.2 %shard_map.105 = (f32[4,8,8,128]{3,2,1,0:T(8,128)S(1)}, f32[4,8,8,128]{3,2,1,0:T(8,128)S(1)}, f32[8,8,128]{2,1,0:T(8,128)S(1)}, f32[2,8,128]{2,1,0:T(8,128)S(1)}...) custom-call(f32[128,8,128]{2,1,0:T(8,128)S(1)} %get-tuple-element.45.t, f32[128,8,128]{2,1,0:T(8,128)S(1)} %get-tuple-element.46.s, ...), custom_call_target="tpu_custom_call" | custom-call | bytes 4194304 | tf_op jit(solution)/shard_map/pallas_call | solution.py:717
  24.9 0.0 collective-permute-start.6
  24.9 5.1 %collective-permute-start.7 = (f32[2,8,128]{2,1,0:T(8,128)S(1)}, f32[2,8,128]{2,1,0:T(8,128)S(1)}, u32[]{:S(2)}, u32[]{:S(2)}) collective-permute-start(f32[2,8,128]{2,1,0:T(8,128)S(1)} %get-tuple-element.82), channel_id=1, source_target_pairs={{0,31},{1,2},{2,1},{3,4},{4,3},{5,6},{6,5},{7,8},{8,7},{9,10},{10,... | collective-permute-start | bytes 24584 | tf_op jit(solution)/shard_map/ppermute | solution.py:688
  30.1 1.1 %shard_map.108 = (f32[256,128]{1,0:T(8,128)S(1)}, f32[256,128]{1,0:T(8,128)S(1)}) custom-call(f32[128,8,128]{2,1,0:T(8,128)S(1)} %get-tuple-element.45.t, f32[128,8,128]{2,1,0:T(8,128)S(1)} %get-tuple-element.46.s, f32[128,8,128]{2,1,0:T(8,128)S(1)} %get-tuple-element.47.u, f32[128,8,128]{2,1,0:T(8,128)S(1)} %get-tuple-element.48.v, ...), custom_call_target="tpu_custom_call" | custom-call | bytes 4194304 | tf_op jit(solution)/shard_map/pallas_call | solution.py:717
  31.2 1.2 %shard_map.107 = (f32[256,128]{1,0:T(8,128)S(1)}, f32[256,128]{1,0:T(8,128)S(1)}) custom-call(f32[128,8,128]{2,1,0:T(8,128)S(1)} %get-tuple-element.45.t, f32[128,8,128]{2,1,0:T(8,128)S(1)} %get-tuple-element.46.s, f32[128,8,128]{2,1,0:T(8,128)S(1)} %get-tuple-element.47.u, f32[128,8,128]{2,1,0:T(8,128)S(1)} %get-tuple-element.48.v, ...), custom_call_target="tpu_custom_call" | custom-call | bytes 4194304 | tf_op jit(solution)/shard_map/pallas_call | solution.py:717
  32.4 2.7 %collective-permute-start.10 = (f32[12,8,128]{2,1,0:T(8,128)S(1)}, f32[12,8,128]{2,1,0:T(8,128)S(1)}, u32[]{:S(2)}, u32[]{:S(2)}) collective-permute-start(f32[12,8,128]{2,1,0:T(8,128)S(1)} %shard_map.112.own), channel_id=1, source_target_pairs={{0,192},{32,224},{64,128},{96,160},{128,64},{160,96},{192,0},{224,... | collective-permute-start | bytes 147464 | tf_op jit(solution)/shard_map/ppermute | solution.py:688
  35.2 0.0 collective-permute-start.9
  35.2 0.3 shard_map.106
  35.5 1.2 %shard_map.110 = (f32[256,128]{1,0:T(8,128)S(1)}, f32[256,128]{1,0:T(8,128)S(1)}) custom-call(f32[128,8,128]{2,1,0:T(8,128)S(1)} %get-tuple-element.45.t, f32[128,8,128]{2,1,0:T(8,128)S(1)} %get-tuple-element.46.s, f32[128,8,128]{2,1,0:T(8,128)S(1)} %get-tuple-element.47.u, f32[128,8,128]{2,1,0:T(8,128)S(1)} %get-tuple-element.48.v, ...), custom_call_target="tpu_custom_call" | custom-call | bytes 4194304 | tf_op jit(solution)/shard_map/pallas_call | solution.py:717
  36.7 1.2 %shard_map.109 = (f32[256,128]{1,0:T(8,128)S(1)}, f32[256,128]{1,0:T(8,128)S(1)}) custom-call(f32[128,8,128]{2,1,0:T(8,128)S(1)} %get-tuple-element.45.t, f32[128,8,128]{2,1,0:T(8,128)S(1)} %get-tuple-element.46.s, f32[128,8,128]{2,1,0:T(8,128)S(1)} %get-tuple-element.47.u, f32[128,8,128]{2,1,0:T(8,128)S(1)} %get-tuple-element.48.v, ...), custom_call_target="tpu_custom_call" | custom-call | bytes 4194304 | tf_op jit(solution)/shard_map/pallas_call | solution.py:717
  37.8 0.1 collective-permute-start.8
  37.9 0.0 collective-permute-done.10.chip_1
  37.9 0.6 %collective-permute-done.9.chip_0 = f32[12,8,128]{2,1,0:T(8,128)S(1)} collective-permute-done((f32[12,8,128]{2,1,0:T(8,128)S(1)}, f32[12,8,128]{2,1,0:T(8,128)S(1)}, u32[]{:S(2)}, u32[]{:S(2)}) %collective-permute-start.9) | collective-permute-done | bytes 49184 | tf_op jit(solution)/shard_map/ppermute | solution.py:688
  38.5 0.7 %collective-permute-start.11 = (f32[12,8,128]{2,1,0:T(8,128)S(1)}, f32[12,8,128]{2,1,0:T(8,128)S(1)}, u32[]{:S(2)}, u32[]{:S(2)}) collective-permute-start(f32[12,8,128]{2,1,0:T(8,128)S(1)} %shard_map.113), channel_id=1, source_target_pairs={{0,32},{32,0},{64,96},{96,64},{128,160},{160,128},{192,224},{224,1... | collective-permute-start | bytes 147464 | tf_op jit(solution)/shard_map/ppermute | solution.py:688
  39.2 1.4 %shard_map.111 = (f32[992,128]{1,0:T(8,128)}, f32[992,128]{1,0:T(8,128)}, f32[992,128]{1,0:T(8,128)}, f32[992,128]{1,0:T(8,128)}, f32[8,128]{1,0:T(8,128)S(1)}) custom-call(f32[1024,128]{1,0:T(8,128)S(1)} %get-tuple-element.65.u_next.refs_4_, f32[1024,128]{1,0:T(8,128)S(1)} %get-tuple-element.66.v_next.refs_5_, ...), custom_call_target="tpu_custom_call" | custom-call | bytes 4194304 | tf_op jit(solution)/shard_map/pallas_call | solution.py:717
  40.5 0.0 collective-permute-done.8.core
  40.6 3.7 %shard_map.114 = f32[16,128]{1,0:T(8,128)} custom-call(f32[12,8,128]{2,1,0:T(8,128)S(1)} %shard_map.112.own, f32[12,8,128]{2,1,0:T(8,128)S(1)} %collective-permute-done.8.core, f32[12,8,128]{2,1,0:T(8,128)S(1)} %collective-permute-done.9.chip_0, f32[12,8,128]{2,1,0:T(8,128)S(1)} %collective-permute-done.10.chip_1, ...), custom_call_target="tpu_custom_call" | custom-call | bytes 4194304 | tf_op jit(solution)/shard_map/pallas_call | solution.py:717
  (6 shorter events, 0.0 us)
Async XLA Ops:
  3.5 19.1 %collective-permute-start.2 = (f32[66,8,128]{2,1,0:T(8,128)S(1)}, f32[66,8,128]{2,1,0:T(8,128)S(1)}, u32[]{:S(2)}, u32[]{:S(2)}) collective-permute-start(f32[66,8,128]{2,1,0:T(8,128)S(1)} %get-tuple-element.56), channel_id=1, source_target_pairs={{0,32},{32,0},{64,96},{96,64},{128,160},{160,128},{192,224},{224,1... | collective-permute-start | bytes 811016 | tf_op jit(solution)/shard_map/ppermute | solution.py:688
  6.9 15.8 %collective-permute-start.3 = (f32[66,8,128]{2,1,0:T(8,128)S(1)}, f32[66,8,128]{2,1,0:T(8,128)S(1)}, u32[]{:S(2)}, u32[]{:S(2)}) collective-permute-start(f32[66,8,128]{2,1,0:T(8,128)S(1)} %get-tuple-element.57), channel_id=1, source_target_pairs={{0,224},{32,64},{64,32},{96,128},{128,96},{160,192},{192,160},{224... | collective-permute-start | bytes 811016 | tf_op jit(solution)/shard_map/ppermute | solution.py:688
  6.9 8.0 %collective-permute-start = (f32[9,8,128]{2,1,0:T(8,128)S(1)}, f32[9,8,128]{2,1,0:T(8,128)S(1)}, u32[]{:S(2)}, u32[]{:S(2)}) collective-permute-start(f32[9,8,128]{2,1,0:T(8,128)S(1)} %get-tuple-element.51), channel_id=1, source_target_pairs={{0,1},{1,0},{2,3},{3,2},{4,5},{5,4},{6,7},{7,6},{8,9},{9,8},{10,11... | collective-permute-start | bytes 110600 | tf_op jit(solution)/shard_map/ppermute | solution.py:688
  7.6 8.5 %collective-permute-start.1 = (f32[9,8,128]{2,1,0:T(8,128)S(1)}, f32[9,8,128]{2,1,0:T(8,128)S(1)}, u32[]{:S(2)}, u32[]{:S(2)}) collective-permute-start(f32[9,8,128]{2,1,0:T(8,128)S(1)} %get-tuple-element.52), channel_id=1, source_target_pairs={{0,31},{1,2},{2,1},{3,4},{4,3},{5,6},{6,5},{7,8},{8,7},{9,10},{10,... | collective-permute-start | bytes 110600 | tf_op jit(solution)/shard_map/ppermute | solution.py:688
  16.3 6.3 %collective-permute-start.4 = (f32[2,8,128]{2,1,0:T(8,128)S(1)}, f32[2,8,128]{2,1,0:T(8,128)S(1)}, u32[]{:S(2)}, u32[]{:S(2)}) collective-permute-start(f32[2,8,128]{2,1,0:T(8,128)S(1)} %get-tuple-element.58), channel_id=1, source_target_pairs={{0,32},{32,0},{64,96},{96,64},{128,160},{160,128},{192,224},{224,1... | collective-permute-start | bytes 24584 | tf_op jit(solution)/shard_map/ppermute | solution.py:688
  19.2 3.4 %collective-permute-start.5 = (f32[2,8,128]{2,1,0:T(8,128)S(1)}, f32[2,8,128]{2,1,0:T(8,128)S(1)}, u32[]{:S(2)}, u32[]{:S(2)}) collective-permute-start(f32[2,8,128]{2,1,0:T(8,128)S(1)} %get-tuple-element.59), channel_id=1, source_target_pairs={{0,224},{32,64},{64,32},{96,128},{128,96},{160,192},{192,160},{224... | collective-permute-start | bytes 24584 | tf_op jit(solution)/shard_map/ppermute | solution.py:688
  24.9 7.5 %collective-permute-start.6 = (f32[2,8,128]{2,1,0:T(8,128)S(1)}, f32[2,8,128]{2,1,0:T(8,128)S(1)}, u32[]{:S(2)}, u32[]{:S(2)}) collective-permute-start(f32[2,8,128]{2,1,0:T(8,128)S(1)} %get-tuple-element.81), channel_id=1, source_target_pairs={{0,1},{1,0},{2,3},{3,2},{4,5},{5,4},{6,7},{7,6},{8,9},{9,8},{10,11... | collective-permute-start | bytes 24584 | tf_op jit(solution)/shard_map/ppermute | solution.py:688
  24.9 7.5 %collective-permute-start.7 = (f32[2,8,128]{2,1,0:T(8,128)S(1)}, f32[2,8,128]{2,1,0:T(8,128)S(1)}, u32[]{:S(2)}, u32[]{:S(2)}) collective-permute-start(f32[2,8,128]{2,1,0:T(8,128)S(1)} %get-tuple-element.82), channel_id=1, source_target_pairs={{0,31},{1,2},{2,1},{3,4},{4,3},{5,6},{6,5},{7,8},{8,7},{9,10},{10,... | collective-permute-start | bytes 24584 | tf_op jit(solution)/shard_map/ppermute | solution.py:688
  32.4 5.5 %collective-permute-start.10 = (f32[12,8,128]{2,1,0:T(8,128)S(1)}, f32[12,8,128]{2,1,0:T(8,128)S(1)}, u32[]{:S(2)}, u32[]{:S(2)}) collective-permute-start(f32[12,8,128]{2,1,0:T(8,128)S(1)} %shard_map.112.own), channel_id=1, source_target_pairs={{0,192},{32,224},{64,128},{96,160},{128,64},{160,96},{192,0},{224,... | collective-permute-start | bytes 147464 | tf_op jit(solution)/shard_map/ppermute | solution.py:688
  35.2 3.3 %collective-permute-start.9 = (f32[12,8,128]{2,1,0:T(8,128)S(1)}, f32[12,8,128]{2,1,0:T(8,128)S(1)}, u32[]{:S(2)}, u32[]{:S(2)}) collective-permute-start(f32[12,8,128]{2,1,0:T(8,128)S(1)} %shard_map.112.own), channel_id=1, source_target_pairs={{0,64},{32,96},{64,0},{96,32},{128,192},{160,224},{192,128},{224,1... | collective-permute-start | bytes 147464 | tf_op jit(solution)/shard_map/ppermute | solution.py:688
  37.8 2.7 %collective-permute-start.8 = (f32[12,8,128]{2,1,0:T(8,128)S(1)}, f32[12,8,128]{2,1,0:T(8,128)S(1)}, u32[]{:S(2)}, u32[]{:S(2)}) collective-permute-start(f32[12,8,128]{2,1,0:T(8,128)S(1)} %shard_map.112.own), channel_id=1, source_target_pairs={{0,32},{32,0},{64,96},{96,64},{128,160},{160,128},{192,224},{224,1... | collective-permute-start | bytes 147464 | tf_op jit(solution)/shard_map/ppermute | solution.py:688
  38.5 2.0 %collective-permute-start.11 = (f32[12,8,128]{2,1,0:T(8,128)S(1)}, f32[12,8,128]{2,1,0:T(8,128)S(1)}, u32[]{:S(2)}, u32[]{:S(2)}) collective-permute-start(f32[12,8,128]{2,1,0:T(8,128)S(1)} %shard_map.113), channel_id=1, source_target_pairs={{0,32},{32,0},{64,96},{96,64},{128,160},{160,128},{192,224},{224,1... | collective-permute-start | bytes 147464 | tf_op jit(solution)/shard_map/ppermute | solution.py:688

commit v8 on v7

--- a/solution.py
+++ b/solution.py
@@ -392,7 +392,7 @@
                 sum_v[r] += new_v
         return carry
 
-    lax.fori_loop(0, GROUPS, body, 0, unroll=GROUPS if corners else 1)
+    lax.fori_loop(0, GROUPS, body, 0, unroll=4 if corners else 1)
 
 
 def write_sums(windows, sum_u, sum_v, block):

time: 44.3 us -> 44.1 us (level)
  no operation moved by 1% of the time
where the time goes in v8:
time: 44.1 us; the launch traced here: 43.9 us
  starting transfers between devices  22.9 us (52%)
  Pallas kernels  18.3 us (41%)
  waiting for transfers between devices  1.92 us (4%)
  between operations  0.81 us (2%)
    ppermute x12, starting transfers between devices, swap(): lax.ppermute(value, axis, [(i, partner(i) % count) for i in range(count)])  22.9 us
    pallas_call x14, Pallas kernels, call(): pl.pallas_call(kernel, out_shape=outs, in_specs=ins or [VMEM] * len(args)...  18.3 us
    ppermute x12, waiting for transfers between devices, swap(): lax.ppermute(value, axis, [(i, partner(i) % count) for i in range(count)])  1.92 us
  transfers between devices with their start and end apart: 12, of which 2 were waited for; matrix products, arithmetic and copies ran while one was open for 0% of the time, Pallas kernels for 22%

profile of v8, /device:TPU:1, one launch (start us, length us, event | category | flops | bytes accessed | tf_op | source)
XLA Modules:
  0.0 43.9 jit_solution(8123888257964833131)
XLA Ops:
  0.6 2.8 %shard_map.101 = (f32[128,8,128]{2,1,0:T(8,128)S(1)}, f32[128,8,128]{2,1,0:T(8,128)S(1)}, f32[128,8,128]{2,1,0:T(8,128)S(1)}, f32[128,8,128]{2,1,0:T(8,128)S(1)}...) custom-call(f32[992,128]{1,0:T(8,128)} %bitcast.8, ...), custom_call_target="tpu_custom_call" | custom-call | bytes 4194304 | tf_op jit(solution)/shard_map/pallas_call | solution.py:717
  3.4 0.1 shard_map.103
  3.5 3.3 %collective-permute-start.2 = (f32[66,8,128]{2,1,0:T(8,128)S(1)}, f32[66,8,128]{2,1,0:T(8,128)S(1)}, u32[]{:S(2)}, u32[]{:S(2)}) collective-permute-start(f32[66,8,128]{2,1,0:T(8,128)S(1)} %get-tuple-element.56), channel_id=1, source_target_pairs={{0,32},{32,0},{64,96},{96,64},{128,160},{160,128},{192,224},{224,1... | collective-permute-start | bytes 811016 | tf_op jit(solution)/shard_map/ppermute | solution.py:688
  6.9 0.8 %collective-permute-start = (f32[9,8,128]{2,1,0:T(8,128)S(1)}, f32[9,8,128]{2,1,0:T(8,128)S(1)}, u32[]{:S(2)}, u32[]{:S(2)}) collective-permute-start(f32[9,8,128]{2,1,0:T(8,128)S(1)} %get-tuple-element.51), channel_id=1, source_target_pairs={{0,1},{1,0},{2,3},{3,2},{4,5},{5,4},{6,7},{7,6},{8,9},{9,8},{10,11... | collective-permute-start | bytes 110600 | tf_op jit(solution)/shard_map/ppermute | solution.py:688
  7.6 7.2 %collective-permute-start.1 = (f32[9,8,128]{2,1,0:T(8,128)S(1)}, f32[9,8,128]{2,1,0:T(8,128)S(1)}, u32[]{:S(2)}, u32[]{:S(2)}) collective-permute-start(f32[9,8,128]{2,1,0:T(8,128)S(1)} %get-tuple-element.52), channel_id=1, source_target_pairs={{0,31},{1,2},{2,1},{3,4},{4,3},{5,6},{6,5},{7,8},{8,7},{9,10},{10,... | collective-permute-start | bytes 110600 | tf_op jit(solution)/shard_map/ppermute | solution.py:688
  14.8 0.0 collective-permute-done.side_0
  14.8 1.3 %collective-permute-done.1.side_1 = f32[9,8,128]{2,1,0:T(8,128)S(1)} collective-permute-done((f32[9,8,128]{2,1,0:T(8,128)S(1)}, f32[9,8,128]{2,1,0:T(8,128)S(1)}, u32[]{:S(2)}, u32[]{:S(2)}) %collective-permute-start.1) | collective-permute-done | bytes 36896 | tf_op jit(solution)/shard_map/ppermute | solution.py:688
  16.2 0.2 shard_map.104
  16.3 2.9 %collective-permute-start.4 = (f32[2,8,128]{2,1,0:T(8,128)S(1)}, f32[2,8,128]{2,1,0:T(8,128)S(1)}, u32[]{:S(2)}, u32[]{:S(2)}) collective-permute-start(f32[2,8,128]{2,1,0:T(8,128)S(1)} %get-tuple-element.58), channel_id=1, source_target_pairs={{0,32},{32,0},{64,96},{96,64},{128,160},{160,128},{192,224},{224,1... | collective-permute-start | bytes 24584 | tf_op jit(solution)/shard_map/ppermute | solution.py:688
  19.2 0.0 collective-permute-start.5
  19.2 3.4 %shard_map.102 = (f32[128,8,128]{2,1,0:T(8,128)S(1)}, f32[128,8,128]{2,1,0:T(8,128)S(1)}, f32[4,8,128]{2,1,0:T(8,128)S(1)}, f32[48,8,128]{2,1,0:T(8,128)S(1)}, f32[8,8,8,128]{3,2,1,0:T(8,128)S(1)}) custom-call(f32[128,8,128]{2,1,0:T(8,128)S(1)} %get-tuple-element.45.t, f32[128,8,128]{2,1,0:T(8,128)S(1)} %get-tuple-element.46.s, ...), custom_call_target="tpu_custom_call" | custom-call | bytes 4194304 | tf_op jit(solution)/shard_map/pallas_call | solution.py:717
  22.6 0.0 collective-permute-done.4.corner_0
  22.6 0.0 collective-permute-done.5.corner_1
  22.7 0.0 collective-permute-done.3.swap_1
  22.7 1.9 %shard_map.105 = (f32[4,8,8,128]{3,2,1,0:T(8,128)S(1)}, f32[4,8,8,128]{3,2,1,0:T(8,128)S(1)}, f32[8,8,128]{2,1,0:T(8,128)S(1)}, f32[2,8,128]{2,1,0:T(8,128)S(1)}...) custom-call(f32[128,8,128]{2,1,0:T(8,128)S(1)} %get-tuple-element.45.t, f32[128,8,128]{2,1,0:T(8,128)S(1)} %get-tuple-element.46.s, ...), custom_call_target="tpu_custom_call" | custom-call | bytes 4194304 | tf_op jit(solution)/shard_map/pallas_call | solution.py:717
  24.5 0.1 collective-permute-start.6
  24.6 5.1 %collective-permute-start.7 = (f32[2,8,128]{2,1,0:T(8,128)S(1)}, f32[2,8,128]{2,1,0:T(8,128)S(1)}, u32[]{:S(2)}, u32[]{:S(2)}) collective-permute-start(f32[2,8,128]{2,1,0:T(8,128)S(1)} %get-tuple-element.82), channel_id=1, source_target_pairs={{0,31},{1,2},{2,1},{3,4},{4,3},{5,6},{6,5},{7,8},{8,7},{9,10},{10,... | collective-permute-start | bytes 24584 | tf_op jit(solution)/shard_map/ppermute | solution.py:688
  29.8 1.1 %shard_map.108 = (f32[256,128]{1,0:T(8,128)S(1)}, f32[256,128]{1,0:T(8,128)S(1)}) custom-call(f32[128,8,128]{2,1,0:T(8,128)S(1)} %get-tuple-element.45.t, f32[128,8,128]{2,1,0:T(8,128)S(1)} %get-tuple-element.46.s, f32[128,8,128]{2,1,0:T(8,128)S(1)} %get-tuple-element.47.u, f32[128,8,128]{2,1,0:T(8,128)S(1)} %get-tuple-element.48.v, ...), custom_call_target="tpu_custom_call" | custom-call | bytes 4194304 | tf_op jit(solution)/shard_map/pallas_call | solution.py:717
  31.0 1.2 %shard_map.107 = (f32[256,128]{1,0:T(8,128)S(1)}, f32[256,128]{1,0:T(8,128)S(1)}) custom-call(f32[128,8,128]{2,1,0:T(8,128)S(1)} %get-tuple-element.45.t, f32[128,8,128]{2,1,0:T(8,128)S(1)} %get-tuple-element.46.s, f32[128,8,128]{2,1,0:T(8,128)S(1)} %get-tuple-element.47.u, f32[128,8,128]{2,1,0:T(8,128)S(1)} %get-tuple-element.48.v, ...), custom_call_target="tpu_custom_call" | custom-call | bytes 4194304 | tf_op jit(solution)/shard_map/pallas_call | solution.py:717
  32.1 0.0 collective-permute-done.7.refs_2_
  32.2 2.7 %collective-permute-start.10 = (f32[12,8,128]{2,1,0:T(8,128)S(1)}, f32[12,8,128]{2,1,0:T(8,128)S(1)}, u32[]{:S(2)}, u32[]{:S(2)}) collective-permute-start(f32[12,8,128]{2,1,0:T(8,128)S(1)} %shard_map.112.own), channel_id=1, source_target_pairs={{0,192},{32,224},{64,128},{96,160},{128,64},{160,96},{192,0},{224,... | collective-permute-start | bytes 147464 | tf_op jit(solution)/shard_map/ppermute | solution.py:688
  34.9 0.0 collective-permute-start.9
  34.9 0.3 shard_map.106
  35.2 1.2 %shard_map.110 = (f32[256,128]{1,0:T(8,128)S(1)}, f32[256,128]{1,0:T(8,128)S(1)}) custom-call(f32[128,8,128]{2,1,0:T(8,128)S(1)} %get-tuple-element.45.t, f32[128,8,128]{2,1,0:T(8,128)S(1)} %get-tuple-element.46.s, f32[128,8,128]{2,1,0:T(8,128)S(1)} %get-tuple-element.47.u, f32[128,8,128]{2,1,0:T(8,128)S(1)} %get-tuple-element.48.v, ...), custom_call_target="tpu_custom_call" | custom-call | bytes 4194304 | tf_op jit(solution)/shard_map/pallas_call | solution.py:717
  36.4 1.2 %shard_map.109 = (f32[256,128]{1,0:T(8,128)S(1)}, f32[256,128]{1,0:T(8,128)S(1)}) custom-call(f32[128,8,128]{2,1,0:T(8,128)S(1)} %get-tuple-element.45.t, f32[128,8,128]{2,1,0:T(8,128)S(1)} %get-tuple-element.46.s, f32[128,8,128]{2,1,0:T(8,128)S(1)} %get-tuple-element.47.u, f32[128,8,128]{2,1,0:T(8,128)S(1)} %get-tuple-element.48.v, ...), custom_call_target="tpu_custom_call" | custom-call | bytes 4194304 | tf_op jit(solution)/shard_map/pallas_call | solution.py:717
  37.6 0.1 collective-permute-start.8
  37.7 0.0 collective-permute-done.10.chip_1
  37.7 0.6 %collective-permute-done.9.chip_0 = f32[12,8,128]{2,1,0:T(8,128)S(1)} collective-permute-done((f32[12,8,128]{2,1,0:T(8,128)S(1)}, f32[12,8,128]{2,1,0:T(8,128)S(1)}, u32[]{:S(2)}, u32[]{:S(2)}) %collective-permute-start.9) | collective-permute-done | bytes 49184 | tf_op jit(solution)/shard_map/ppermute | solution.py:688
  38.2 0.7 %collective-permute-start.11 = (f32[12,8,128]{2,1,0:T(8,128)S(1)}, f32[12,8,128]{2,1,0:T(8,128)S(1)}, u32[]{:S(2)}, u32[]{:S(2)}) collective-permute-start(f32[12,8,128]{2,1,0:T(8,128)S(1)} %shard_map.113), channel_id=1, source_target_pairs={{0,32},{32,0},{64,96},{96,64},{128,160},{160,128},{192,224},{224,1... | collective-permute-start | bytes 147464 | tf_op jit(solution)/shard_map/ppermute | solution.py:688
  38.9 1.4 %shard_map.111 = (f32[992,128]{1,0:T(8,128)}, f32[992,128]{1,0:T(8,128)}, f32[992,128]{1,0:T(8,128)}, f32[992,128]{1,0:T(8,128)}, f32[8,128]{1,0:T(8,128)S(1)}) custom-call(f32[1024,128]{1,0:T(8,128)S(1)} %get-tuple-element.65.u_next.refs_4_, f32[1024,128]{1,0:T(8,128)S(1)} %get-tuple-element.66.v_next.refs_5_, ...), custom_call_target="tpu_custom_call" | custom-call | bytes 4194304 | tf_op jit(solution)/shard_map/pallas_call | solution.py:717
  40.3 0.0 collective-permute-done.11.passed
  40.3 3.7 %shard_map.114 = f32[16,128]{1,0:T(8,128)} custom-call(f32[12,8,128]{2,1,0:T(8,128)S(1)} %shard_map.112.own, f32[12,8,128]{2,1,0:T(8,128)S(1)} %collective-permute-done.8.core, f32[12,8,128]{2,1,0:T(8,128)S(1)} %collective-permute-done.9.chip_0, f32[12,8,128]{2,1,0:T(8,128)S(1)} %collective-permute-done.10.chip_1, ...), custom_call_target="tpu_custom_call" | custom-call | bytes 4194304 | tf_op jit(solution)/shard_map/pallas_call | solution.py:717
  (6 shorter events, 0.0 us)
Async XLA Ops:
  3.5 19.1 %collective-permute-start.2 = (f32[66,8,128]{2,1,0:T(8,128)S(1)}, f32[66,8,128]{2,1,0:T(8,128)S(1)}, u32[]{:S(2)}, u32[]{:S(2)}) collective-permute-start(f32[66,8,128]{2,1,0:T(8,128)S(1)} %get-tuple-element.56), channel_id=1, source_target_pairs={{0,32},{32,0},{64,96},{96,64},{128,160},{160,128},{192,224},{224,1... | collective-permute-start | bytes 811016 | tf_op jit(solution)/shard_map/ppermute | solution.py:688
  6.9 15.8 %collective-permute-start.3 = (f32[66,8,128]{2,1,0:T(8,128)S(1)}, f32[66,8,128]{2,1,0:T(8,128)S(1)}, u32[]{:S(2)}, u32[]{:S(2)}) collective-permute-start(f32[66,8,128]{2,1,0:T(8,128)S(1)} %get-tuple-element.57), channel_id=1, source_target_pairs={{0,224},{32,64},{64,32},{96,128},{128,96},{160,192},{192,160},{224... | collective-permute-start | bytes 811016 | tf_op jit(solution)/shard_map/ppermute | solution.py:688
  6.9 8.0 %collective-permute-start = (f32[9,8,128]{2,1,0:T(8,128)S(1)}, f32[9,8,128]{2,1,0:T(8,128)S(1)}, u32[]{:S(2)}, u32[]{:S(2)}) collective-permute-start(f32[9,8,128]{2,1,0:T(8,128)S(1)} %get-tuple-element.51), channel_id=1, source_target_pairs={{0,1},{1,0},{2,3},{3,2},{4,5},{5,4},{6,7},{7,6},{8,9},{9,8},{10,11... | collective-permute-start | bytes 110600 | tf_op jit(solution)/shard_map/ppermute | solution.py:688
  7.6 8.5 %collective-permute-start.1 = (f32[9,8,128]{2,1,0:T(8,128)S(1)}, f32[9,8,128]{2,1,0:T(8,128)S(1)}, u32[]{:S(2)}, u32[]{:S(2)}) collective-permute-start(f32[9,8,128]{2,1,0:T(8,128)S(1)} %get-tuple-element.52), channel_id=1, source_target_pairs={{0,31},{1,2},{2,1},{3,4},{4,3},{5,6},{6,5},{7,8},{8,7},{9,10},{10,... | collective-permute-start | bytes 110600 | tf_op jit(solution)/shard_map/ppermute | solution.py:688
  16.3 6.3 %collective-permute-start.4 = (f32[2,8,128]{2,1,0:T(8,128)S(1)}, f32[2,8,128]{2,1,0:T(8,128)S(1)}, u32[]{:S(2)}, u32[]{:S(2)}) collective-permute-start(f32[2,8,128]{2,1,0:T(8,128)S(1)} %get-tuple-element.58), channel_id=1, source_target_pairs={{0,32},{32,0},{64,96},{96,64},{128,160},{160,128},{192,224},{224,1... | collective-permute-start | bytes 24584 | tf_op jit(solution)/shard_map/ppermute | solution.py:688
  19.2 3.4 %collective-permute-start.5 = (f32[2,8,128]{2,1,0:T(8,128)S(1)}, f32[2,8,128]{2,1,0:T(8,128)S(1)}, u32[]{:S(2)}, u32[]{:S(2)}) collective-permute-start(f32[2,8,128]{2,1,0:T(8,128)S(1)} %get-tuple-element.59), channel_id=1, source_target_pairs={{0,224},{32,64},{64,32},{96,128},{128,96},{160,192},{192,160},{224... | collective-permute-start | bytes 24584 | tf_op jit(solution)/shard_map/ppermute | solution.py:688
  24.5 7.6 %collective-permute-start.6 = (f32[2,8,128]{2,1,0:T(8,128)S(1)}, f32[2,8,128]{2,1,0:T(8,128)S(1)}, u32[]{:S(2)}, u32[]{:S(2)}) collective-permute-start(f32[2,8,128]{2,1,0:T(8,128)S(1)} %get-tuple-element.81), channel_id=1, source_target_pairs={{0,1},{1,0},{2,3},{3,2},{4,5},{5,4},{6,7},{7,6},{8,9},{9,8},{10,11... | collective-permute-start | bytes 24584 | tf_op jit(solution)/shard_map/ppermute | solution.py:688
  24.6 7.5 %collective-permute-start.7 = (f32[2,8,128]{2,1,0:T(8,128)S(1)}, f32[2,8,128]{2,1,0:T(8,128)S(1)}, u32[]{:S(2)}, u32[]{:S(2)}) collective-permute-start(f32[2,8,128]{2,1,0:T(8,128)S(1)} %get-tuple-element.82), channel_id=1, source_target_pairs={{0,31},{1,2},{2,1},{3,4},{4,3},{5,6},{6,5},{7,8},{8,7},{9,10},{10,... | collective-permute-start | bytes 24584 | tf_op jit(solution)/shard_map/ppermute | solution.py:688
  32.2 5.5 %collective-permute-start.10 = (f32[12,8,128]{2,1,0:T(8,128)S(1)}, f32[12,8,128]{2,1,0:T(8,128)S(1)}, u32[]{:S(2)}, u32[]{:S(2)}) collective-permute-start(f32[12,8,128]{2,1,0:T(8,128)S(1)} %shard_map.112.own), channel_id=1, source_target_pairs={{0,192},{32,224},{64,128},{96,160},{128,64},{160,96},{192,0},{224,... | collective-permute-start | bytes 147464 | tf_op jit(solution)/shard_map/ppermute | solution.py:688
  34.9 3.3 %collective-permute-start.9 = (f32[12,8,128]{2,1,0:T(8,128)S(1)}, f32[12,8,128]{2,1,0:T(8,128)S(1)}, u32[]{:S(2)}, u32[]{:S(2)}) collective-permute-start(f32[12,8,128]{2,1,0:T(8,128)S(1)} %shard_map.112.own), channel_id=1, source_target_pairs={{0,64},{32,96},{64,0},{96,32},{128,192},{160,224},{192,128},{224,1... | collective-permute-start | bytes 147464 | tf_op jit(solution)/shard_map/ppermute | solution.py:688
  37.6 2.7 %collective-permute-start.8 = (f32[12,8,128]{2,1,0:T(8,128)S(1)}, f32[12,8,128]{2,1,0:T(8,128)S(1)}, u32[]{:S(2)}, u32[]{:S(2)}) collective-permute-start(f32[12,8,128]{2,1,0:T(8,128)S(1)} %shard_map.112.own), channel_id=1, source_target_pairs={{0,32},{32,0},{64,96},{96,64},{128,160},{160,128},{192,224},{224,1... | collective-permute-start | bytes 147464 | tf_op jit(solution)/shard_map/ppermute | solution.py:688
  38.2 2.0 %collective-permute-start.11 = (f32[12,8,128]{2,1,0:T(8,128)S(1)}, f32[12,8,128]{2,1,0:T(8,128)S(1)}, u32[]{:S(2)}, u32[]{:S(2)}) collective-permute-start(f32[12,8,128]{2,1,0:T(8,128)S(1)} %shard_map.113), channel_id=1, source_target_pairs={{0,32},{32,0},{64,96},{96,64},{128,160},{160,128},{192,224},{224,1... | collective-permute-start | bytes 147464 | tf_op jit(solution)/shard_map/ppermute | solution.py:688

commit v9 on v8

--- a/solution.py
+++ b/solution.py
@@ -26,7 +26,7 @@
 PADDED = GROUPS * GROUP * ROWS
 PARTS = 4
 PART = PADDED // PARTS
-LOADS = 4
+LOADS = 2
 HALO = 2 * 4 * GROUPS
 PACKS = 2 * GROUPS
 SIDE = GROUPS + 1

time: 44.1 us -> 44 us (level)
  no operation moved by 1% of the time
where the time goes in v9:
time: 44 us; the launch traced here: 43.9 us
  starting transfers between devices  22.9 us (52%)
  Pallas kernels  18.2 us (41%)
  waiting for transfers between devices  1.92 us (4%)
  between operations  0.81 us (2%)
    ppermute x12, starting transfers between devices, swap(): lax.ppermute(value, axis, [(i, partner(i) % count) for i in range(count)])  22.9 us
    pallas_call x14, Pallas kernels, call(): pl.pallas_call(kernel, out_shape=outs, in_specs=ins or [VMEM] * len(args)...  18.2 us
    ppermute x12, waiting for transfers between devices, swap(): lax.ppermute(value, axis, [(i, partner(i) % count) for i in range(count)])  1.92 us
  transfers between devices with their start and end apart: 12, of which 2 were waited for; matrix products, arithmetic and copies ran while one was open for 0% of the time, Pallas kernels for 22%

profile of v9, /device:TPU:1, one launch (start us, length us, event | category | flops | bytes accessed | tf_op | source)
XLA Modules:
  0.0 43.9 jit_solution(1971056563752855708)
XLA Ops:
  0.6 2.7 %shard_map.101 = (f32[128,8,128]{2,1,0:T(8,128)S(1)}, f32[128,8,128]{2,1,0:T(8,128)S(1)}, f32[128,8,128]{2,1,0:T(8,128)S(1)}, f32[128,8,128]{2,1,0:T(8,128)S(1)}...) custom-call(f32[992,128]{1,0:T(8,128)} %bitcast.8, ...), custom_call_target="tpu_custom_call" | custom-call | bytes 4194304 | tf_op jit(solution)/shard_map/pallas_call | solution.py:717
  3.3 0.1 shard_map.103
  3.4 3.3 %collective-permute-start.2 = (f32[66,8,128]{2,1,0:T(8,128)S(1)}, f32[66,8,128]{2,1,0:T(8,128)S(1)}, u32[]{:S(2)}, u32[]{:S(2)}) collective-permute-start(f32[66,8,128]{2,1,0:T(8,128)S(1)} %get-tuple-element.56), channel_id=1, source_target_pairs={{0,32},{32,0},{64,96},{96,64},{128,160},{160,128},{192,224},{224,1... | collective-permute-start | bytes 811016 | tf_op jit(solution)/shard_map/ppermute | solution.py:688
  6.8 0.8 %collective-permute-start = (f32[9,8,128]{2,1,0:T(8,128)S(1)}, f32[9,8,128]{2,1,0:T(8,128)S(1)}, u32[]{:S(2)}, u32[]{:S(2)}) collective-permute-start(f32[9,8,128]{2,1,0:T(8,128)S(1)} %get-tuple-element.51), channel_id=1, source_target_pairs={{0,1},{1,0},{2,3},{3,2},{4,5},{5,4},{6,7},{7,6},{8,9},{9,8},{10,11... | collective-permute-start | bytes 110600 | tf_op jit(solution)/shard_map/ppermute | solution.py:688
  7.5 7.2 %collective-permute-start.1 = (f32[9,8,128]{2,1,0:T(8,128)S(1)}, f32[9,8,128]{2,1,0:T(8,128)S(1)}, u32[]{:S(2)}, u32[]{:S(2)}) collective-permute-start(f32[9,8,128]{2,1,0:T(8,128)S(1)} %get-tuple-element.52), channel_id=1, source_target_pairs={{0,31},{1,2},{2,1},{3,4},{4,3},{5,6},{6,5},{7,8},{8,7},{9,10},{10,... | collective-permute-start | bytes 110600 | tf_op jit(solution)/shard_map/ppermute | solution.py:688
  14.7 0.0 collective-permute-done.side_0
  14.7 1.3 %collective-permute-done.1.side_1 = f32[9,8,128]{2,1,0:T(8,128)S(1)} collective-permute-done((f32[9,8,128]{2,1,0:T(8,128)S(1)}, f32[9,8,128]{2,1,0:T(8,128)S(1)}, u32[]{:S(2)}, u32[]{:S(2)}) %collective-permute-start.1) | collective-permute-done | bytes 36896 | tf_op jit(solution)/shard_map/ppermute | solution.py:688
  16.1 0.2 shard_map.104
  16.2 2.9 %collective-permute-start.4 = (f32[2,8,128]{2,1,0:T(8,128)S(1)}, f32[2,8,128]{2,1,0:T(8,128)S(1)}, u32[]{:S(2)}, u32[]{:S(2)}) collective-permute-start(f32[2,8,128]{2,1,0:T(8,128)S(1)} %get-tuple-element.58), channel_id=1, source_target_pairs={{0,32},{32,0},{64,96},{96,64},{128,160},{160,128},{192,224},{224,1... | collective-permute-start | bytes 24584 | tf_op jit(solution)/shard_map/ppermute | solution.py:688
  19.2 0.0 collective-permute-start.5
  19.2 3.4 %shard_map.102 = (f32[128,8,128]{2,1,0:T(8,128)S(1)}, f32[128,8,128]{2,1,0:T(8,128)S(1)}, f32[4,8,128]{2,1,0:T(8,128)S(1)}, f32[48,8,128]{2,1,0:T(8,128)S(1)}, f32[8,8,8,128]{3,2,1,0:T(8,128)S(1)}) custom-call(f32[128,8,128]{2,1,0:T(8,128)S(1)} %get-tuple-element.45.t, f32[128,8,128]{2,1,0:T(8,128)S(1)} %get-tuple-element.46.s, ...), custom_call_target="tpu_custom_call" | custom-call | bytes 4194304 | tf_op jit(solution)/shard_map/pallas_call | solution.py:717
  22.5 0.0 collective-permute-done.4.corner_0
  22.6 0.0 collective-permute-done.5.corner_1
  22.6 0.0 collective-permute-done.3.swap_1
  22.6 1.9 %shard_map.105 = (f32[4,8,8,128]{3,2,1,0:T(8,128)S(1)}, f32[4,8,8,128]{3,2,1,0:T(8,128)S(1)}, f32[8,8,128]{2,1,0:T(8,128)S(1)}, f32[2,8,128]{2,1,0:T(8,128)S(1)}...) custom-call(f32[128,8,128]{2,1,0:T(8,128)S(1)} %get-tuple-element.45.t, f32[128,8,128]{2,1,0:T(8,128)S(1)} %get-tuple-element.46.s, ...), custom_call_target="tpu_custom_call" | custom-call | bytes 4194304 | tf_op jit(solution)/shard_map/pallas_call | solution.py:717
  24.5 0.1 collective-permute-start.6
  24.6 5.1 %collective-permute-start.7 = (f32[2,8,128]{2,1,0:T(8,128)S(1)}, f32[2,8,128]{2,1,0:T(8,128)S(1)}, u32[]{:S(2)}, u32[]{:S(2)}) collective-permute-start(f32[2,8,128]{2,1,0:T(8,128)S(1)} %get-tuple-element.82), channel_id=1, source_target_pairs={{0,31},{1,2},{2,1},{3,4},{4,3},{5,6},{6,5},{7,8},{8,7},{9,10},{10,... | collective-permute-start | bytes 24584 | tf_op jit(solution)/shard_map/ppermute | solution.py:688
  29.7 1.1 %shard_map.108 = (f32[256,128]{1,0:T(8,128)S(1)}, f32[256,128]{1,0:T(8,128)S(1)}) custom-call(f32[128,8,128]{2,1,0:T(8,128)S(1)} %get-tuple-element.45.t, f32[128,8,128]{2,1,0:T(8,128)S(1)} %get-tuple-element.46.s, f32[128,8,128]{2,1,0:T(8,128)S(1)} %get-tuple-element.47.u, f32[128,8,128]{2,1,0:T(8,128)S(1)} %get-tuple-element.48.v, ...), custom_call_target="tpu_custom_call" | custom-call | bytes 4194304 | tf_op jit(solution)/shard_map/pallas_call | solution.py:717
  30.9 1.2 %shard_map.107 = (f32[256,128]{1,0:T(8,128)S(1)}, f32[256,128]{1,0:T(8,128)S(1)}) custom-call(f32[128,8,128]{2,1,0:T(8,128)S(1)} %get-tuple-element.45.t, f32[128,8,128]{2,1,0:T(8,128)S(1)} %get-tuple-element.46.s, f32[128,8,128]{2,1,0:T(8,128)S(1)} %get-tuple-element.47.u, f32[128,8,128]{2,1,0:T(8,128)S(1)} %get-tuple-element.48.v, ...), custom_call_target="tpu_custom_call" | custom-call | bytes 4194304 | tf_op jit(solution)/shard_map/pallas_call | solution.py:717
  32.0 0.0 collective-permute-done.7.refs_2_
  32.1 2.7 %collective-permute-start.10 = (f32[12,8,128]{2,1,0:T(8,128)S(1)}, f32[12,8,128]{2,1,0:T(8,128)S(1)}, u32[]{:S(2)}, u32[]{:S(2)}) collective-permute-start(f32[12,8,128]{2,1,0:T(8,128)S(1)} %shard_map.112.own), channel_id=1, source_target_pairs={{0,192},{32,224},{64,128},{96,160},{128,64},{160,96},{192,0},{224,... | collective-permute-start | bytes 147464 | tf_op jit(solution)/shard_map/ppermute | solution.py:688
  34.8 0.0 collective-permute-start.9
  34.8 0.3 shard_map.106
  35.1 1.2 %shard_map.110 = (f32[256,128]{1,0:T(8,128)S(1)}, f32[256,128]{1,0:T(8,128)S(1)}) custom-call(f32[128,8,128]{2,1,0:T(8,128)S(1)} %get-tuple-element.45.t, f32[128,8,128]{2,1,0:T(8,128)S(1)} %get-tuple-element.46.s, f32[128,8,128]{2,1,0:T(8,128)S(1)} %get-tuple-element.47.u, f32[128,8,128]{2,1,0:T(8,128)S(1)} %get-tuple-element.48.v, ...), custom_call_target="tpu_custom_call" | custom-call | bytes 4194304 | tf_op jit(solution)/shard_map/pallas_call | solution.py:717
  36.3 1.2 %shard_map.109 = (f32[256,128]{1,0:T(8,128)S(1)}, f32[256,128]{1,0:T(8,128)S(1)}) custom-call(f32[128,8,128]{2,1,0:T(8,128)S(1)} %get-tuple-element.45.t, f32[128,8,128]{2,1,0:T(8,128)S(1)} %get-tuple-element.46.s, f32[128,8,128]{2,1,0:T(8,128)S(1)} %get-tuple-element.47.u, f32[128,8,128]{2,1,0:T(8,128)S(1)} %get-tuple-element.48.v, ...), custom_call_target="tpu_custom_call" | custom-call | bytes 4194304 | tf_op jit(solution)/shard_map/pallas_call | solution.py:717
  37.5 0.1 collective-permute-start.8
  37.6 0.0 collective-permute-done.10.chip_1
  37.6 0.6 %collective-permute-done.9.chip_0 = f32[12,8,128]{2,1,0:T(8,128)S(1)} collective-permute-done((f32[12,8,128]{2,1,0:T(8,128)S(1)}, f32[12,8,128]{2,1,0:T(8,128)S(1)}, u32[]{:S(2)}, u32[]{:S(2)}) %collective-permute-start.9) | collective-permute-done | bytes 49184 | tf_op jit(solution)/shard_map/ppermute | solution.py:688
  38.2 0.7 %collective-permute-start.11 = (f32[12,8,128]{2,1,0:T(8,128)S(1)}, f32[12,8,128]{2,1,0:T(8,128)S(1)}, u32[]{:S(2)}, u32[]{:S(2)}) collective-permute-start(f32[12,8,128]{2,1,0:T(8,128)S(1)} %shard_map.113), channel_id=1, source_target_pairs={{0,32},{32,0},{64,96},{96,64},{128,160},{160,128},{192,224},{224,1... | collective-permute-start | bytes 147464 | tf_op jit(solution)/shard_map/ppermute | solution.py:688
  38.8 1.4 %shard_map.111 = (f32[992,128]{1,0:T(8,128)}, f32[992,128]{1,0:T(8,128)}, f32[992,128]{1,0:T(8,128)}, f32[992,128]{1,0:T(8,128)}, f32[8,128]{1,0:T(8,128)S(1)}) custom-call(f32[1024,128]{1,0:T(8,128)S(1)} %get-tuple-element.65.u_next.refs_4_, f32[1024,128]{1,0:T(8,128)S(1)} %get-tuple-element.66.v_next.refs_5_, ...), custom_call_target="tpu_custom_call" | custom-call | bytes 4194304 | tf_op jit(solution)/shard_map/pallas_call | solution.py:717
  40.2 0.0 collective-permute-done.11.passed
  40.2 3.7 %shard_map.114 = f32[16,128]{1,0:T(8,128)} custom-call(f32[12,8,128]{2,1,0:T(8,128)S(1)} %shard_map.112.own, f32[12,8,128]{2,1,0:T(8,128)S(1)} %collective-permute-done.8.core, f32[12,8,128]{2,1,0:T(8,128)S(1)} %collective-permute-done.9.chip_0, f32[12,8,128]{2,1,0:T(8,128)S(1)} %collective-permute-done.10.chip_1, ...), custom_call_target="tpu_custom_call" | custom-call | bytes 4194304 | tf_op jit(solution)/shard_map/pallas_call | solution.py:717
  (6 shorter events, 0.0 us)
Async XLA Ops:
  3.4 19.1 %collective-permute-start.2 = (f32[66,8,128]{2,1,0:T(8,128)S(1)}, f32[66,8,128]{2,1,0:T(8,128)S(1)}, u32[]{:S(2)}, u32[]{:S(2)}) collective-permute-start(f32[66,8,128]{2,1,0:T(8,128)S(1)} %get-tuple-element.56), channel_id=1, source_target_pairs={{0,32},{32,0},{64,96},{96,64},{128,160},{160,128},{192,224},{224,1... | collective-permute-start | bytes 811016 | tf_op jit(solution)/shard_map/ppermute | solution.py:688
  6.8 15.8 %collective-permute-start.3 = (f32[66,8,128]{2,1,0:T(8,128)S(1)}, f32[66,8,128]{2,1,0:T(8,128)S(1)}, u32[]{:S(2)}, u32[]{:S(2)}) collective-permute-start(f32[66,8,128]{2,1,0:T(8,128)S(1)} %get-tuple-element.57), channel_id=1, source_target_pairs={{0,224},{32,64},{64,32},{96,128},{128,96},{160,192},{192,160},{224... | collective-permute-start | bytes 811016 | tf_op jit(solution)/shard_map/ppermute | solution.py:688
  6.8 8.0 %collective-permute-start = (f32[9,8,128]{2,1,0:T(8,128)S(1)}, f32[9,8,128]{2,1,0:T(8,128)S(1)}, u32[]{:S(2)}, u32[]{:S(2)}) collective-permute-start(f32[9,8,128]{2,1,0:T(8,128)S(1)} %get-tuple-element.51), channel_id=1, source_target_pairs={{0,1},{1,0},{2,3},{3,2},{4,5},{5,4},{6,7},{7,6},{8,9},{9,8},{10,11... | collective-permute-start | bytes 110600 | tf_op jit(solution)/shard_map/ppermute | solution.py:688
  7.5 8.5 %collective-permute-start.1 = (f32[9,8,128]{2,1,0:T(8,128)S(1)}, f32[9,8,128]{2,1,0:T(8,128)S(1)}, u32[]{:S(2)}, u32[]{:S(2)}) collective-permute-start(f32[9,8,128]{2,1,0:T(8,128)S(1)} %get-tuple-element.52), channel_id=1, source_target_pairs={{0,31},{1,2},{2,1},{3,4},{4,3},{5,6},{6,5},{7,8},{8,7},{9,10},{10,... | collective-permute-start | bytes 110600 | tf_op jit(solution)/shard_map/ppermute | solution.py:688
  16.2 6.3 %collective-permute-start.4 = (f32[2,8,128]{2,1,0:T(8,128)S(1)}, f32[2,8,128]{2,1,0:T(8,128)S(1)}, u32[]{:S(2)}, u32[]{:S(2)}) collective-permute-start(f32[2,8,128]{2,1,0:T(8,128)S(1)} %get-tuple-element.58), channel_id=1, source_target_pairs={{0,32},{32,0},{64,96},{96,64},{128,160},{160,128},{192,224},{224,1... | collective-permute-start | bytes 24584 | tf_op jit(solution)/shard_map/ppermute | solution.py:688
  19.2 3.4 %collective-permute-start.5 = (f32[2,8,128]{2,1,0:T(8,128)S(1)}, f32[2,8,128]{2,1,0:T(8,128)S(1)}, u32[]{:S(2)}, u32[]{:S(2)}) collective-permute-start(f32[2,8,128]{2,1,0:T(8,128)S(1)} %get-tuple-element.59), channel_id=1, source_target_pairs={{0,224},{32,64},{64,32},{96,128},{128,96},{160,192},{192,160},{224... | collective-permute-start | bytes 24584 | tf_op jit(solution)/shard_map/ppermute | solution.py:688
  24.5 7.6 %collective-permute-start.6 = (f32[2,8,128]{2,1,0:T(8,128)S(1)}, f32[2,8,128]{2,1,0:T(8,128)S(1)}, u32[]{:S(2)}, u32[]{:S(2)}) collective-permute-start(f32[2,8,128]{2,1,0:T(8,128)S(1)} %get-tuple-element.81), channel_id=1, source_target_pairs={{0,1},{1,0},{2,3},{3,2},{4,5},{5,4},{6,7},{7,6},{8,9},{9,8},{10,11... | collective-permute-start | bytes 24584 | tf_op jit(solution)/shard_map/ppermute | solution.py:688
  24.6 7.5 %collective-permute-start.7 = (f32[2,8,128]{2,1,0:T(8,128)S(1)}, f32[2,8,128]{2,1,0:T(8,128)S(1)}, u32[]{:S(2)}, u32[]{:S(2)}) collective-permute-start(f32[2,8,128]{2,1,0:T(8,128)S(1)} %get-tuple-element.82), channel_id=1, source_target_pairs={{0,31},{1,2},{2,1},{3,4},{4,3},{5,6},{6,5},{7,8},{8,7},{9,10},{10,... | collective-permute-start | bytes 24584 | tf_op jit(solution)/shard_map/ppermute | solution.py:688
  32.1 5.5 %collective-permute-start.10 = (f32[12,8,128]{2,1,0:T(8,128)S(1)}, f32[12,8,128]{2,1,0:T(8,128)S(1)}, u32[]{:S(2)}, u32[]{:S(2)}) collective-permute-start(f32[12,8,128]{2,1,0:T(8,128)S(1)} %shard_map.112.own), channel_id=1, source_target_pairs={{0,192},{32,224},{64,128},{96,160},{128,64},{160,96},{192,0},{224,... | collective-permute-start | bytes 147464 | tf_op jit(solution)/shard_map/ppermute | solution.py:688
  34.8 3.3 %collective-permute-start.9 = (f32[12,8,128]{2,1,0:T(8,128)S(1)}, f32[12,8,128]{2,1,0:T(8,128)S(1)}, u32[]{:S(2)}, u32[]{:S(2)}) collective-permute-start(f32[12,8,128]{2,1,0:T(8,128)S(1)} %shard_map.112.own), channel_id=1, source_target_pairs={{0,64},{32,96},{64,0},{96,32},{128,192},{160,224},{192,128},{224,1... | collective-permute-start | bytes 147464 | tf_op jit(solution)/shard_map/ppermute | solution.py:688
  37.5 2.7 %collective-permute-start.8 = (f32[12,8,128]{2,1,0:T(8,128)S(1)}, f32[12,8,128]{2,1,0:T(8,128)S(1)}, u32[]{:S(2)}, u32[]{:S(2)}) collective-permute-start(f32[12,8,128]{2,1,0:T(8,128)S(1)} %shard_map.112.own), channel_id=1, source_target_pairs={{0,32},{32,0},{64,96},{96,64},{128,160},{160,128},{192,224},{224,1... | collective-permute-start | bytes 147464 | tf_op jit(solution)/shard_map/ppermute | solution.py:688
  38.2 2.0 %collective-permute-start.11 = (f32[12,8,128]{2,1,0:T(8,128)S(1)}, f32[12,8,128]{2,1,0:T(8,128)S(1)}, u32[]{:S(2)}, u32[]{:S(2)}) collective-permute-start(f32[12,8,128]{2,1,0:T(8,128)S(1)} %shard_map.113), channel_id=1, source_target_pairs={{0,32},{32,0},{64,96},{96,64},{128,160},{160,128},{192,224},{224,1... | collective-permute-start | bytes 147464 | tf_op jit(solution)/shard_map/ppermute | solution.py:688
